TPU v7x, 128 devices: a whole 4x4x4 slice. The times are simulated.
128 devices in a mesh: lap: 4 (over x), space: 32 (over y, z, core).
Axes of the slice: x: 4, y: 4, z: 4, core: 2. Of those that a mesh axis runs over, the one named last changes fastest.
Arguments:
- slowness: float32 [64, 512, 128], P('space'), may hold values from 0.25 to 1
- damping: float32 [16], P('lap'), may hold values from 0.2 to 1.5
- src_index: int32 [32768], P('space'), may hold values from 0 to 4194303, as said below
- src_amp: float32 [16, 32768], P('lap', 'space'), may hold values from -12 to 12
- rec_index: int32 [32768], P('space'), may hold values from 0 to 4194303, as said below
- observed: float32 [16, 32768], P('lap', 'space'), may hold values from -0.6 to 0.6
- dual: float32 [3, 64, 512, 128], P(None, 'space', 'lap'), may hold values from -2 to 2
Outputs:
- model: float32 [64, 512, 128], P('space', 'lap')
- dual_next: float32 [3, 64, 512, 128], P(None, 'space', 'lap')
Inputs may be any that keep to these rules, and one draw needn't show every extreme that they name: `src_index`: entry k lies in the slab of grid cells whose first index is from (k // 1024) * 2 to (k // 1024) * 2 + 1; cells may repeat. `rec_index`: entry k lies in the slab of grid cells whose first index is from (k // 1024) * 2 to (k // 1024) * 2 + 1; cells may repeat.
All inputs are finite; a program needn't handle non-finite values.
Results may differ from a plain program's by a relative error of at most 0.0001.
Values sent between devices are 32-bit elements; how exact they have to be, the bound alone decides.
No kernel may reach another device: no remote copies, remote signals or barrier semaphores. Data moves between devices by JAX's collectives and lax.ppermute only.
A program may use at most 192 MiB of HBM per device.

v0:
```python
import functools

import jax
import jax.numpy as jnp
from jax import lax
from jax.experimental import pallas as pl
from jax.experimental.pallas import tpu as pltpu
from jax.sharding import Mesh
from jax.sharding import PartitionSpec as P


HALF = 2
PLANES = 13
KEPT = 9
PAD = 8
ROWS = 1024
LIST = 88
SLAB = ROWS + LIST

dual_step = 0.5
primal_step = 0.2
tv_weight = 0.5

VMEM = pl.BlockSpec(memory_space=pltpu.VMEM)
SMEM = pl.BlockSpec(memory_space=pltpu.SMEM)


def params(mib):
    return pltpu.CompilerParams(vmem_limit_bytes=mib * 2**20)


def spread_points(index, parts, right_planes, write):
    points = index.shape[1]
    column = (index >> 16) * 128 + (index & 127)
    row = ((index >> 7) & 511) - lax.broadcasted_iota(jnp.int32, (8, points), 0) // HALF
    lanes = lax.broadcasted_iota(jnp.int32, (right_planes * 128, points), 0)
    right = jnp.where(lanes == column, 1.0, 0.0).astype(jnp.bfloat16)
    tile = lax.broadcasted_iota(jnp.int32, (ROWS // 8, 8, points), 0)
    mask = row[None] == (8 // HALF) * tile
    for which, part in enumerate(parts):
        total = None
        for piece in part:
            left = jnp.where(mask, piece[None], 0.0).reshape(ROWS, points).astype(jnp.bfloat16)
            got = lax.dot_general(
                left, right, (((1,), (1,)), ((), ())), preferred_element_type=jnp.float32
            )
            total = got if total is None else total + got
        for p in range(right_planes):
            write(which, p, total[:, p * 128 : (p + 1) * 128])


def pieces_of(value, count):
    high = value.astype(jnp.bfloat16).astype(jnp.float32)
    return [high, value - high][:count]


def list_row(ref, base, i):
    block = ref[base + 8 * i : base + 8 * i + 8, :]
    return jnp.concatenate([block[j : j + 1] for j in range(8)], 1)


def either(core, zero, one):
    return lambda i: jnp.where(core == 0, list_row(*zero, i), list_row(*one, i))


def by_parity(even, odd, points):
    parity = lax.broadcasted_iota(jnp.int32, (8, points), 0) % HALF
    return jnp.where(parity == 0, even, odd)


def points_of(core, row, first):
    even = jnp.where(core == 0, row(first), row(first + 2))
    odd = jnp.where(core == 0, row(first + 1), row(first + 3))
    return by_parity(even, odd, even.shape[1])


def writer(stores):
    def write(which, p, value):
        ref, first = stores[which]
        ref[first + p] = value

    return write


def scatter_src(core, row, count, store, first, divisor=None, planes=2):
    amp = points_of(core, row, 2)
    if divisor is not None:
        amp = amp / divisor
    index = row(0).astype(jnp.int32)
    spread_points(index, [pieces_of(amp, count)], planes, writer([(store, first)]))


def scatter_rec(core, row, count, planes, ob, cn, first):
    obs = points_of(core, row, 6)
    parts = [pieces_of(obs, count), [jnp.ones_like(obs)]]
    index = row(1).astype(jnp.int32)
    spread_points(index, parts, planes, writer([(ob, first), (cn, first)]))


def squares(damp):
    core = lax.axis_index("core")
    first, second = damp[HALF * core], damp[HALF * core + 1]
    return first * first, second * second


def diagonal_at(damp, row):
    sigma = row(10)
    first, second = squares(damp)
    return by_parity(6.0 + first * sigma, 6.0 + second * sigma, sigma.shape[1])


def pack_kernel(slow_in, src_in, rec_in, amp_in, obs_in, out, far, src, rec, amp, obs, sem):
    slab = lax.axis_index("pair") * 2 + lax.axis_index("core")
    offset = slab * (2 * 512 * 128)
    pairs = ((src_in, src), (rec_in, rec), (amp_in, amp), (obs_in, obs), (slow_in, out.at[0:ROWS]))
    copies = [pltpu.make_async_copy(x, y, sem.at[k]) for k, (x, y) in enumerate(pairs)]
    for copy in copies:
        copy.start()
    for copy in copies:
        copy.wait()
    points = amp.shape[1]
    far[0:8, :] = (src[...] - offset).astype(jnp.float32)
    far[8:16, :] = (rec[...] - offset).astype(jnp.float32)
    for k, values in ((2, amp), (6, obs)):
        for i in range(4):
            for j in range(8):
                at = 8 * (k + i) + j
                far[at : at + 1, :] = values[i : i + 1, 128 * j : 128 * j + 128]
    index = list_row(far, 0, 0).astype(jnp.int32)
    rows = lax.broadcasted_iota(jnp.int32, (ROWS, points), 0)
    pick = jnp.where(rows == index >> 7, 1.0, 0.0).astype(jnp.bfloat16)
    sigma = out[0:ROWS, :]
    high = sigma.astype(jnp.bfloat16)
    low = (sigma - high.astype(jnp.float32)).astype(jnp.bfloat16)
    dims = (((0,), (0,)), ((), ()))
    got = lax.dot_general(high, pick, dims, preferred_element_type=jnp.float32)
    got = got + lax.dot_general(low, pick, dims, preferred_element_type=jnp.float32)
    lane = lax.broadcasted_iota(jnp.int32, (128, points), 0)
    found = jnp.sum(jnp.where(lane == index & 127, got, 0.0), axis=0, keepdims=True)
    for j in range(8):
        far[80 + j : 81 + j, :] = found[:, 128 * j : 128 * j + 128]
    out[ROWS : ROWS + LIST, :] = far[...]


def scatter_slab(h, row, b, ob, cn):
    core = lax.axis_index("core")
    scatter_src(core, row, 2, b, 2 * h)
    scatter_rec(core, row, 2, 2, ob, cn, 2 * h)


def scatter_own_kernel(lists, b, ob, cn):
    scatter_slab(lax.axis_index("core"), functools.partial(list_row, lists, 0), b, ob, cn)


def scatter_other_kernel(lists, other, b_in, ob_in, cn_in, b, ob, cn, first):
    core = lax.axis_index("core")
    first[...] = jnp.where(core == 0, lists[...], other[ROWS:SLAB, :])
    row = functools.partial(list_row, other, ROWS)
    scatter_slab(1 - lax.axis_index("core"), row, b, ob, cn)


def scatter_near(core, damp, heavy, heavy_low, light, light_low, b):
    scatter_src(core, heavy, 2, b, jnp.where(heavy_low, 2, 4))
    divisor = jnp.where(light_low, diagonal_at(damp, light), 1.0)
    scatter_src(core, light, 1, b, jnp.where(light_low, 0, 6), divisor)


def scatter_mine_kernel(damp, low, high, b, ob, cn):
    core = lax.axis_index("core")
    heavy = either(core, (high, ROWS), (low, ROWS))
    light = either(core, (low, ROWS), (high, ROWS))
    scatter_near(core, damp, heavy, core == 1, light, core == 0, b)
    scatter_rec(core, heavy, 2, 2, ob, cn, jnp.where(core == 1, 0, 2))


def scatter_theirs_kernel(damp, far, near, b_in, b):
    core = lax.axis_index("core")
    low_at, high_at = ROWS, SLAB + ROWS
    heavy = either(core, (near, low_at), (near, high_at))
    light = either(core, (near, high_at), (near, low_at))
    scatter_near(core, damp, heavy, core == 0, light, core == 1, b)
    last = functools.partial(list_row, far, 0)
    scatter_src(core, last, 1, b, 8, diagonal_at(damp, last), 1)


def scatter_late_kernel(high, near, ob_in, cn_in, ob, cn):
    core = lax.axis_index("core")
    low_at, high_at = ROWS, SLAB + ROWS
    heavy = either(core, (near, low_at), (near, high_at))
    scatter_rec(core, heavy, 2, 2, ob, cn, jnp.where(core == 0, 0, 2))
    scatter_rec(core, either(core, (near, high_at), (high, ROWS)), 1, 1, ob, cn, 4)


def shift_matrix():
    i = lax.broadcasted_iota(jnp.int32, (128, 128), 0)
    j = lax.broadcasted_iota(jnp.int32, (128, 128), 1)
    return jnp.where(jnp.abs(i - j) == 1, 1.0, 0.0).astype(jnp.bfloat16)


def neighbours(ref, t):
    ext = ref[t]
    x = ext[PAD : PAD + ROWS]
    total = ROWS + 2 * PAD
    down = pltpu.roll(ext, HALF, 0)[PAD : PAD + ROWS]
    up = pltpu.roll(ext, total - HALF, 0)[PAD : PAD + ROWS]
    high = x.astype(jnp.bfloat16)
    low = (x - high.astype(jnp.float32)).astype(jnp.bfloat16)
    matrix = shift_matrix()
    along = jnp.dot(high, matrix, preferred_element_type=jnp.float32)
    along = along + jnp.dot(low, matrix, preferred_element_type=jnp.float32)
    return x, (down + up) + along


def fold(x):
    return jnp.sum(x.reshape(ROWS // 8, 8, 128), 0)


def walk(first, last, body, carry):
    return lax.fori_loop(first, last, body, carry)


INNER = pl.ds(PAD, 1024)


def advance(src, s_off, inv, i_off, dst, d_off, first, last, dots):
    def body(t, carry):
        x, q = neighbours(src, t - s_off)
        q = q + (src[t - s_off - 1, INNER, :] + src[t - s_off + 1, INNER, :])
        new = inv[t - i_off] * q
        dst[t - d_off, INNER, :] = new
        if not dots:
            return carry
        return carry[0] + fold(x * q), carry[1] + fold(new * q)

    zero = jnp.zeros((8, 128), jnp.float32)
    return walk(first, last, body, (zero, zero) if dots else 0)


def last_moment(src, off):
    def body(t, carry):
        x, q = neighbours(src, t - off)
        q = q + 2.0 * src[t - off + 1, INNER, :]
        return carry + fold(x * q)

    return walk(4, 8, body, jnp.zeros((8, 128), jnp.float32))


def clear_pads(*refs):
    for ref in refs:
        zero = jnp.zeros((8, 128), jnp.float32)
        for t in range(ref.shape[0]):
            ref[t, 0:PAD, :] = zero
            ref[t, ref.shape[1] - PAD :, :] = zero


def message(moments):
    sub = lax.broadcasted_iota(jnp.int32, (8, 128), 0)
    lane = lax.broadcasted_iota(jnp.int32, (8, 128), 1)
    out = jnp.zeros((8, 128), jnp.float32)
    for k, moment in enumerate(moments):
        for c in range(HALF):
            total = jnp.sum(jnp.where(sub % HALF == c, moment, 0.0))
            out = out + jnp.where((sub == k) & (lane == c), total, 0.0)
    return out


def coefficients(moments):
    m = [moments[k : k + 1, :] for k in range(6)]

    def product(p, shift):
        total = 0.0
        for i, a in enumerate(p):
            for j, b in enumerate(p):
                total = total + a * b * (m[i + j] - m[i + j + 1] if shift else m[i + j])
        return total

    one = jnp.ones_like(m[0])
    z, p, energy = [one], [one], m[0]
    x = [0.0 * one] * 3
    for it in range(3):
        stride = energy / product(p, True)
        x = [x[i] + (stride * p[i] if i < len(p) else 0.0) for i in range(3)]
        if it < 2:
            applied = [a - b for a, b in zip(p + [0.0 * one], [0.0 * one] + p)]
            z = [a - stride * b for a, b in zip(z + [0.0 * one], applied)]
            new = product(z, False)
            p = [a + new / energy * b for a, b in zip(z, p + [0.0 * one])]
            energy = new
    lane = lax.broadcasted_iota(jnp.int32, (1, 128), 1)
    sub = lax.broadcasted_iota(jnp.int32, (8, 128), 0)
    out = []
    for v in x:
        value = [jnp.sum(jnp.where(lane == c, v, 0.0)) for c in range(HALF)]
        out.append(jnp.where(sub % HALF == 0, value[0], value[1]))
    return out


def times(pattern, x):
    return (pattern[None] * x.reshape(ROWS // 8, 8, 128)).reshape(ROWS, 128)


def fill_inverse(core, square, inv, slab, mine, theirs, base, valid, first=0):
    def fill(p, _):
        at = pl.multiple_of(p * 512, 512)
        here = mine[pl.ds(at, 512), :]
        there = theirs[pl.ds(pl.multiple_of(base + at, 8), 512), :]
        sigma = jnp.where(core == slab % 2, here, there)
        for c in range(HALF):
            inv[2 * slab + p, pl.ds(c, 512, stride=HALF), :] = valid / (6.0 + square[c] * sigma)
        return 0

    lax.fori_loop(first, 2, fill, 0)


def forward_own_kernel(damp, own_m, own_t, b_own, inv, v0, v1, held):
    core = lax.axis_index("core")
    square = squares(damp)
    clear_pads(v0, v1)
    for slab in (2, 3):
        fill_inverse(core, square, inv, slab, own_m, own_t, 0, 1.0)

    def start(t, carry):
        right = b_own[t - 4]
        new = inv[t] * right
        v0[t, INNER, :] = new
        return carry + fold(new * right)

    held[0:8, :] = walk(4, 8, start, jnp.zeros((8, 128), jnp.float32))
    held[8:16, :], held[16:24, :] = advance(v0, 0, inv, 0, v1, 1, 5, 7, True)


def forward_kernel(
    damp, low_m, high_m, near_t, b_near, held, inv_in, v0_in, v1_in, inv, v0, v1, v2, msg
):
    pair, core = lax.axis_index("pair"), lax.axis_index("core")
    low = jnp.where(pair >= 1, 1.0, 0.0)
    high = jnp.where(pair + 1 < lax.axis_size("pair"), 1.0, 0.0)
    square = squares(damp)
    clear_pads(v2)
    fill_inverse(core, square, inv, 0, low_m, near_t, 0, low, 1)
    fill_inverse(core, square, inv, 1, low_m, near_t, 0, low)
    fill_inverse(core, square, inv, 4, high_m, near_t, SLAB, high)
    fill_inverse(core, square, inv, 5, high_m, near_t, SLAB, high)

    def start(off):
        def body(t, carry):
            v0[t, INNER, :] = inv[t] * b_near[t - off]
            return carry

        return body

    for t, k in ((0, 0), (1, 1), (12, 8)):
        v0[t, INNER, :] = b_near[k]
    walk(2, 4, start(0), 0)
    walk(8, 12, start(4), 0)
    advance(v0, 0, inv, 0, v1, 1, 1, 4, False)
    m1, m2 = advance(v0, 0, inv, 0, v1, 1, 4, 5, True)
    more1, more2 = advance(v0, 0, inv, 0, v1, 1, 7, 8, True)
    advance(v0, 0, inv, 0, v1, 1, 8, 12, False)
    m1 = m1 + more1 + held[8:16, :]
    m2 = m2 + more2 + held[16:24, :]
    advance(v1, 1, inv, 0, v2, 2, 2, 4, False)
    m3, m4 = advance(v1, 1, inv, 0, v2, 2, 4, 8, True)
    advance(v1, 1, inv, 0, v2, 2, 8, 11, False)
    m5 = last_moment(v2, 2)
    msg[...] = message([held[0:8, :], m1, m2, m3, m4, m5])


def adjoint_kernel(
    total, inv, v0, v1, v2, ob_own, cn_own, ob_near, cn_near, wave, u0, u1, u2, msg
):
    a = coefficients(total[...])

    def start(ob, cn, off, own):
        def body(t, carry):
            w = times(a[0], v0[t, INNER, :]) + times(a[1], v1[t - 1, INNER, :])
            w = w + times(a[2], v2[t - 2, INNER, :])
            right = cn[t - off] * w - ob[t - off]
            new = inv[t] * right
            u0[t, INNER, :] = new
            if not own:
                return carry
            wave[t - 4] = w
            return carry + fold(new * right)

        return body

    zero = jnp.zeros((8, 128), jnp.float32)
    walk(2, 4, start(ob_near, cn_near, 2, False), 0)
    m0 = walk(4, 8, start(ob_own, cn_own, 4, True), zero)
    walk(8, 11, start(ob_near, cn_near, 6, False), 0)
    advance(u0, 0, inv, 0, u1, 1, 3, 4, False)
    m1, m2 = advance(u0, 0, inv, 0, u1, 1, 4, 8, True)
    advance(u0, 0, inv, 0, u1, 1, 8, 10, False)
    m3, m4 = advance(u1, 1, inv, 0, u2, 2, 4, 8, True)
    advance(u1, 1, inv, 0, u2, 2, 8, 9, False)
    m5 = last_moment(u2, 2)
    msg[...] = message([m0, m1, m2, m3, m4, m5])


def gradient_kernel(other, damp, total, wave, u0, u1, u2, *rest):
    out, held = rest[-2:]
    a = coefficients(total[...])
    sub = lax.broadcasted_iota(jnp.int32, (8, 128), 0)
    square = jnp.where(sub % HALF == 0, *squares(damp))
    a = [-square * v for v in a]
    core = lax.axis_index("core")
    core = 1 - core if other else core
    for p in range(2):
        t = 4 + 2 * core + p
        x = times(a[0], u0[t, INNER, :]) + times(a[1], u1[t - 1, INNER, :])
        x = x + times(a[2], u2[t - 2, INNER, :])
        held[...] = x * wave[t - 4]
        for band in range(4):
            at = band * 256
            both = held[pl.ds(at, 128, stride=HALF), :] + held[pl.ds(at + 1, 128, stride=HALF), :]
            out[band, p] = both if other else both + rest[0][band, p]


def power_kernel(parts, own, msg):
    g = (parts[0] + parts[1]) + (parts[2] + parts[3])
    own[...] = g
    msg[...] = jnp.full((128, 128), jnp.sum(g * g), jnp.float32)


def variation_kernel(slow, own_t, near_t, dual, dual_next, base, send_x, send_y):
    lap, pair, core = (lax.axis_index(name) for name in ("lap", "pair", "core"))
    start = pl.multiple_of(lap * 128, 128)
    band = pl.ds(start, 128)
    after = pl.ds(pl.multiple_of(jnp.minimum(start + 128, 504), 8), 8)
    row = lax.broadcasted_iota(jnp.int32, (128, 128), 0)
    lane = lax.broadcasted_iota(jnp.int32, (128, 128), 1)
    last_y = (row == 127) & (lap == 3)
    last_z = lane == 127
    comps = []
    for p in range(2):
        here = slow[p, band, :]
        if p == 0:
            step_x = slow[1, band, :] - here
        else:
            beyond = near_t[pl.ds(pl.multiple_of(SLAB + start, 8), 128), :]
            step_x = jnp.where(core == 0, own_t[band, :], beyond) - here
            step_x = jnp.where((core == 1) & (pair == 15), 0.0, step_x)
        rolled = pltpu.roll(here, 127, 0)
        step_y = jnp.where(row == 127, slow[p, after, :][0:1], rolled) - here
        step_y = jnp.where(last_y, 0.0, step_y)
        step_z = jnp.where(last_z, 0.0, pltpu.roll(here, 127, 1) - here)
        trial = [dual[k, p] + dual_step * step for k, step in enumerate((step_x, step_y, step_z))]
        magnitude = jnp.sqrt(trial[0] * trial[0] + trial[1] * trial[1] + trial[2] * trial[2])
        scale = jnp.maximum(1.0, magnitude / tv_weight)
        new = [x / scale for x in trial]
        for k in range(3):
            dual_next[k, p] = new[k]
        if p == 1:
            new[0] = jnp.where((core == 1) & (pair == 15), 0.0, new[0])
        new[1] = jnp.where(last_y, 0.0, new[1])
        new[2] = jnp.where(last_z, 0.0, new[2])
        comps.append(new)
    for p in range(2):
        x, y, z = comps[p]
        back = jnp.where(row == 0, 0.0, pltpu.roll(y, 1, 0)) - y
        back = back + (jnp.where(lane == 0, 0.0, pltpu.roll(z, 1, 1)) - z)
        back = back + (comps[0][0] - x if p == 1 else -x)
        base[p] = slow[p, band, :] - primal_step * back
        send_y[p] = y[120:128]
    send_x[0] = comps[1][0]


def model_kernel(cells, base, grad, power, prior_x, prior_y, model):
    total = power[0]
    for k in range(1, 16):
        total = total + power[k]
    total = jnp.sum(total, axis=0, keepdims=True)
    scale = 1.0 / jnp.sqrt(total / cells + 1e-06)
    row = lax.broadcasted_iota(jnp.int32, (128, 128), 0)
    for p in range(2):
        back = jnp.where(row == 0, prior_y[p][7:8], 0.0)
        if p == 0:
            back = back + prior_x[0]
        model[p] = base[p] - primal_step * (grad[p] * scale + back)


def cost(work):
    return pl.CostEstimate(flops=work * 10**9, bytes_accessed=10**6, transcendentals=0)


def struct(*shape):
    return jax.ShapeDtypeStruct(shape, jnp.float32)


def moved(x, axis, by):
    peers = lax.axis_size(axis)
    return lax.ppermute(x, axis, [(i, i + by) for i in range(peers) if 0 <= i + by < peers])


def swapped(x):
    return lax.ppermute(x, "core", [(0, 1), (1, 0)])


def pair_sum(x):
    for masks in ((1, 2, 3), (4, 8, 12)):
        x = x + sum(lax.ppermute(x, "pair", [(i, i ^ d) for i in range(16)]) for d in masks)
    return x


def scatter(kernel, name, work, inputs, shapes, into=()):
    scalars = 1 if inputs[0].ndim == 1 else 0
    first = len(inputs)
    return pl.pallas_call(
        kernel,
        out_shape=tuple(struct(*shape) for shape in shapes),
        in_specs=[SMEM] * scalars + [VMEM] * (len(inputs) - scalars + len(into)),
        out_specs=(VMEM,) * len(shapes),
        input_output_aliases={first + k: k for k in range(len(into))},
        compiler_params=params(12),
        cost_estimate=cost(work),
        name=name,
    )(*inputs, *into)


def on_device(slowness, damping, src_index, src_amp, rec_index, observed, dual):
    width_x, rows_y, depth_z = slowness.shape
    slab_cells = width_x * rows_y * depth_z
    pairs = lax.axis_size("pair")

    packed, lists = pl.pallas_call(
        pack_kernel,
        out_shape=(struct(SLAB, 128), struct(LIST, 128)),
        in_specs=[pl.BlockSpec(memory_space=pltpu.HBM)] * 5,
        out_specs=(VMEM,) * 2,
        scratch_shapes=[
            pltpu.VMEM((8, 128), jnp.int32), pltpu.VMEM((8, 128), jnp.int32),
            pltpu.VMEM(src_amp.shape, jnp.float32), pltpu.VMEM(observed.shape, jnp.float32),
            pltpu.SemaphoreType.DMA((5,)),
        ],
        compiler_params=params(8),
        name="pack",
    )(
        *(
            pltpu.with_memory_space_constraint(x, pltpu.HBM)
            for x in (
                slowness.reshape(ROWS, 128), src_index.reshape(8, 128), rec_index.reshape(8, 128),
                src_amp, observed,
            )
        )
    )
    low_m, high_m = moved(packed, "pair", 1), moved(packed, "pair", -1)
    own_t = swapped(packed)

    block, near_block = (4, ROWS, 128), (5, ROWS, 128)
    own = scatter(scatter_own_kernel, "scatter_own", 5, (lists,), [block] * 3)
    b_own, ob_own, cn_own, first = scatter(
        scatter_other_kernel, "scatter_other", 5, (lists, own_t), [block] * 3 + [(LIST, 128)], own
    )
    far_m = moved(first, "pair", -2)
    padded = ROWS + 2 * PAD
    inv, v0, v1, held = pl.pallas_call(
        forward_own_kernel,
        out_shape=(
            struct(PLANES, ROWS, 128), struct(13, padded, 128), struct(11, padded, 128),
            struct(24, 128),
        ),
        in_specs=[SMEM] + [VMEM] * 3,
        out_specs=(VMEM,) * 4,
        compiler_params=params(8),
        cost_estimate=cost(4),
        name="forward_own",
    )(damping, slowness.reshape(ROWS, 128), own_t, b_own)
    low_m, high_m, far_m, held = lax.optimization_barrier((low_m, high_m, far_m, held))
    near_t = swapped(jnp.concatenate([low_m, high_m]))
    b_near, ob_near, cn_near = scatter(
        scatter_mine_kernel, "scatter_mine", 6, (damping, low_m, high_m),
        [(9, ROWS, 128), near_block, near_block],
    )
    near_t, b_near = lax.optimization_barrier((near_t, b_near))
    b_near, = scatter(
        scatter_theirs_kernel, "scatter_theirs", 5, (damping, far_m, near_t), [(9, ROWS, 128)],
        (b_near,),
    )

    inv, v0, v1, v2, msg = pl.pallas_call(
        forward_kernel,
        out_shape=(
            struct(PLANES, ROWS, 128), struct(13, padded, 128), struct(11, padded, 128),
            struct(9, padded, 128), struct(8, 128),
        ),
        in_specs=[SMEM] + [VMEM] * 8,
        out_specs=(VMEM,) * 5,
        input_output_aliases={6: 0, 7: 1, 8: 2},
        compiler_params=params(8),
        cost_estimate=cost(20),
        name="forward",
    )(damping, low_m, high_m, near_t, b_near, held, inv, v0, v1)

    near_t, msg = lax.optimization_barrier((near_t, msg))
    ob_near, cn_near = scatter(
        scatter_late_kernel, "scatter_late", 5, (high_m, near_t), [near_block] * 2,
        (ob_near, cn_near),
    )
    wave, u0, u1, u2, msg = pl.pallas_call(
        adjoint_kernel,
        out_shape=(
            struct(4, ROWS, 128), struct(13, padded, 128), struct(11, padded, 128),
            struct(9, padded, 128), struct(8, 128),
        ),
        in_specs=[VMEM] * 9,
        out_specs=(VMEM,) * 5,
        input_output_aliases={2: 1, 3: 2, 4: 3},
        compiler_params=params(8),
        cost_estimate=cost(14),
        name="adjoint",
    )(pair_sum(msg), inv, v0, v1, v2, ob_own, cn_own, ob_near, cn_near)

    total = pair_sum(msg)

    def gradient(other, *more):
        return pl.pallas_call(
            functools.partial(gradient_kernel, other),
            out_shape=struct(4, 2, 128, 128),
            in_specs=[SMEM] + [VMEM] * (5 + len(more)),
            out_specs=VMEM,
            scratch_shapes=[pltpu.VMEM((ROWS, 128), jnp.float32)],
            compiler_params=params(8),
            name="gradient",
        )(damping, total, wave, u0, u1, u2, *more)

    parts = gradient(False, swapped(gradient(True)))
    slowness, dual, own_t, near_t, parts = lax.optimization_barrier(
        (slowness, dual, own_t, near_t, parts)
    )
    arrived = lax.all_to_all(parts, "lap", 0, 0, tiled=True)
    dual_next, base, send_x, send_y = pl.pallas_call(
        variation_kernel,
        out_shape=(
            struct(3, 2, 128, 128), struct(2, 128, 128), struct(1, 128, 128), struct(2, 8, 128),
        ),
        in_specs=[VMEM] * 4,
        out_specs=(VMEM,) * 4,
        compiler_params=params(8),
        cost_estimate=cost(1),
        name="variation",
    )(slowness, own_t, near_t, dual)
    prior_x = moved(send_x, ("pair", "core"), 1)
    prior_y = moved(send_y, "lap", 1)
    arrived, prior_x, prior_y = lax.optimization_barrier((arrived, prior_x, prior_y))
    own_grad, power = pl.pallas_call(
        power_kernel,
        out_shape=(struct(2, 128, 128), struct(128, 128)),
        in_specs=[VMEM],
        out_specs=(VMEM, VMEM),
        compiler_params=params(8),
        name="power",
    )(arrived)
    power = lax.all_to_all(power, ("lap", "pair", "core"), 0, 0, tiled=True)
    model = pl.pallas_call(
        functools.partial(model_kernel, float(slab_cells * 2 * pairs)),
        out_shape=struct(2, 128, 128),
        in_specs=[VMEM] * 5,
        out_specs=VMEM,
        compiler_params=params(8),
        name="model",
    )(base, own_grad, power.reshape(16, 8, 128), prior_x, prior_y)
    return (model, dual_next)


def solution(mesh):
    space = mesh.devices.shape[1]
    mesh = Mesh(mesh.devices.reshape(-1, space // 2, 2), ("lap", "pair", "core"))
    both = ("pair", "core")
    in_specs = (
        P(both, None, None),
        P("lap"),
        P(both),
        P("lap", both),
        P(both),
        P("lap", both),
        P(None, both, "lap", None),
    )
    out_specs = (P(both, "lap", None), P(None, both, "lap", None))
    return jax.shard_map(
        on_device, mesh=mesh, in_specs=in_specs, out_specs=out_specs, check_vma=False
    )
```

profile of v0, /device:TPU:1, one launch (start us, length us, event | category | flops | bytes accessed | tf_op | source)
XLA Modules:
  0.0 120.9 jit_solution(16432689934867030198)
XLA Ops:
  0.6 2.4 %pack.1 = (f32[1112,128]{1,0:T(8,128)S(1)}, f32[88,128]{1,0:T(8,128)S(1)}) custom-call(f32[1024,128]{1,0:T(8,128)} %bitcast.7, s32[8,128]{1,0:T(8,128)} %bitcast.11, s32[8,128]{1,0:T(8,128)} %bitcast.12, f32[4,1024]{1,0:T(4,128)} %amp_in.1, f32[4,1024]{1,0:T(4,128)} %obs_in.1), custom_call_target="tpu_custom_call" | custom-call | tf_op jit(solution)/shard_map/pack/pallas_call | solution.py:526
  3.0 1.5 %collective-permute-start = (f32[1112,128]{1,0:T(8,128)S(1)}, f32[1112,128]{1,0:T(8,128)S(1)}, u32[]{:S(2)}, u32[]{:S(2)}) collective-permute-start(f32[1112,128]{1,0:T(8,128)S(1)} %get-tuple-element.52), channel_id=1, source_target_pairs={{0,1},{1,0},{2,3},{3,2},{4,5},{5,4},{6,7},{7,6},{8,9},{9,8},{10,11... | collective-permute-start | bytes 1708040 | tf_op jit(solution)/shard_map/ppermute | solution.py:497
  4.5 1.3 %collective-permute-start.2 = (f32[1112,128]{1,0:T(8,128)S(1)}, f32[1112,128]{1,0:T(8,128)S(1)}, u32[]{:S(2)}, u32[]{:S(2)}) collective-permute-start(f32[1112,128]{1,0:T(8,128)S(1)} %get-tuple-element.52), channel_id=1, source_target_pairs={{2,0},{4,2},{6,4},{8,6},{10,8},{12,10},{14,12},{16,14},{18,16},{20... | collective-permute-start | bytes 1708040 | tf_op jit(solution)/shard_map/ppermute | solution.py:493
  5.8 4.3 %collective-permute-start.1 = (f32[1112,128]{1,0:T(8,128)S(1)}, f32[1112,128]{1,0:T(8,128)S(1)}, u32[]{:S(2)}, u32[]{:S(2)}) collective-permute-start(f32[1112,128]{1,0:T(8,128)S(1)} %get-tuple-element.52), channel_id=1, source_target_pairs={{0,2},{2,4},{4,6},{6,8},{8,10},{10,12},{12,14},{14,16},{16,18},{18... | collective-permute-start | bytes 1708040 | tf_op jit(solution)/shard_map/ppermute | solution.py:493
  10.1 2.9 %scatter_own.1 = (f32[4,1024,128]{2,1,0:T(8,128)S(1)}, f32[4,1024,128]{2,1,0:T(8,128)S(1)}, f32[4,1024,128]{2,1,0:T(8,128)S(1)}) custom-call(f32[88,128]{1,0:T(8,128)S(1)} %get-tuple-element.53.lists), custom_call_target="tpu_custom_call" | custom-call | flops 5000000000 | bytes 1000000 | tf_op jit(solution)/shard_map/scatter_own/pallas_call | solution.py:509
  13.1 2.9 %scatter_other.1 = (f32[4,1024,128]{2,1,0:T(8,128)S(1)}, f32[4,1024,128]{2,1,0:T(8,128)S(1)}, f32[4,1024,128]{2,1,0:T(8,128)S(1)}, f32[88,128]{1,0:T(8,128)S(1)}) custom-call(f32[88,128]{1,0:T(8,128)S(1)} %get-tuple-element.53.lists, f32[1112,128]{1,0:T(8,128)S(1)} %collective-permute-done.other.own_t, ...), custom_call_target="tpu_custom_call", output_to_operand_aliasing={{0}: (2, {}), {1}: (3, {}), {2}: (4, {})} | custom-call | flops 5000000000 | bytes 1000000 | tf_op jit(solution)/shard_map/scatter_other/pallas_call | solution.py:509
  16.0 1.3 %collective-permute-start.3 = (f32[88,128]{1,0:T(8,128)S(1)}, f32[88,128]{1,0:T(8,128)S(1)}, u32[]{:S(2)}, u32[]{:S(2)}) collective-permute-start(f32[88,128]{1,0:T(8,128)S(1)} %get-tuple-element.57), channel_id=1, source_target_pairs={{4,0},{6,2},{8,4},{10,6},{12,8},{14,10},{16,12},{18,14},{20,16},{2... | collective-permute-start | bytes 135176 | tf_op jit(solution)/shard_map/ppermute | solution.py:493
  17.3 2.4 %forward_own.1 = (f32[13,1024,128]{2,1,0:T(8,128)S(1)}, f32[13,1040,128]{2,1,0:T(8,128)S(1)}, f32[11,1040,128]{2,1,0:T(8,128)S(1)}, f32[24,128]{1,0:T(8,128)S(1)}) custom-call(f32[4]{0:T(128)S(1)} %copy-done.1, f32[1024,128]{1,0:T(8,128)S(1)} %bitcast.8, f32[1112,128]{1,0:T(8,128)S(1)} %collective-permute-done.other.own_t, ...), custom_call_target="tpu_custom_call" | custom-call | flops 4000000000 | bytes 1000000 | tf_op jit(solution)/shard_map/forward_own/pallas_call | solution.py:557
  19.7 1.6 %collective-permute-done.2.high.high_m = f32[1112,128]{1,0:T(8,128)S(1)} collective-permute-done((f32[1112,128]{1,0:T(8,128)S(1)}, f32[1112,128]{1,0:T(8,128)S(1)}, u32[]{:S(2)}, u32[]{:S(2)}) %collective-permute-start.2) | collective-permute-done | bytes 569376 | tf_op jit(solution)/shard_map/ppermute | solution.py:493
  21.3 1.0 collective-permute-done.1.low.low_m
  22.3 4.5 %collective-permute-done.3.far = f32[88,128]{1,0:T(8,128)S(1)} collective-permute-done((f32[88,128]{1,0:T(8,128)S(1)}, f32[88,128]{1,0:T(8,128)S(1)}, u32[]{:S(2)}, u32[]{:S(2)}) %collective-permute-start.3) | collective-permute-done | bytes 45088 | tf_op jit(solution)/shard_map/ppermute | solution.py:493
  26.8 0.1 pad_maximum_fusion
  26.9 1.7 %collective-permute-start.4 = (f32[2224,128]{1,0:T(8,128)S(1)}, f32[2224,128]{1,0:T(8,128)S(1)}, u32[]{:S(2)}, u32[]{:S(2)}) collective-permute-start(f32[2224,128]{1,0:T(8,128)S(1)} %pad_maximum_fusion), channel_id=1, source_target_pairs={{0,1},{1,0},{2,3},{3,2},{4,5},{5,4},{6,7},{7,6},{8,9},{9,8},{10,11... | collective-permute-start | bytes 3416072 | tf_op jit(solution)/shard_map/ppermute | solution.py:497
  28.6 4.0 %scatter_mine.1 = (f32[9,1024,128]{2,1,0:T(8,128)S(1)}, f32[5,1024,128]{2,1,0:T(8,128)S(1)}, f32[5,1024,128]{2,1,0:T(8,128)S(1)}) custom-call(f32[4]{0:T(128)S(1)} %copy-done.1, f32[1112,128]{1,0:T(8,128)S(1)} %collective-permute-done.1.low.low_m, f32[1112,128]{1,0:T(8,128)S(1)} %collective-permute-done.2.high.high_m), custom_call_target="tpu_custom_call" | custom-call | flops 6000000000 | bytes 1000000 | tf_op jit(solution)/shard_map/scatter_mine/pallas_call | solution.py:509
  32.6 2.9 %scatter_theirs.1.b_near = f32[9,1024,128]{2,1,0:T(8,128)S(1)} custom-call(f32[4]{0:T(128)S(1)} %copy-done.1, f32[88,128]{1,0:T(8,128)S(1)} %collective-permute-done.3.far, f32[2224,128]{1,0:T(8,128)S(1)} %collective-permute-done.4.near.near_t, f32[9,1024,128]{2,1,0:T(8,128)S(1)} %get-tuple-element.65.b_in), custom_call_target="tpu_custom_call", output_to_operand_aliasing={{}: (3, {})} | custom-call | flops 5000000000 | bytes 1000000 | tf_op jit(solution)/shard_map/scatter_theirs/pallas_call | solution.py:509
  35.6 10.0 %forward.1 = (f32[13,1024,128]{2,1,0:T(8,128)S(1)}, f32[13,1040,128]{2,1,0:T(8,128)S(1)}, f32[11,1040,128]{2,1,0:T(8,128)S(1)}, f32[9,1040,128]{2,1,0:T(8,128)S(1)}, f32[8,128]{1,0:T(8,128)S(1)}) custom-call(f32[4]{0:T(128)S(1)} %copy-done.1, ...), custom_call_target="tpu_custom_call", output_to_operand_aliasing={{0}: (6, {}), {1}: (7, {}), {2}: (8, {})} | custom-call | flops 20000000000 | bytes 1000000 | tf_op jit(solution)/shard_map/forward/pallas_call | solution.py:581
  45.6 2.4 %collective-permute-start.7 = (f32[8,128]{1,0:T(8,128)S(1)}, f32[8,128]{1,0:T(8,128)S(1)}, u32[]{:S(2)}, u32[]{:S(2)}) collective-permute-start(f32[8,128]{1,0:T(8,128)S(1)} %get-tuple-element.72), channel_id=1, source_target_pairs={{0,6},{2,4},{4,2},{6,0},{8,14},{10,12},{12,10},{14,8},{16,22},{18,... | collective-permute-start | bytes 12296 | tf_op jit(solution)/shard_map/ppermute | solution.py:502
  48.0 0.9 collective-permute-start.5
  48.9 0.4 collective-permute-done.7
  49.3 2.6 %collective-permute-done.6 = f32[8,128]{1,0:T(8,128)S(1)} collective-permute-done((f32[8,128]{1,0:T(8,128)S(1)}, f32[8,128]{1,0:T(8,128)S(1)}, u32[]{:S(2)}, u32[]{:S(2)}) %collective-permute-start.6) | collective-permute-done | bytes 4128 | tf_op jit(solution)/shard_map/ppermute | solution.py:502
  52.0 3.5 %collective-permute-start.10 = (f32[8,128]{1,0:T(8,128)S(1)}, f32[8,128]{1,0:T(8,128)S(1)}, u32[]{:S(2)}, u32[]{:S(2)}) collective-permute-start(f32[8,128]{1,0:T(8,128)S(1)} %add_add_fusion.3), channel_id=1, source_target_pairs={{0,24},{2,26},{4,28},{6,30},{8,16},{10,18},{12,20},{14,22},{16,8},... | collective-permute-start | bytes 12296 | tf_op jit(solution)/shard_map/ppermute | solution.py:502
  55.4 0.1 collective-permute-start.9
  55.5 0.6 collective-permute-start.8
  56.1 2.9 %scatter_late.1 = (f32[5,1024,128]{2,1,0:T(8,128)S(1)}, f32[5,1024,128]{2,1,0:T(8,128)S(1)}) custom-call(f32[1112,128]{1,0:T(8,128)S(1)} %collective-permute-done.2.high.high_m, f32[2224,128]{1,0:T(8,128)S(1)} %collective-permute-done.4.near.near_t, f32[5,1024,128]{2,1,0:T(8,128)S(1)} %get-tuple-element.79.ob_in, ...), custom_call_target="tpu_custom_call", output_to_operand_aliasing={{0}: (2, {}), {1}: (3, {})} | custom-call | flops 5000000000 | bytes 1000000 | tf_op jit(solution)/shard_map/scatter_late/pallas_call | solution.py:509
  59.0 0.4 collective-permute-done.9
  59.4 8.5 %adjoint.1 = (f32[4,1024,128]{2,1,0:T(8,128)S(1)}, f32[13,1040,128]{2,1,0:T(8,128)S(1)}, f32[11,1040,128]{2,1,0:T(8,128)S(1)}, f32[9,1040,128]{2,1,0:T(8,128)S(1)}, f32[8,128]{1,0:T(8,128)S(1)}) custom-call(f32[8,128]{1,0:T(8,128)S(1)} %add_add_fusion.2.total, ...), custom_call_target="tpu_custom_call", output_to_operand_aliasing={{1}: (2, {}), {2}: (3, {}), {3}: (4, {})} | custom-call | flops 14000000000 | bytes 1000000 | tf_op jit(solution)/shard_map/adjoint/pallas_call | solution.py:600
  67.9 2.2 %collective-permute-start.13 = (f32[8,128]{1,0:T(8,128)S(1)}, f32[8,128]{1,0:T(8,128)S(1)}, u32[]{:S(2)}, u32[]{:S(2)}) collective-permute-start(f32[8,128]{1,0:T(8,128)S(1)} %get-tuple-element.83), channel_id=1, source_target_pairs={{0,6},{2,4},{4,2},{6,0},{8,14},{10,12},{12,10},{14,8},{16,22},{18,... | collective-permute-start | bytes 12296 | tf_op jit(solution)/shard_map/ppermute | solution.py:502
  70.1 0.8 collective-permute-start.12
  70.9 0.3 collective-permute-start.11
  71.2 0.4 collective-permute-done.13
  71.6 2.4 %collective-permute-done.12 = f32[8,128]{1,0:T(8,128)S(1)} collective-permute-done((f32[8,128]{1,0:T(8,128)S(1)}, f32[8,128]{1,0:T(8,128)S(1)}, u32[]{:S(2)}, u32[]{:S(2)}) %collective-permute-start.12) | collective-permute-done | bytes 4128 | tf_op jit(solution)/shard_map/ppermute | solution.py:502
  74.1 2.3 %collective-permute-start.16 = (f32[8,128]{1,0:T(8,128)S(1)}, f32[8,128]{1,0:T(8,128)S(1)}, u32[]{:S(2)}, u32[]{:S(2)}) collective-permute-start(f32[8,128]{1,0:T(8,128)S(1)} %add_add_fusion.1), channel_id=1, source_target_pairs={{0,24},{2,26},{4,28},{6,30},{8,16},{10,18},{12,20},{14,22},{16,8},... | collective-permute-start | bytes 12296 | tf_op jit(solution)/shard_map/ppermute | solution.py:502
  76.5 0.9 collective-permute-start.14
  77.4 0.6 collective-permute-done.16
  78.0 2.4 %collective-permute-done.15 = f32[8,128]{1,0:T(8,128)S(1)} collective-permute-done((f32[8,128]{1,0:T(8,128)S(1)}, f32[8,128]{1,0:T(8,128)S(1)}, u32[]{:S(2)}, u32[]{:S(2)}) %collective-permute-start.15) | collective-permute-done | bytes 4128 | tf_op jit(solution)/shard_map/ppermute | solution.py:502
  80.4 1.2 %gradient.2 = f32[4,2,128,128]{3,2,1,0:T(8,128)S(1)} custom-call(f32[4]{0:T(128)S(1)} %copy-done.1, f32[8,128]{1,0:T(8,128)S(1)} %add_add_fusion.total, f32[4,1024,128]{2,1,0:T(8,128)S(1)} %get-tuple-element.84.wave, f32[13,1040,128]{2,1,0:T(8,128)S(1)} %get-tuple-element.85.u0, f32[11,1040,128]{2,1,0:T(8,128)S(1)} %get-tuple-element.86.u1, ...), custom_call_target="tpu_custom_call" | custom-call | tf_op jit(solution)/shard_map/gradient/pallas_call | solution.py:617
  81.7 5.2 %collective-permute-start.17 = (f32[4,2,128,128]{3,2,1,0:T(8,128)S(1)}, f32[4,2,128,128]{3,2,1,0:T(8,128)S(1)}, u32[]{:S(2)}, u32[]{:S(2)}) collective-permute-start(f32[4,2,128,128]{3,2,1,0:T(8,128)S(1)} %gradient.2), channel_id=1, source_target_pairs={{0,1},{1,0},{2,3},{3,2},{4,5},{5,4},{6,7},{7,6},{8,9},{9,8},{10,11... | collective-permute-start | bytes 1572872 | tf_op jit(solution)/shard_map/ppermute | solution.py:497
  86.9 1.5 %collective-permute-done.17.rest_0_ = f32[4,2,128,128]{3,2,1,0:T(8,128)S(1)} collective-permute-done((f32[4,2,128,128]{3,2,1,0:T(8,128)S(1)}, f32[4,2,128,128]{3,2,1,0:T(8,128)S(1)}, u32[]{:S(2)}, u32[]{:S(2)}) %collective-permute-start.17) | collective-permute-done | bytes 524320 | tf_op jit(solution)/shard_map/ppermute | solution.py:497
  88.4 2.1 %gradient.3 = f32[4,2,128,128]{3,2,1,0:T(8,128)} custom-call(f32[4]{0:T(128)S(1)} %copy-done.1, f32[8,128]{1,0:T(8,128)S(1)} %add_add_fusion.total, f32[4,1024,128]{2,1,0:T(8,128)S(1)} %get-tuple-element.84.wave, f32[13,1040,128]{2,1,0:T(8,128)S(1)} %get-tuple-element.85.u0, f32[11,1040,128]{2,1,0:T(8,128)S(1)} %get-tuple-element.86.u1, ...), custom_call_target="tpu_custom_call" | custom-call | tf_op jit(solution)/shard_map/gradient/pallas_call | solution.py:617
  90.5 4.0 %all-to-all-start = ((f32[4,2,128,128]{3,2,1,0:T(8,128)}), f32[4,2,128,128]{3,2,1,0:T(8,128)S(1)}, u32[]{:S(2)}, u32[]{:S(2)}) async-start(f32[4,2,128,128]{3,2,1,0:T(8,128)} %gradient.3), calls=%async_computation | async-start | bytes 1048576 | tf_op jit(solution)/shard_map/all_to_all | solution.py:631
  94.5 0.9 variation.1
  95.4 2.0 %collective-permute-start.18 = (f32[1,128,128]{2,1,0:T(8,128)S(1)}, f32[1,128,128]{2,1,0:T(8,128)S(1)}, u32[]{:S(2)}, u32[]{:S(2)}) collective-permute-start(f32[1,128,128]{2,1,0:T(8,128)S(1)} %get-tuple-element.94), channel_id=1, source_target_pairs={{0,1},{1,2},{2,3},{3,4},{4,5},{5,6},{6,7},{7,8},{8,9},{9,10},{10,1... | collective-permute-start | bytes 196616 | tf_op jit(solution)/shard_map/ppermute | solution.py:493
  97.4 3.6 %collective-permute-start.19 = (f32[2,8,128]{2,1,0:T(8,128)S(1)}, f32[2,8,128]{2,1,0:T(8,128)S(1)}, u32[]{:S(2)}, u32[]{:S(2)}) collective-permute-start(f32[2,8,128]{2,1,0:T(8,128)S(1)} %get-tuple-element.95), channel_id=1, source_target_pairs={{0,32},{32,64},{64,96},{1,33},{33,65},{65,97},{2,34},{34,66},{66,9... | collective-permute-start | bytes 24584 | tf_op jit(solution)/shard_map/ppermute | solution.py:493
  101.1 0.8 collective-permute-done.19.prior_y
  101.8 1.6 %all-to-all-done.parts = f32[4,2,128,128]{3,2,1,0:T(8,128)S(1)} async-done(((f32[4,2,128,128]{3,2,1,0:T(8,128)}), f32[4,2,128,128]{3,2,1,0:T(8,128)S(1)}, u32[]{:S(2)}, u32[]{:S(2)}) %all-to-all-start) | async-done | bytes 524320 | tf_op jit(solution)/shard_map/all_to_all | solution.py:631
  103.4 0.2 power.1
  103.6 16.6 %all_to_all.14 = f32[128,1,128]{2,1,0:T(1,128)S(1)} all-to-all(f32[128,1,128]{2,1,0:T(1,128)S(1)} %bitcast.10), channel_id=1, replica_groups=mesh['lap'=4,'pair'=16,'core'=2] {'lap','pair','core'}, dimensions={0} | all-to-all | bytes 131072 | tf_op jit(solution)/shard_map/all_to_all | solution.py:654
  120.2 0.7 model.1
  (20 shorter events, 0.1 us)
Async XLA Ops:
  3.0 10.0 %collective-permute-start = (f32[1112,128]{1,0:T(8,128)S(1)}, f32[1112,128]{1,0:T(8,128)S(1)}, u32[]{:S(2)}, u32[]{:S(2)}) collective-permute-start(f32[1112,128]{1,0:T(8,128)S(1)} %get-tuple-element.52), channel_id=1, source_target_pairs={{0,1},{1,0},{2,3},{3,2},{4,5},{5,4},{6,7},{7,6},{8,9},{9,8},{10,11... | collective-permute-start | bytes 1708040 | tf_op jit(solution)/shard_map/ppermute | solution.py:497
  4.5 16.8 %collective-permute-start.2 = (f32[1112,128]{1,0:T(8,128)S(1)}, f32[1112,128]{1,0:T(8,128)S(1)}, u32[]{:S(2)}, u32[]{:S(2)}) collective-permute-start(f32[1112,128]{1,0:T(8,128)S(1)} %get-tuple-element.52), channel_id=1, source_target_pairs={{2,0},{4,2},{6,4},{8,6},{10,8},{12,10},{14,12},{16,14},{18,16},{20... | collective-permute-start | bytes 1708040 | tf_op jit(solution)/shard_map/ppermute | solution.py:493
  5.8 16.5 %collective-permute-start.1 = (f32[1112,128]{1,0:T(8,128)S(1)}, f32[1112,128]{1,0:T(8,128)S(1)}, u32[]{:S(2)}, u32[]{:S(2)}) collective-permute-start(f32[1112,128]{1,0:T(8,128)S(1)} %get-tuple-element.52), channel_id=1, source_target_pairs={{0,2},{2,4},{4,6},{6,8},{8,10},{10,12},{12,14},{14,16},{16,18},{18... | collective-permute-start | bytes 1708040 | tf_op jit(solution)/shard_map/ppermute | solution.py:493
  13.0 4.3 %copy-start = (f32[2,512,128]{2,1,0:T(8,128)S(1)}, f32[2,512,128]{2,1,0:T(8,128)}, u32[]{:S(2)}) copy-start(f32[2,512,128]{2,1,0:T(8,128)} %slow) | copy-start | bytes 1572868
  13.1 4.3 %copy-start.1 = (f32[4]{0:T(128)S(1)}, f32[4]{0:T(128)}, u32[]{:S(2)}) copy-start(f32[4]{0:T(128)} %damp.11) | copy-start | bytes 52
  16.0 10.8 %collective-permute-start.3 = (f32[88,128]{1,0:T(8,128)S(1)}, f32[88,128]{1,0:T(8,128)S(1)}, u32[]{:S(2)}, u32[]{:S(2)}) collective-permute-start(f32[88,128]{1,0:T(8,128)S(1)} %get-tuple-element.57), channel_id=1, source_target_pairs={{4,0},{6,2},{8,4},{10,6},{12,8},{14,10},{16,12},{18,14},{20,16},{2... | collective-permute-start | bytes 135176 | tf_op jit(solution)/shard_map/ppermute | solution.py:493
  26.9 5.7 %collective-permute-start.4 = (f32[2224,128]{1,0:T(8,128)S(1)}, f32[2224,128]{1,0:T(8,128)S(1)}, u32[]{:S(2)}, u32[]{:S(2)}) collective-permute-start(f32[2224,128]{1,0:T(8,128)S(1)} %pad_maximum_fusion), channel_id=1, source_target_pairs={{0,1},{1,0},{2,3},{3,2},{4,5},{5,4},{6,7},{7,6},{8,9},{9,8},{10,11... | collective-permute-start | bytes 3416072 | tf_op jit(solution)/shard_map/ppermute | solution.py:497
  45.6 3.7 %collective-permute-start.7 = (f32[8,128]{1,0:T(8,128)S(1)}, f32[8,128]{1,0:T(8,128)S(1)}, u32[]{:S(2)}, u32[]{:S(2)}) collective-permute-start(f32[8,128]{1,0:T(8,128)S(1)} %get-tuple-element.72), channel_id=1, source_target_pairs={{0,6},{2,4},{4,2},{6,0},{8,14},{10,12},{12,10},{14,8},{16,22},{18,... | collective-permute-start | bytes 12296 | tf_op jit(solution)/shard_map/ppermute | solution.py:502
  48.0 4.0 %collective-permute-start.6 = (f32[8,128]{1,0:T(8,128)S(1)}, f32[8,128]{1,0:T(8,128)S(1)}, u32[]{:S(2)}, u32[]{:S(2)}) collective-permute-start(f32[8,128]{1,0:T(8,128)S(1)} %get-tuple-element.72), channel_id=1, source_target_pairs={{0,4},{2,6},{4,0},{6,2},{8,12},{10,14},{12,8},{14,10},{16,20},{18,... | collective-permute-start | bytes 12296 | tf_op jit(solution)/shard_map/ppermute | solution.py:502
  48.0 4.0 %collective-permute-start.5 = (f32[8,128]{1,0:T(8,128)S(1)}, f32[8,128]{1,0:T(8,128)S(1)}, u32[]{:S(2)}, u32[]{:S(2)}) collective-permute-start(f32[8,128]{1,0:T(8,128)S(1)} %get-tuple-element.72), channel_id=1, source_target_pairs={{0,2},{2,0},{4,6},{6,4},{8,10},{10,8},{12,14},{14,12},{16,18},{18,... | collective-permute-start | bytes 12296 | tf_op jit(solution)/shard_map/ppermute | solution.py:502
  52.0 7.1 %collective-permute-start.10 = (f32[8,128]{1,0:T(8,128)S(1)}, f32[8,128]{1,0:T(8,128)S(1)}, u32[]{:S(2)}, u32[]{:S(2)}) collective-permute-start(f32[8,128]{1,0:T(8,128)S(1)} %add_add_fusion.3), channel_id=1, source_target_pairs={{0,24},{2,26},{4,28},{6,30},{8,16},{10,18},{12,20},{14,22},{16,8},... | collective-permute-start | bytes 12296 | tf_op jit(solution)/shard_map/ppermute | solution.py:502
  55.4 4.0 %collective-permute-start.9 = (f32[8,128]{1,0:T(8,128)S(1)}, f32[8,128]{1,0:T(8,128)S(1)}, u32[]{:S(2)}, u32[]{:S(2)}) collective-permute-start(f32[8,128]{1,0:T(8,128)S(1)} %add_add_fusion.3), channel_id=1, source_target_pairs={{0,16},{2,18},{4,20},{6,22},{8,24},{10,26},{12,28},{14,30},{16,0},... | collective-permute-start | bytes 12296 | tf_op jit(solution)/shard_map/ppermute | solution.py:502
  55.5 3.9 %collective-permute-start.8 = (f32[8,128]{1,0:T(8,128)S(1)}, f32[8,128]{1,0:T(8,128)S(1)}, u32[]{:S(2)}, u32[]{:S(2)}) collective-permute-start(f32[8,128]{1,0:T(8,128)S(1)} %add_add_fusion.3), channel_id=1, source_target_pairs={{0,8},{2,10},{4,12},{6,14},{8,0},{10,2},{12,4},{14,6},{16,24},{18,... | collective-permute-start | bytes 12296 | tf_op jit(solution)/shard_map/ppermute | solution.py:502
  67.9 3.7 %collective-permute-start.13 = (f32[8,128]{1,0:T(8,128)S(1)}, f32[8,128]{1,0:T(8,128)S(1)}, u32[]{:S(2)}, u32[]{:S(2)}) collective-permute-start(f32[8,128]{1,0:T(8,128)S(1)} %get-tuple-element.83), channel_id=1, source_target_pairs={{0,6},{2,4},{4,2},{6,0},{8,14},{10,12},{12,10},{14,8},{16,22},{18,... | collective-permute-start | bytes 12296 | tf_op jit(solution)/shard_map/ppermute | solution.py:502
  70.1 4.0 %collective-permute-start.12 = (f32[8,128]{1,0:T(8,128)S(1)}, f32[8,128]{1,0:T(8,128)S(1)}, u32[]{:S(2)}, u32[]{:S(2)}) collective-permute-start(f32[8,128]{1,0:T(8,128)S(1)} %get-tuple-element.83), channel_id=1, source_target_pairs={{0,4},{2,6},{4,0},{6,2},{8,12},{10,14},{12,8},{14,10},{16,20},{18,... | collective-permute-start | bytes 12296 | tf_op jit(solution)/shard_map/ppermute | solution.py:502
  70.9 3.2 %collective-permute-start.11 = (f32[8,128]{1,0:T(8,128)S(1)}, f32[8,128]{1,0:T(8,128)S(1)}, u32[]{:S(2)}, u32[]{:S(2)}) collective-permute-start(f32[8,128]{1,0:T(8,128)S(1)} %get-tuple-element.83), channel_id=1, source_target_pairs={{0,2},{2,0},{4,6},{6,4},{8,10},{10,8},{12,14},{14,12},{16,18},{18,... | collective-permute-start | bytes 12296 | tf_op jit(solution)/shard_map/ppermute | solution.py:502
  74.1 3.9 %collective-permute-start.16 = (f32[8,128]{1,0:T(8,128)S(1)}, f32[8,128]{1,0:T(8,128)S(1)}, u32[]{:S(2)}, u32[]{:S(2)}) collective-permute-start(f32[8,128]{1,0:T(8,128)S(1)} %add_add_fusion.1), channel_id=1, source_target_pairs={{0,24},{2,26},{4,28},{6,30},{8,16},{10,18},{12,20},{14,22},{16,8},... | collective-permute-start | bytes 12296 | tf_op jit(solution)/shard_map/ppermute | solution.py:502
  76.4 4.0 %collective-permute-start.15 = (f32[8,128]{1,0:T(8,128)S(1)}, f32[8,128]{1,0:T(8,128)S(1)}, u32[]{:S(2)}, u32[]{:S(2)}) collective-permute-start(f32[8,128]{1,0:T(8,128)S(1)} %add_add_fusion.1), channel_id=1, source_target_pairs={{0,16},{2,18},{4,20},{6,22},{8,24},{10,26},{12,28},{14,30},{16,0},... | collective-permute-start | bytes 12296 | tf_op jit(solution)/shard_map/ppermute | solution.py:502
  76.5 3.9 %collective-permute-start.14 = (f32[8,128]{1,0:T(8,128)S(1)}, f32[8,128]{1,0:T(8,128)S(1)}, u32[]{:S(2)}, u32[]{:S(2)}) collective-permute-start(f32[8,128]{1,0:T(8,128)S(1)} %add_add_fusion.1), channel_id=1, source_target_pairs={{0,8},{2,10},{4,12},{6,14},{8,0},{10,2},{12,4},{14,6},{16,24},{18,... | collective-permute-start | bytes 12296 | tf_op jit(solution)/shard_map/ppermute | solution.py:502
  81.6 12.9 %copy-start.2 = (f32[3,2,128,128]{3,2,1,0:T(8,128)S(1)}, f32[3,2,128,128]{3,2,1,0:T(8,128)}, u32[]{:S(2)}) copy-start(f32[3,2,128,128]{3,2,1,0:T(8,128)} %dual) | copy-start | bytes 1179652
  81.7 6.7 %collective-permute-start.17 = (f32[4,2,128,128]{3,2,1,0:T(8,128)S(1)}, f32[4,2,128,128]{3,2,1,0:T(8,128)S(1)}, u32[]{:S(2)}, u32[]{:S(2)}) collective-permute-start(f32[4,2,128,128]{3,2,1,0:T(8,128)S(1)} %gradient.2), channel_id=1, source_target_pairs={{0,1},{1,0},{2,3},{3,2},{4,5},{5,4},{6,7},{7,6},{8,9},{9,8},{10,11... | collective-permute-start | bytes 1572872 | tf_op jit(solution)/shard_map/ppermute | solution.py:497
  90.5 12.9 %all-to-all-start = ((f32[4,2,128,128]{3,2,1,0:T(8,128)}), f32[4,2,128,128]{3,2,1,0:T(8,128)S(1)}, u32[]{:S(2)}, u32[]{:S(2)}) async-start(f32[4,2,128,128]{3,2,1,0:T(8,128)} %gradient.3), calls=%async_computation | async-start | bytes 1048576 | tf_op jit(solution)/shard_map/all_to_all | solution.py:631
  95.4 6.4 %collective-permute-start.18 = (f32[1,128,128]{2,1,0:T(8,128)S(1)}, f32[1,128,128]{2,1,0:T(8,128)S(1)}, u32[]{:S(2)}, u32[]{:S(2)}) collective-permute-start(f32[1,128,128]{2,1,0:T(8,128)S(1)} %get-tuple-element.94), channel_id=1, source_target_pairs={{0,1},{1,2},{2,3},{3,4},{4,5},{5,6},{6,7},{7,8},{8,9},{9,10},{10,1... | collective-permute-start | bytes 196616 | tf_op jit(solution)/shard_map/ppermute | solution.py:493
  97.4 4.4 %collective-permute-start.19 = (f32[2,8,128]{2,1,0:T(8,128)S(1)}, f32[2,8,128]{2,1,0:T(8,128)S(1)}, u32[]{:S(2)}, u32[]{:S(2)}) collective-permute-start(f32[2,8,128]{2,1,0:T(8,128)S(1)} %get-tuple-element.95), channel_id=1, source_target_pairs={{0,32},{32,64},{64,96},{1,33},{33,65},{65,97},{2,34},{34,66},{66,9... | collective-permute-start | bytes 24584 | tf_op jit(solution)/shard_map/ppermute | solution.py:493
where the time goes:
time: 121 us
  Pallas kernels  44.1 us (36%)
  starting transfers between devices  39 us (32%)
  waiting for transfers between devices  20.2 us (17%)
  blocking collectives  16.6 us (14%)
    all_to_all x1, blocking collectives, on_device(): power = lax.all_to_all(power, ('lap', 'pair', 'core'), 0, 0, tiled=True)  16.6 us
    pallas_call x5, Pallas kernels, scatter(): pl.pallas_call(kernel, out_shape=tuple((struct(*shape) for shape in shape...  15.8 us
    ppermute x12, starting transfers between devices, pair_sum(): lax.ppermute(x, 'pair', [(i, i ^ d) for i in range(16)])  14.1 us
    ppermute x5, starting transfers between devices, moved(): lax.ppermute(x, axis, [(i, i + by) for i in range(peers) if 0 <= i + by <...  12.5 us
    pallas_call x1, Pallas kernels, on_device(): pl.pallas_call(forward_kernel, out_shape=(struct(PLANES, ROWS, 128), stru...  9.99 us
    ppermute x12, waiting for transfers between devices, pair_sum(): lax.ppermute(x, 'pair', [(i, i ^ d) for i in range(16)])  9.23 us
    pallas_call x1, Pallas kernels, on_device(): pl.pallas_call(adjoint_kernel, out_shape=(struct(4, ROWS, 128), struct(13...  8.48 us
    ppermute x3, starting transfers between devices, swapped(): return lax.ppermute(x, 'core', [(0, 1), (1, 0)])  8.4 us
  transfers between devices with their start and end apart: 21, of which 13 were waited for; matrix products, arithmetic and copies ran while one was open for 0% of the time, Pallas kernels for 13%

commit v1 on v0

--- a/solution.py
+++ b/solution.py
@@ -32,21 +32,31 @@
 def spread_points(index, parts, right_planes, write):
     points = index.shape[1]
     column = (index >> 16) * 128 + (index & 127)
-    row = ((index >> 7) & 511) - lax.broadcasted_iota(jnp.int32, (8, points), 0) // HALF
-    lanes = lax.broadcasted_iota(jnp.int32, (right_planes * 128, points), 0)
+    row = (index >> 7) & 511
+    rows = ROWS
+    if right_planes == 1:
+        rows = ROWS // 2
+        column = jnp.where(index >> 16 == 0, (row >> 8) * 128 + (index & 127), -1)
+        row = row & 255
+    row = row - lax.broadcasted_iota(jnp.int32, (8, points), 0) // HALF
+    lanes = lax.broadcasted_iota(jnp.int32, (256, points), 0)
     right = jnp.where(lanes == column, 1.0, 0.0).astype(jnp.bfloat16)
-    tile = lax.broadcasted_iota(jnp.int32, (ROWS // 8, 8, points), 0)
+    tile = lax.broadcasted_iota(jnp.int32, (rows // 8, 8, points), 0)
     mask = row[None] == (8 // HALF) * tile
     for which, part in enumerate(parts):
         total = None
         for piece in part:
-            left = jnp.where(mask, piece[None], 0.0).reshape(ROWS, points).astype(jnp.bfloat16)
+            left = jnp.where(mask, piece[None], 0.0).reshape(rows, points).astype(jnp.bfloat16)
             got = lax.dot_general(
                 left, right, (((1,), (1,)), ((), ())), preferred_element_type=jnp.float32
             )
             total = got if total is None else total + got
-        for p in range(right_planes):
-            write(which, p, total[:, p * 128 : (p + 1) * 128])
+        lower, upper = total[:, 0:128], total[:, 128:256]
+        if right_planes == 1:
+            write(which, 0, jnp.concatenate([lower, upper]))
+        else:
+            write(which, 0, lower)
+            write(which, 1, upper)
 
 
 def pieces_of(value, count):
@@ -114,10 +124,11 @@
     offset = slab * (2 * 512 * 128)
     pairs = ((src_in, src), (rec_in, rec), (amp_in, amp), (obs_in, obs), (slow_in, out.at[0:ROWS]))
     copies = [pltpu.make_async_copy(x, y, sem.at[k]) for k, (x, y) in enumerate(pairs)]
-    for copy in copies:
+    for copy in copies[::-1]:
         copy.start()
-    for copy in copies:
+    for copy in copies[:4]:
         copy.wait()
+    far[80:88, :] = jnp.zeros((8, 128), jnp.float32)
     points = amp.shape[1]
     far[0:8, :] = (src[...] - offset).astype(jnp.float32)
     far[8:16, :] = (rec[...] - offset).astype(jnp.float32)
@@ -126,10 +137,16 @@
             for j in range(8):
                 at = 8 * (k + i) + j
                 far[at : at + 1, :] = values[i : i + 1, 128 * j : 128 * j + 128]
-    index = list_row(far, 0, 0).astype(jnp.int32)
+    out[ROWS : ROWS + LIST, :] = far[...]
+    for copy in copies[4:]:
+        copy.wait()
+
+
+def gather_sigma(sigma, row, store):
+    index = row(0).astype(jnp.int32)
+    points = index.shape[1]
     rows = lax.broadcasted_iota(jnp.int32, (ROWS, points), 0)
     pick = jnp.where(rows == index >> 7, 1.0, 0.0).astype(jnp.bfloat16)
-    sigma = out[0:ROWS, :]
     high = sigma.astype(jnp.bfloat16)
     low = (sigma - high.astype(jnp.float32)).astype(jnp.bfloat16)
     dims = (((0,), (0,)), ((), ()))
@@ -138,8 +155,7 @@
     lane = lax.broadcasted_iota(jnp.int32, (128, points), 0)
     found = jnp.sum(jnp.where(lane == index & 127, got, 0.0), axis=0, keepdims=True)
     for j in range(8):
-        far[80 + j : 81 + j, :] = found[:, 128 * j : 128 * j + 128]
-    out[ROWS : ROWS + LIST, :] = far[...]
+        store[80 + j : 81 + j, :] = found[:, 128 * j : 128 * j + 128]
 
 
 def scatter_slab(h, row, b, ob, cn):
@@ -152,24 +168,25 @@
     scatter_slab(lax.axis_index("core"), functools.partial(list_row, lists, 0), b, ob, cn)
 
 
-def scatter_other_kernel(lists, other, b_in, ob_in, cn_in, b, ob, cn, first):
+def scatter_other_kernel(mine, other, b_in, ob_in, cn_in, b, ob, cn, first):
     core = lax.axis_index("core")
-    first[...] = jnp.where(core == 0, lists[...], other[ROWS:SLAB, :])
+    whole = jnp.where(core == 0, mine[...], other[...])
+    first[...] = whole[ROWS:SLAB]
+    gather_sigma(whole[0:ROWS], functools.partial(list_row, first, 0), first)
     row = functools.partial(list_row, other, ROWS)
     scatter_slab(1 - lax.axis_index("core"), row, b, ob, cn)
 
 
-def scatter_near(core, damp, heavy, heavy_low, light, light_low, b):
+def scatter_near(core, heavy, heavy_low, light, light_low, b):
     scatter_src(core, heavy, 2, b, jnp.where(heavy_low, 2, 4))
-    divisor = jnp.where(light_low, diagonal_at(damp, light), 1.0)
-    scatter_src(core, light, 1, b, jnp.where(light_low, 0, 6), divisor)
-
-
-def scatter_mine_kernel(damp, low, high, b, ob, cn):
+    scatter_src(core, light, 1, b, jnp.where(light_low, 0, 6))
+
+
+def scatter_mine_kernel(low, high, b, ob, cn):
     core = lax.axis_index("core")
     heavy = either(core, (high, ROWS), (low, ROWS))
     light = either(core, (low, ROWS), (high, ROWS))
-    scatter_near(core, damp, heavy, core == 1, light, core == 0, b)
+    scatter_near(core, heavy, core == 1, light, core == 0, b)
     scatter_rec(core, heavy, 2, 2, ob, cn, jnp.where(core == 1, 0, 2))
 
 
@@ -178,7 +195,7 @@
     low_at, high_at = ROWS, SLAB + ROWS
     heavy = either(core, (near, low_at), (near, high_at))
     light = either(core, (near, high_at), (near, low_at))
-    scatter_near(core, damp, heavy, core == 0, light, core == 1, b)
+    scatter_near(core, heavy, core == 0, light, core == 1, b)
     last = functools.partial(list_row, far, 0)
     scatter_src(core, last, 1, b, 8, diagonal_at(damp, last), 1)
 
@@ -264,7 +281,8 @@
     return out
 
 
-def coefficients(moments):
+def coefficients(terms):
+    moments = (terms[0][...] + terms[1][...]) + (terms[2][...] + terms[3][...])
     m = [moments[k : k + 1, :] for k in range(6)]
 
     def product(p, shift):
@@ -299,7 +317,7 @@
     return (pattern[None] * x.reshape(ROWS // 8, 8, 128)).reshape(ROWS, 128)
 
 
-def fill_inverse(core, square, inv, slab, mine, theirs, base, valid, first=0):
+def fill_inverse(core, square, inv, slab, mine, theirs, base, valid):
     def fill(p, _):
         at = pl.multiple_of(p * 512, 512)
         here = mine[pl.ds(at, 512), :]
@@ -309,7 +327,7 @@
             inv[2 * slab + p, pl.ds(c, 512, stride=HALF), :] = valid / (6.0 + square[c] * sigma)
         return 0
 
-    lax.fori_loop(first, 2, fill, 0)
+    lax.fori_loop(0, 2, fill, 0)
 
 
 def forward_own_kernel(damp, own_m, own_t, b_own, inv, v0, v1, held):
@@ -337,7 +355,7 @@
     high = jnp.where(pair + 1 < lax.axis_size("pair"), 1.0, 0.0)
     square = squares(damp)
     clear_pads(v2)
-    fill_inverse(core, square, inv, 0, low_m, near_t, 0, low, 1)
+    fill_inverse(core, square, inv, 0, low_m, near_t, 0, low)
     fill_inverse(core, square, inv, 1, low_m, near_t, 0, low)
     fill_inverse(core, square, inv, 4, high_m, near_t, SLAB, high)
     fill_inverse(core, square, inv, 5, high_m, near_t, SLAB, high)
@@ -349,9 +367,8 @@
 
         return body
 
-    for t, k in ((0, 0), (1, 1), (12, 8)):
-        v0[t, INNER, :] = b_near[k]
-    walk(2, 4, start(0), 0)
+    v0[12, INNER, :] = b_near[8]
+    walk(0, 4, start(0), 0)
     walk(8, 12, start(4), 0)
     advance(v0, 0, inv, 0, v1, 1, 1, 4, False)
     m1, m2 = advance(v0, 0, inv, 0, v1, 1, 4, 5, True)
@@ -367,9 +384,9 @@
 
 
 def adjoint_kernel(
-    total, inv, v0, v1, v2, ob_own, cn_own, ob_near, cn_near, wave, u0, u1, u2, msg
+    t0, t1, t2, t3, inv, v0, v1, v2, ob_own, cn_own, ob_near, cn_near, wave, u0, u1, u2, msg
 ):
-    a = coefficients(total[...])
+    a = coefficients((t0, t1, t2, t3))
 
     def start(ob, cn, off, own):
         def body(t, carry):
@@ -398,14 +415,15 @@
     msg[...] = message([m0, m1, m2, m3, m4, m5])
 
 
-def gradient_kernel(other, damp, total, wave, u0, u1, u2, *rest):
-    out, held = rest[-2:]
-    a = coefficients(total[...])
+def gradient_kernel(other, damp, t0, t1, t2, t3, wave, u0, u1, u2, *rest):
+    held = rest[-1]
+    a = coefficients((t0, t1, t2, t3))
     sub = lax.broadcasted_iota(jnp.int32, (8, 128), 0)
     square = jnp.where(sub % HALF == 0, *squares(damp))
     a = [-square * v for v in a]
     core = lax.axis_index("core")
     core = 1 - core if other else core
+    bands = rest[0] if other else rest[-2]
     for p in range(2):
         t = 4 + 2 * core + p
         x = times(a[0], u0[t, INNER, :]) + times(a[1], u1[t - 1, INNER, :])
@@ -414,11 +432,15 @@
         for band in range(4):
             at = band * 256
             both = held[pl.ds(at, 128, stride=HALF), :] + held[pl.ds(at + 1, 128, stride=HALF), :]
-            out[band, p] = both if other else both + rest[0][band, p]
-
-
-def power_kernel(parts, own, msg):
-    g = (parts[0] + parts[1]) + (parts[2] + parts[3])
+            bands[band, p] = both if other else both + rest[0][band, p]
+    if not other:
+        lap = lax.axis_index("lap")
+        for d in range(4):
+            rest[1 + d][...] = bands[lap ^ d]
+
+
+def power_kernel(g0, g1, g2, g3, own, msg):
+    g = (g0[...] + g1[...]) + (g2[...] + g3[...])
     own[...] = g
     msg[...] = jnp.full((128, 128), jnp.sum(g * g), jnp.float32)
 
@@ -498,9 +520,11 @@
 
 
 def pair_sum(x):
-    for masks in ((1, 2, 3), (4, 8, 12)):
-        x = x + sum(lax.ppermute(x, "pair", [(i, i ^ d) for i in range(16)]) for d in masks)
-    return x
+    def others(x, masks):
+        return [lax.ppermute(x, "pair", [(i, i ^ d) for i in range(16)]) for d in masks]
+
+    x = x + sum(others(x, (1, 2, 3)))
+    return [x] + others(x, (4, 8, 12))
 
 
 def scatter(kernel, name, work, inputs, shapes, into=()):
@@ -512,7 +536,7 @@
         in_specs=[SMEM] * scalars + [VMEM] * (len(inputs) - scalars + len(into)),
         out_specs=(VMEM,) * len(shapes),
         input_output_aliases={first + k: k for k in range(len(into))},
-        compiler_params=params(12),
+        compiler_params=params(8),
         cost_estimate=cost(work),
         name=name,
     )(*inputs, *into)
@@ -550,7 +574,7 @@
     block, near_block = (4, ROWS, 128), (5, ROWS, 128)
     own = scatter(scatter_own_kernel, "scatter_own", 5, (lists,), [block] * 3)
     b_own, ob_own, cn_own, first = scatter(
-        scatter_other_kernel, "scatter_other", 5, (lists, own_t), [block] * 3 + [(LIST, 128)], own
+        scatter_other_kernel, "scatter_other", 5, (packed, own_t), [block] * 3 + [(LIST, 128)], own
     )
     far_m = moved(first, "pair", -2)
     padded = ROWS + 2 * PAD
@@ -562,14 +586,14 @@
         ),
         in_specs=[SMEM] + [VMEM] * 3,
         out_specs=(VMEM,) * 4,
-        compiler_params=params(8),
+        compiler_params=params(2),
         cost_estimate=cost(4),
         name="forward_own",
     )(damping, slowness.reshape(ROWS, 128), own_t, b_own)
     low_m, high_m, far_m, held = lax.optimization_barrier((low_m, high_m, far_m, held))
     near_t = swapped(jnp.concatenate([low_m, high_m]))
     b_near, ob_near, cn_near = scatter(
-        scatter_mine_kernel, "scatter_mine", 6, (damping, low_m, high_m),
+        scatter_mine_kernel, "scatter_mine", 6, (low_m, high_m),
         [(9, ROWS, 128), near_block, near_block],
     )
     near_t, b_near = lax.optimization_barrier((near_t, b_near))
@@ -587,7 +611,7 @@
         in_specs=[SMEM] + [VMEM] * 8,
         out_specs=(VMEM,) * 5,
         input_output_aliases={6: 0, 7: 1, 8: 2},
-        compiler_params=params(8),
+        compiler_params=params(2),
         cost_estimate=cost(20),
         name="forward",
     )(damping, low_m, high_m, near_t, b_near, held, inv, v0, v1)
@@ -603,32 +627,36 @@
             struct(4, ROWS, 128), struct(13, padded, 128), struct(11, padded, 128),
             struct(9, padded, 128), struct(8, 128),
         ),
-        in_specs=[VMEM] * 9,
+        in_specs=[VMEM] * 12,
         out_specs=(VMEM,) * 5,
-        input_output_aliases={2: 1, 3: 2, 4: 3},
-        compiler_params=params(8),
+        input_output_aliases={5: 1, 6: 2, 7: 3},
+        compiler_params=params(2),
         cost_estimate=cost(14),
         name="adjoint",
-    )(pair_sum(msg), inv, v0, v1, v2, ob_own, cn_own, ob_near, cn_near)
-
-    total = pair_sum(msg)
+    )(*pair_sum(msg), inv, v0, v1, v2, ob_own, cn_own, ob_near, cn_near)
+
+    terms = pair_sum(msg)
 
     def gradient(other, *more):
+        bands = (4, 2, 128, 128)
+        scratch = [] if other else [pltpu.VMEM(bands, jnp.float32)]
         return pl.pallas_call(
             functools.partial(gradient_kernel, other),
-            out_shape=struct(4, 2, 128, 128),
-            in_specs=[SMEM] + [VMEM] * (5 + len(more)),
-            out_specs=VMEM,
-            scratch_shapes=[pltpu.VMEM((ROWS, 128), jnp.float32)],
+            out_shape=struct(*bands) if other else (struct(*bands[1:]),) * 4,
+            in_specs=[SMEM] + [VMEM] * (8 + len(more)),
+            out_specs=VMEM if other else (VMEM,) * 4,
+            scratch_shapes=scratch + [pltpu.VMEM((ROWS, 128), jnp.float32)],
             compiler_params=params(8),
             name="gradient",
-        )(damping, total, wave, u0, u1, u2, *more)
-
-    parts = gradient(False, swapped(gradient(True)))
-    slowness, dual, own_t, near_t, parts = lax.optimization_barrier(
-        (slowness, dual, own_t, near_t, parts)
+        )(damping, *terms, wave, u0, u1, u2, *more)
+
+    bands = gradient(False, swapped(gradient(True)))
+    slowness, dual, own_t, near_t, bands = lax.optimization_barrier(
+        (slowness, dual, own_t, near_t, bands)
     )
-    arrived = lax.all_to_all(parts, "lap", 0, 0, tiled=True)
+    arrived = [bands[0]] + [
+        lax.ppermute(bands[d], "lap", [(i, i ^ d) for i in range(4)]) for d in (1, 2, 3)
+    ]
     dual_next, base, send_x, send_y = pl.pallas_call(
         variation_kernel,
         out_shape=(
@@ -646,11 +674,11 @@
     own_grad, power = pl.pallas_call(
         power_kernel,
         out_shape=(struct(2, 128, 128), struct(128, 128)),
-        in_specs=[VMEM],
+        in_specs=[VMEM] * 4,
         out_specs=(VMEM, VMEM),
         compiler_params=params(8),
         name="power",
-    )(arrived)
+    )(*arrived)
     power = lax.all_to_all(power, ("lap", "pair", "core"), 0, 0, tiled=True)
     model = pl.pallas_call(
         functools.partial(model_kernel, float(slab_cells * 2 * pairs)),

time: 121 us -> 118 us (0.975)
  Pallas kernels: 44.1 us -> 42.3 us
    all_to_all x1 -> x0, starting transfers between devices: 4.02 us -> none  [on_device(): arrived = lax.all_to_all(parts, 'lap', 0, 0, tiled=True)]
    ppermute x12 -> x15, starting transfers between devices: 14.1 us -> 18.1 us  [the longest x12 14.1 us: others(): lax.ppermute(x, 'pair', [(i, i ^ d) for i in range(16)])]
    ppermute x12 -> x15, waiting for transfers between devices: 9.23 us -> 10.9 us  [the longest x12 9.24 us: others(): lax.ppermute(x, 'pair', [(i, i ^ d) for i in range(16)])]
    all_to_all x1 -> x0, waiting for transfers between devices: 1.57 us -> none  [on_device(): arrived = lax.all_to_all(parts, 'lap', 0, 0, tiled=True)]
    pallas_call x1, Pallas kernels: 2.36 us -> 1.09 us  [on_device(): pl.pallas_call(pack_kernel, out_shape=(struct(SLAB, 128), struct(LIST, 12...]
  transfers between devices with their start and end apart: 21 -> 23, of which waited for: 13 -> 13; matrix products, arithmetic and copies ran while one was open for 0% -> 0% of each run, Pallas kernels for 13% -> 14%
where the time goes in v1:
time: 118 us
  Pallas kernels  42.3 us (36%)
  starting transfers between devices  38.3 us (32%)
  waiting for transfers between devices  19.2 us (16%)
  blocking collectives  17.5 us (15%)
    all_to_all x1, blocking collectives, on_device(): power = lax.all_to_all(power, ('lap', 'pair', 'core'), 0, 0, tiled=True)  17.5 us
    pallas_call x5, Pallas kernels, scatter(): pl.pallas_call(kernel, out_shape=tuple((struct(*shape) for shape in shape...  15.5 us
    ppermute x12, starting transfers between devices, others(): lax.ppermute(x, 'pair', [(i, i ^ d) for i in range(16)])  14.1 us
    ppermute x5, starting transfers between devices, moved(): lax.ppermute(x, axis, [(i, i + by) for i in range(peers) if 0 <= i + by <...  11.8 us
    pallas_call x1, Pallas kernels, on_device(): pl.pallas_call(forward_kernel, out_shape=(struct(PLANES, ROWS, 128), stru...  9.97 us
    ppermute x12, waiting for transfers between devices, others(): lax.ppermute(x, 'pair', [(i, i ^ d) for i in range(16)])  9.24 us
    pallas_call x1, Pallas kernels, on_device(): pl.pallas_call(adjoint_kernel, out_shape=(struct(4, ROWS, 128), struct(13...  8.81 us
    ppermute x3, starting transfers between devices, swapped(): return lax.ppermute(x, 'core', [(0, 1), (1, 0)])  8.41 us
  transfers between devices with their start and end apart: 23, of which 13 were waited for; matrix products, arithmetic and copies ran while one was open for 0% of the time, Pallas kernels for 14%

profile of v1, /device:TPU:1, one launch (start us, length us, event | category | flops | bytes accessed | tf_op | source)
XLA Modules:
  0.0 118.2 jit_solution(6941051934911014901)
XLA Ops:
  0.6 1.1 pack.1
  1.7 1.5 %collective-permute-start = (f32[1112,128]{1,0:T(8,128)S(1)}, f32[1112,128]{1,0:T(8,128)S(1)}, u32[]{:S(2)}, u32[]{:S(2)}) collective-permute-start(f32[1112,128]{1,0:T(8,128)S(1)} %get-tuple-element.62.mine), channel_id=1, source_target_pairs={{0,1},{1,0},{2,3},{3,2},{4,5},{5,4},{6,7},{7,6},{8,9},{9,8},{10,11... | collective-permute-start | bytes 1708040 | tf_op jit(solution)/shard_map/ppermute | solution.py:519
  3.2 1.3 %collective-permute-start.2 = (f32[1112,128]{1,0:T(8,128)S(1)}, f32[1112,128]{1,0:T(8,128)S(1)}, u32[]{:S(2)}, u32[]{:S(2)}) collective-permute-start(f32[1112,128]{1,0:T(8,128)S(1)} %get-tuple-element.62.mine), channel_id=1, source_target_pairs={{2,0},{4,2},{6,4},{8,6},{10,8},{12,10},{14,12},{16,14},{18,16},{20... | collective-permute-start | bytes 1708040 | tf_op jit(solution)/shard_map/ppermute | solution.py:515
  4.5 4.3 %collective-permute-start.1 = (f32[1112,128]{1,0:T(8,128)S(1)}, f32[1112,128]{1,0:T(8,128)S(1)}, u32[]{:S(2)}, u32[]{:S(2)}) collective-permute-start(f32[1112,128]{1,0:T(8,128)S(1)} %get-tuple-element.62.mine), channel_id=1, source_target_pairs={{0,2},{2,4},{4,6},{6,8},{8,10},{10,12},{12,14},{14,16},{16,18},{18... | collective-permute-start | bytes 1708040 | tf_op jit(solution)/shard_map/ppermute | solution.py:515
  8.8 2.9 %scatter_own.1 = (f32[4,1024,128]{2,1,0:T(8,128)S(1)}, f32[4,1024,128]{2,1,0:T(8,128)S(1)}, f32[4,1024,128]{2,1,0:T(8,128)S(1)}) custom-call(f32[88,128]{1,0:T(8,128)S(1)} %get-tuple-element.63.lists), custom_call_target="tpu_custom_call" | custom-call | flops 5000000000 | bytes 1000000 | tf_op jit(solution)/shard_map/scatter_own/pallas_call | solution.py:533
  11.8 4.0 %scatter_other.1 = (f32[4,1024,128]{2,1,0:T(8,128)S(1)}, f32[4,1024,128]{2,1,0:T(8,128)S(1)}, f32[4,1024,128]{2,1,0:T(8,128)S(1)}, f32[88,128]{1,0:T(8,128)S(1)}) custom-call(f32[1112,128]{1,0:T(8,128)S(1)} %get-tuple-element.62.mine, f32[1112,128]{1,0:T(8,128)S(1)} %collective-permute-done.other.own_t, ...), custom_call_target="tpu_custom_call", output_to_operand_aliasing={{0}: (2, {}), {1}: (3, {}), {2}: (4, {})} | custom-call | flops 5000000000 | bytes 1000000 | tf_op jit(solution)/shard_map/scatter_other/pallas_call | solution.py:533
  15.8 1.3 %collective-permute-start.3 = (f32[88,128]{1,0:T(8,128)S(1)}, f32[88,128]{1,0:T(8,128)S(1)}, u32[]{:S(2)}, u32[]{:S(2)}) collective-permute-start(f32[88,128]{1,0:T(8,128)S(1)} %get-tuple-element.67), channel_id=1, source_target_pairs={{4,0},{6,2},{8,4},{10,6},{12,8},{14,10},{16,12},{18,14},{20,16},{2... | collective-permute-start | bytes 135176 | tf_op jit(solution)/shard_map/ppermute | solution.py:515
  17.1 2.4 %forward_own.1 = (f32[13,1024,128]{2,1,0:T(8,128)S(1)}, f32[13,1040,128]{2,1,0:T(8,128)S(1)}, f32[11,1040,128]{2,1,0:T(8,128)S(1)}, f32[24,128]{1,0:T(8,128)S(1)}) custom-call(f32[4]{0:T(128)S(1)} %copy-done.1, f32[1024,128]{1,0:T(8,128)S(1)} %bitcast.8, f32[1112,128]{1,0:T(8,128)S(1)} %collective-permute-done.other.own_t, ...), custom_call_target="tpu_custom_call" | custom-call | flops 4000000000 | bytes 1000000 | tf_op jit(solution)/shard_map/forward_own/pallas_call | solution.py:581
  19.6 0.5 collective-permute-done.2.high.high_m
  20.1 1.0 collective-permute-done.1.low.low_m
  21.0 4.5 %collective-permute-done.3.far = f32[88,128]{1,0:T(8,128)S(1)} collective-permute-done((f32[88,128]{1,0:T(8,128)S(1)}, f32[88,128]{1,0:T(8,128)S(1)}, u32[]{:S(2)}, u32[]{:S(2)}) %collective-permute-start.3) | collective-permute-done | bytes 45088 | tf_op jit(solution)/shard_map/ppermute | solution.py:515
  25.6 1.7 %collective-permute-start.4 = (f32[2224,128]{1,0:T(8,128)S(1)}, f32[2224,128]{1,0:T(8,128)S(1)}, u32[]{:S(2)}, u32[]{:S(2)}) collective-permute-start(f32[2224,128]{1,0:T(8,128)S(1)} %pad_maximum_fusion), channel_id=1, source_target_pairs={{0,1},{1,0},{2,3},{3,2},{4,5},{5,4},{6,7},{7,6},{8,9},{9,8},{10,11... | collective-permute-start | bytes 3416072 | tf_op jit(solution)/shard_map/ppermute | solution.py:519
  27.3 3.5 %scatter_mine.1 = (f32[9,1024,128]{2,1,0:T(8,128)S(1)}, f32[5,1024,128]{2,1,0:T(8,128)S(1)}, f32[5,1024,128]{2,1,0:T(8,128)S(1)}) custom-call(f32[1112,128]{1,0:T(8,128)S(1)} %collective-permute-done.1.low.low_m, f32[1112,128]{1,0:T(8,128)S(1)} %collective-permute-done.2.high.high_m), custom_call_target="tpu_custom_call" | custom-call | flops 6000000000 | bytes 1000000 | tf_op jit(solution)/shard_map/scatter_mine/pallas_call | solution.py:533
  30.9 2.7 %scatter_theirs.1.b_near = f32[9,1024,128]{2,1,0:T(8,128)S(1)} custom-call(f32[4]{0:T(128)S(1)} %copy-done.1, f32[88,128]{1,0:T(8,128)S(1)} %collective-permute-done.3.far, f32[2224,128]{1,0:T(8,128)S(1)} %collective-permute-done.4.near.near_t, f32[9,1024,128]{2,1,0:T(8,128)S(1)} %get-tuple-element.75.b_in), custom_call_target="tpu_custom_call", output_to_operand_aliasing={{}: (3, {})} | custom-call | flops 5000000000 | bytes 1000000 | tf_op jit(solution)/shard_map/scatter_theirs/pallas_call | solution.py:533
  33.5 10.0 %forward.1 = (f32[13,1024,128]{2,1,0:T(8,128)S(1)}, f32[13,1040,128]{2,1,0:T(8,128)S(1)}, f32[11,1040,128]{2,1,0:T(8,128)S(1)}, f32[9,1040,128]{2,1,0:T(8,128)S(1)}, f32[8,128]{1,0:T(8,128)S(1)}) custom-call(f32[4]{0:T(128)S(1)} %copy-done.1, ...), custom_call_target="tpu_custom_call", output_to_operand_aliasing={{0}: (6, {}), {1}: (7, {}), {2}: (8, {})} | custom-call | flops 20000000000 | bytes 1000000 | tf_op jit(solution)/shard_map/forward/pallas_call | solution.py:605
  43.5 3.5 %collective-permute-start.7 = (f32[8,128]{1,0:T(8,128)S(1)}, f32[8,128]{1,0:T(8,128)S(1)}, u32[]{:S(2)}, u32[]{:S(2)}) collective-permute-start(f32[8,128]{1,0:T(8,128)S(1)} %get-tuple-element.82), channel_id=1, source_target_pairs={{0,6},{2,4},{4,2},{6,0},{8,14},{10,12},{12,10},{14,8},{16,22},{18,... | collective-permute-start | bytes 12296 | tf_op jit(solution)/shard_map/ppermute | solution.py:524
  47.0 0.7 collective-permute-start.5
  47.6 0.3 collective-permute-done.7
  48.0 3.0 %collective-permute-done.6 = f32[8,128]{1,0:T(8,128)S(1)} collective-permute-done((f32[8,128]{1,0:T(8,128)S(1)}, f32[8,128]{1,0:T(8,128)S(1)}, u32[]{:S(2)}, u32[]{:S(2)}) %collective-permute-start.6) | collective-permute-done | bytes 4128 | tf_op jit(solution)/shard_map/ppermute | solution.py:524
  50.9 2.4 %collective-permute-start.10 = (f32[8,128]{1,0:T(8,128)S(1)}, f32[8,128]{1,0:T(8,128)S(1)}, u32[]{:S(2)}, u32[]{:S(2)}) collective-permute-start(f32[8,128]{1,0:T(8,128)S(1)} %add_add_fusion.1.t0), channel_id=1, source_target_pairs={{0,24},{2,26},{4,28},{6,30},{8,16},{10,18},{12,20},{14,22},{16,8},... | collective-permute-start | bytes 12296 | tf_op jit(solution)/shard_map/ppermute | solution.py:524
  53.4 0.8 collective-permute-start.9
  54.3 2.4 %scatter_late.1 = (f32[5,1024,128]{2,1,0:T(8,128)S(1)}, f32[5,1024,128]{2,1,0:T(8,128)S(1)}) custom-call(f32[1112,128]{1,0:T(8,128)S(1)} %collective-permute-done.2.high.high_m, f32[2224,128]{1,0:T(8,128)S(1)} %collective-permute-done.4.near.near_t, f32[5,1024,128]{2,1,0:T(8,128)S(1)} %get-tuple-element.89.ob_in, ...), custom_call_target="tpu_custom_call", output_to_operand_aliasing={{0}: (2, {}), {1}: (3, {})} | custom-call | flops 5000000000 | bytes 1000000 | tf_op jit(solution)/shard_map/scatter_late/pallas_call | solution.py:533
  56.7 0.7 collective-permute-done.9.t2
  57.3 8.8 %adjoint.1 = (f32[4,1024,128]{2,1,0:T(8,128)S(1)}, f32[13,1040,128]{2,1,0:T(8,128)S(1)}, f32[11,1040,128]{2,1,0:T(8,128)S(1)}, f32[9,1040,128]{2,1,0:T(8,128)S(1)}, f32[8,128]{1,0:T(8,128)S(1)}) custom-call(f32[8,128]{1,0:T(8,128)S(1)} %add_add_fusion.1.t0, ...), custom_call_target="tpu_custom_call", output_to_operand_aliasing={{1}: (5, {}), {2}: (6, {}), {3}: (7, {})} | custom-call | flops 14000000000 | bytes 1000000 | tf_op jit(solution)/shard_map/adjoint/pallas_call | solution.py:624
  66.2 2.2 %collective-permute-start.13 = (f32[8,128]{1,0:T(8,128)S(1)}, f32[8,128]{1,0:T(8,128)S(1)}, u32[]{:S(2)}, u32[]{:S(2)}) collective-permute-start(f32[8,128]{1,0:T(8,128)S(1)} %get-tuple-element.93), channel_id=1, source_target_pairs={{0,6},{2,4},{4,2},{6,0},{8,14},{10,12},{12,10},{14,8},{16,22},{18,... | collective-permute-start | bytes 12296 | tf_op jit(solution)/shard_map/ppermute | solution.py:524
  68.4 0.8 collective-permute-start.12
  69.2 0.3 collective-permute-start.11
  69.5 0.4 collective-permute-done.13
  69.9 2.4 %collective-permute-done.12 = f32[8,128]{1,0:T(8,128)S(1)} collective-permute-done((f32[8,128]{1,0:T(8,128)S(1)}, f32[8,128]{1,0:T(8,128)S(1)}, u32[]{:S(2)}, u32[]{:S(2)}) %collective-permute-start.12) | collective-permute-done | bytes 4128 | tf_op jit(solution)/shard_map/ppermute | solution.py:524
  72.3 1.8 %collective-permute-start.16 = (f32[8,128]{1,0:T(8,128)S(1)}, f32[8,128]{1,0:T(8,128)S(1)}, u32[]{:S(2)}, u32[]{:S(2)}) collective-permute-start(f32[8,128]{1,0:T(8,128)S(1)} %add_add_fusion.t0), channel_id=1, source_target_pairs={{0,24},{2,26},{4,28},{6,30},{8,16},{10,18},{12,20},{14,22},{16,8},... | collective-permute-start | bytes 12296 | tf_op jit(solution)/shard_map/ppermute | solution.py:524
  74.2 1.5 %collective-permute-start.14 = (f32[8,128]{1,0:T(8,128)S(1)}, f32[8,128]{1,0:T(8,128)S(1)}, u32[]{:S(2)}, u32[]{:S(2)}) collective-permute-start(f32[8,128]{1,0:T(8,128)S(1)} %add_add_fusion.t0), channel_id=1, source_target_pairs={{0,8},{2,10},{4,12},{6,14},{8,0},{10,2},{12,4},{14,6},{16,24},{18,... | collective-permute-start | bytes 12296 | tf_op jit(solution)/shard_map/ppermute | solution.py:524
  75.7 0.6 collective-permute-done.16.t3
  76.3 1.9 %collective-permute-done.15.t2 = f32[8,128]{1,0:T(8,128)S(1)} collective-permute-done((f32[8,128]{1,0:T(8,128)S(1)}, f32[8,128]{1,0:T(8,128)S(1)}, u32[]{:S(2)}, u32[]{:S(2)}) %collective-permute-start.15) | collective-permute-done | bytes 4128 | tf_op jit(solution)/shard_map/ppermute | solution.py:524
  78.1 1.3 %gradient.2 = f32[4,2,128,128]{3,2,1,0:T(8,128)S(1)} custom-call(f32[4]{0:T(128)S(1)} %copy-done.1, f32[8,128]{1,0:T(8,128)S(1)} %add_add_fusion.t0, f32[8,128]{1,0:T(8,128)S(1)} %collective-permute-done.14.t1, f32[8,128]{1,0:T(8,128)S(1)} %collective-permute-done.15.t2, f32[8,128]{1,0:T(8,128)S(1)} %collective-permute-done.16.t3, ...), custom_call_target="tpu_custom_call" | custom-call | tf_op jit(solution)/shard_map/gradient/pallas_call | solution.py:643
  79.4 5.2 %collective-permute-start.17 = (f32[4,2,128,128]{3,2,1,0:T(8,128)S(1)}, f32[4,2,128,128]{3,2,1,0:T(8,128)S(1)}, u32[]{:S(2)}, u32[]{:S(2)}) collective-permute-start(f32[4,2,128,128]{3,2,1,0:T(8,128)S(1)} %gradient.2), channel_id=1, source_target_pairs={{0,1},{1,0},{2,3},{3,2},{4,5},{5,4},{6,7},{7,6},{8,9},{9,8},{10,11... | collective-permute-start | bytes 1572872 | tf_op jit(solution)/shard_map/ppermute | solution.py:519
  84.6 1.5 %collective-permute-done.17.rest_0_ = f32[4,2,128,128]{3,2,1,0:T(8,128)S(1)} collective-permute-done((f32[4,2,128,128]{3,2,1,0:T(8,128)S(1)}, f32[4,2,128,128]{3,2,1,0:T(8,128)S(1)}, u32[]{:S(2)}, u32[]{:S(2)}) %collective-permute-start.17) | collective-permute-done | bytes 524320 | tf_op jit(solution)/shard_map/ppermute | solution.py:519
  86.2 1.3 %gradient.3 = (f32[2,128,128]{2,1,0:T(8,128)S(1)}, f32[2,128,128]{2,1,0:T(8,128)S(1)}, f32[2,128,128]{2,1,0:T(8,128)S(1)}, f32[2,128,128]{2,1,0:T(8,128)S(1)}) custom-call(f32[4]{0:T(128)S(1)} %copy-done.1, f32[8,128]{1,0:T(8,128)S(1)} %add_add_fusion.t0, f32[8,128]{1,0:T(8,128)S(1)} %collective-permute-done.14.t1, f32[8,128]{1,0:T(8,128)S(1)} %collective-permute-done.15.t2, ...), custom_call_target="tpu_custom_call" | custom-call | tf_op jit(solution)/shard_map/gradient/pallas_call | solution.py:643
  87.5 1.3 %collective-permute-start.18 = (f32[2,128,128]{2,1,0:T(8,128)S(1)}, f32[2,128,128]{2,1,0:T(8,128)S(1)}, u32[]{:S(2)}, u32[]{:S(2)}) collective-permute-start(f32[2,128,128]{2,1,0:T(8,128)S(1)} %get-tuple-element.108), channel_id=1, source_target_pairs={{0,32},{32,0},{64,96},{96,64},{1,33},{33,1},{65,97},{97,65},{2,34}... | collective-permute-start | bytes 393224 | tf_op jit(solution)/shard_map/ppermute | solution.py:658
  88.8 2.5 %collective-permute-start.19 = (f32[2,128,128]{2,1,0:T(8,128)S(1)}, f32[2,128,128]{2,1,0:T(8,128)S(1)}, u32[]{:S(2)}, u32[]{:S(2)}) collective-permute-start(f32[2,128,128]{2,1,0:T(8,128)S(1)} %get-tuple-element.109), channel_id=1, source_target_pairs={{0,64},{32,96},{64,0},{96,32},{1,65},{33,97},{65,1},{97,33},{2,66}... | collective-permute-start | bytes 393224 | tf_op jit(solution)/shard_map/ppermute | solution.py:658
  91.2 0.2 collective-permute-start.20
  91.4 0.9 variation.1
  92.4 3.1 %collective-permute-start.21 = (f32[1,128,128]{2,1,0:T(8,128)S(1)}, f32[1,128,128]{2,1,0:T(8,128)S(1)}, u32[]{:S(2)}, u32[]{:S(2)}) collective-permute-start(f32[1,128,128]{2,1,0:T(8,128)S(1)} %get-tuple-element.111), channel_id=1, source_target_pairs={{0,1},{1,2},{2,3},{3,4},{4,5},{5,6},{6,7},{7,8},{8,9},{9,10},{10,1... | collective-permute-start | bytes 196616 | tf_op jit(solution)/shard_map/ppermute | solution.py:515
  95.5 1.9 %collective-permute-start.22 = (f32[2,8,128]{2,1,0:T(8,128)S(1)}, f32[2,8,128]{2,1,0:T(8,128)S(1)}, u32[]{:S(2)}, u32[]{:S(2)}) collective-permute-start(f32[2,8,128]{2,1,0:T(8,128)S(1)} %get-tuple-element.112), channel_id=1, source_target_pairs={{0,32},{32,64},{64,96},{1,33},{33,65},{65,97},{2,34},{34,66},{66,9... | collective-permute-start | bytes 24584 | tf_op jit(solution)/shard_map/ppermute | solution.py:515
  97.4 0.8 collective-permute-done.22.prior_y
  98.2 1.7 %collective-permute-done.20.g3 = f32[2,128,128]{2,1,0:T(8,128)S(1)} collective-permute-done((f32[2,128,128]{2,1,0:T(8,128)S(1)}, f32[2,128,128]{2,1,0:T(8,128)S(1)}, u32[]{:S(2)}, u32[]{:S(2)}) %collective-permute-start.20) | collective-permute-done | bytes 131104 | tf_op jit(solution)/shard_map/ppermute | solution.py:658
  99.8 0.2 power.1
  100.0 17.5 %all_to_all.9 = f32[128,1,128]{2,1,0:T(1,128)S(1)} all-to-all(f32[128,1,128]{2,1,0:T(1,128)S(1)} %bitcast.10), channel_id=1, replica_groups=mesh['lap'=4,'pair'=16,'core'=2] {'lap','pair','core'}, dimensions={0} | all-to-all | bytes 131072 | tf_op jit(solution)/shard_map/all_to_all | solution.py:682
  117.5 0.7 model.1
  (22 shorter events, 0.3 us)
Async XLA Ops:
  1.7 10.0 %collective-permute-start = (f32[1112,128]{1,0:T(8,128)S(1)}, f32[1112,128]{1,0:T(8,128)S(1)}, u32[]{:S(2)}, u32[]{:S(2)}) collective-permute-start(f32[1112,128]{1,0:T(8,128)S(1)} %get-tuple-element.62.mine), channel_id=1, source_target_pairs={{0,1},{1,0},{2,3},{3,2},{4,5},{5,4},{6,7},{7,6},{8,9},{9,8},{10,11... | collective-permute-start | bytes 1708040 | tf_op jit(solution)/shard_map/ppermute | solution.py:519
  3.2 16.8 %collective-permute-start.2 = (f32[1112,128]{1,0:T(8,128)S(1)}, f32[1112,128]{1,0:T(8,128)S(1)}, u32[]{:S(2)}, u32[]{:S(2)}) collective-permute-start(f32[1112,128]{1,0:T(8,128)S(1)} %get-tuple-element.62.mine), channel_id=1, source_target_pairs={{2,0},{4,2},{6,4},{8,6},{10,8},{12,10},{14,12},{16,14},{18,16},{20... | collective-permute-start | bytes 1708040 | tf_op jit(solution)/shard_map/ppermute | solution.py:515
  4.5 16.5 %collective-permute-start.1 = (f32[1112,128]{1,0:T(8,128)S(1)}, f32[1112,128]{1,0:T(8,128)S(1)}, u32[]{:S(2)}, u32[]{:S(2)}) collective-permute-start(f32[1112,128]{1,0:T(8,128)S(1)} %get-tuple-element.62.mine), channel_id=1, source_target_pairs={{0,2},{2,4},{4,6},{6,8},{8,10},{10,12},{12,14},{14,16},{16,18},{18... | collective-permute-start | bytes 1708040 | tf_op jit(solution)/shard_map/ppermute | solution.py:515
  11.8 5.3 %copy-start = (f32[2,512,128]{2,1,0:T(8,128)S(1)}, f32[2,512,128]{2,1,0:T(8,128)}, u32[]{:S(2)}) copy-start(f32[2,512,128]{2,1,0:T(8,128)} %slow) | copy-start | bytes 1572868
  11.8 5.3 %copy-start.1 = (f32[4]{0:T(128)S(1)}, f32[4]{0:T(128)}, u32[]{:S(2)}) copy-start(f32[4]{0:T(128)} %damp.9) | copy-start | bytes 52
  15.8 9.7 %collective-permute-start.3 = (f32[88,128]{1,0:T(8,128)S(1)}, f32[88,128]{1,0:T(8,128)S(1)}, u32[]{:S(2)}, u32[]{:S(2)}) collective-permute-start(f32[88,128]{1,0:T(8,128)S(1)} %get-tuple-element.67), channel_id=1, source_target_pairs={{4,0},{6,2},{8,4},{10,6},{12,8},{14,10},{16,12},{18,14},{20,16},{2... | collective-permute-start | bytes 135176 | tf_op jit(solution)/shard_map/ppermute | solution.py:515
  25.6 5.2 %collective-permute-start.4 = (f32[2224,128]{1,0:T(8,128)S(1)}, f32[2224,128]{1,0:T(8,128)S(1)}, u32[]{:S(2)}, u32[]{:S(2)}) collective-permute-start(f32[2224,128]{1,0:T(8,128)S(1)} %pad_maximum_fusion), channel_id=1, source_target_pairs={{0,1},{1,0},{2,3},{3,2},{4,5},{5,4},{6,7},{7,6},{8,9},{9,8},{10,11... | collective-permute-start | bytes 3416072 | tf_op jit(solution)/shard_map/ppermute | solution.py:519
  43.5 4.5 %collective-permute-start.7 = (f32[8,128]{1,0:T(8,128)S(1)}, f32[8,128]{1,0:T(8,128)S(1)}, u32[]{:S(2)}, u32[]{:S(2)}) collective-permute-start(f32[8,128]{1,0:T(8,128)S(1)} %get-tuple-element.82), channel_id=1, source_target_pairs={{0,6},{2,4},{4,2},{6,0},{8,14},{10,12},{12,10},{14,8},{16,22},{18,... | collective-permute-start | bytes 12296 | tf_op jit(solution)/shard_map/ppermute | solution.py:524
  47.0 4.0 %collective-permute-start.6 = (f32[8,128]{1,0:T(8,128)S(1)}, f32[8,128]{1,0:T(8,128)S(1)}, u32[]{:S(2)}, u32[]{:S(2)}) collective-permute-start(f32[8,128]{1,0:T(8,128)S(1)} %get-tuple-element.82), channel_id=1, source_target_pairs={{0,4},{2,6},{4,0},{6,2},{8,12},{10,14},{12,8},{14,10},{16,20},{18,... | collective-permute-start | bytes 12296 | tf_op jit(solution)/shard_map/ppermute | solution.py:524
  47.0 4.0 %collective-permute-start.5 = (f32[8,128]{1,0:T(8,128)S(1)}, f32[8,128]{1,0:T(8,128)S(1)}, u32[]{:S(2)}, u32[]{:S(2)}) collective-permute-start(f32[8,128]{1,0:T(8,128)S(1)} %get-tuple-element.82), channel_id=1, source_target_pairs={{0,2},{2,0},{4,6},{6,4},{8,10},{10,8},{12,14},{14,12},{16,18},{18,... | collective-permute-start | bytes 12296 | tf_op jit(solution)/shard_map/ppermute | solution.py:524
  50.9 5.7 %collective-permute-start.10 = (f32[8,128]{1,0:T(8,128)S(1)}, f32[8,128]{1,0:T(8,128)S(1)}, u32[]{:S(2)}, u32[]{:S(2)}) collective-permute-start(f32[8,128]{1,0:T(8,128)S(1)} %add_add_fusion.1.t0), channel_id=1, source_target_pairs={{0,24},{2,26},{4,28},{6,30},{8,16},{10,18},{12,20},{14,22},{16,8},... | collective-permute-start | bytes 12296 | tf_op jit(solution)/shard_map/ppermute | solution.py:524
  53.4 4.0 %collective-permute-start.9 = (f32[8,128]{1,0:T(8,128)S(1)}, f32[8,128]{1,0:T(8,128)S(1)}, u32[]{:S(2)}, u32[]{:S(2)}) collective-permute-start(f32[8,128]{1,0:T(8,128)S(1)} %add_add_fusion.1.t0), channel_id=1, source_target_pairs={{0,16},{2,18},{4,20},{6,22},{8,24},{10,26},{12,28},{14,30},{16,0},... | collective-permute-start | bytes 12296 | tf_op jit(solution)/shard_map/ppermute | solution.py:524
  54.1 3.2 %collective-permute-start.8 = (f32[8,128]{1,0:T(8,128)S(1)}, f32[8,128]{1,0:T(8,128)S(1)}, u32[]{:S(2)}, u32[]{:S(2)}) collective-permute-start(f32[8,128]{1,0:T(8,128)S(1)} %add_add_fusion.1.t0), channel_id=1, source_target_pairs={{0,8},{2,10},{4,12},{6,14},{8,0},{10,2},{12,4},{14,6},{16,24},{18,... | collective-permute-start | bytes 12296 | tf_op jit(solution)/shard_map/ppermute | solution.py:524
  66.2 3.7 %collective-permute-start.13 = (f32[8,128]{1,0:T(8,128)S(1)}, f32[8,128]{1,0:T(8,128)S(1)}, u32[]{:S(2)}, u32[]{:S(2)}) collective-permute-start(f32[8,128]{1,0:T(8,128)S(1)} %get-tuple-element.93), channel_id=1, source_target_pairs={{0,6},{2,4},{4,2},{6,0},{8,14},{10,12},{12,10},{14,8},{16,22},{18,... | collective-permute-start | bytes 12296 | tf_op jit(solution)/shard_map/ppermute | solution.py:524
  68.4 4.0 %collective-permute-start.12 = (f32[8,128]{1,0:T(8,128)S(1)}, f32[8,128]{1,0:T(8,128)S(1)}, u32[]{:S(2)}, u32[]{:S(2)}) collective-permute-start(f32[8,128]{1,0:T(8,128)S(1)} %get-tuple-element.93), channel_id=1, source_target_pairs={{0,4},{2,6},{4,0},{6,2},{8,12},{10,14},{12,8},{14,10},{16,20},{18,... | collective-permute-start | bytes 12296 | tf_op jit(solution)/shard_map/ppermute | solution.py:524
  69.2 3.2 %collective-permute-start.11 = (f32[8,128]{1,0:T(8,128)S(1)}, f32[8,128]{1,0:T(8,128)S(1)}, u32[]{:S(2)}, u32[]{:S(2)}) collective-permute-start(f32[8,128]{1,0:T(8,128)S(1)} %get-tuple-element.93), channel_id=1, source_target_pairs={{0,2},{2,0},{4,6},{6,4},{8,10},{10,8},{12,14},{14,12},{16,18},{18,... | collective-permute-start | bytes 12296 | tf_op jit(solution)/shard_map/ppermute | solution.py:524
  72.3 3.9 %collective-permute-start.16 = (f32[8,128]{1,0:T(8,128)S(1)}, f32[8,128]{1,0:T(8,128)S(1)}, u32[]{:S(2)}, u32[]{:S(2)}) collective-permute-start(f32[8,128]{1,0:T(8,128)S(1)} %add_add_fusion.t0), channel_id=1, source_target_pairs={{0,24},{2,26},{4,28},{6,30},{8,16},{10,18},{12,20},{14,22},{16,8},... | collective-permute-start | bytes 12296 | tf_op jit(solution)/shard_map/ppermute | solution.py:524
  74.2 4.0 %collective-permute-start.15 = (f32[8,128]{1,0:T(8,128)S(1)}, f32[8,128]{1,0:T(8,128)S(1)}, u32[]{:S(2)}, u32[]{:S(2)}) collective-permute-start(f32[8,128]{1,0:T(8,128)S(1)} %add_add_fusion.t0), channel_id=1, source_target_pairs={{0,16},{2,18},{4,20},{6,22},{8,24},{10,26},{12,28},{14,30},{16,0},... | collective-permute-start | bytes 12296 | tf_op jit(solution)/shard_map/ppermute | solution.py:524
  74.2 3.9 %collective-permute-start.14 = (f32[8,128]{1,0:T(8,128)S(1)}, f32[8,128]{1,0:T(8,128)S(1)}, u32[]{:S(2)}, u32[]{:S(2)}) collective-permute-start(f32[8,128]{1,0:T(8,128)S(1)} %add_add_fusion.t0), channel_id=1, source_target_pairs={{0,8},{2,10},{4,12},{6,14},{8,0},{10,2},{12,4},{14,6},{16,24},{18,... | collective-permute-start | bytes 12296 | tf_op jit(solution)/shard_map/ppermute | solution.py:524
  79.4 12.0 %copy-start.2 = (f32[3,2,128,128]{3,2,1,0:T(8,128)S(1)}, f32[3,2,128,128]{3,2,1,0:T(8,128)}, u32[]{:S(2)}) copy-start(f32[3,2,128,128]{3,2,1,0:T(8,128)} %dual) | copy-start | bytes 1179652
  79.4 6.8 %collective-permute-start.17 = (f32[4,2,128,128]{3,2,1,0:T(8,128)S(1)}, f32[4,2,128,128]{3,2,1,0:T(8,128)S(1)}, u32[]{:S(2)}, u32[]{:S(2)}) collective-permute-start(f32[4,2,128,128]{3,2,1,0:T(8,128)S(1)} %gradient.2), channel_id=1, source_target_pairs={{0,1},{1,0},{2,3},{3,2},{4,5},{5,4},{6,7},{7,6},{8,9},{9,8},{10,11... | collective-permute-start | bytes 1572872 | tf_op jit(solution)/shard_map/ppermute | solution.py:519
  87.5 10.7 %collective-permute-start.18 = (f32[2,128,128]{2,1,0:T(8,128)S(1)}, f32[2,128,128]{2,1,0:T(8,128)S(1)}, u32[]{:S(2)}, u32[]{:S(2)}) collective-permute-start(f32[2,128,128]{2,1,0:T(8,128)S(1)} %get-tuple-element.108), channel_id=1, source_target_pairs={{0,32},{32,0},{64,96},{96,64},{1,33},{33,1},{65,97},{97,65},{2,34}... | collective-permute-start | bytes 393224 | tf_op jit(solution)/shard_map/ppermute | solution.py:658
  88.8 9.4 %collective-permute-start.19 = (f32[2,128,128]{2,1,0:T(8,128)S(1)}, f32[2,128,128]{2,1,0:T(8,128)S(1)}, u32[]{:S(2)}, u32[]{:S(2)}) collective-permute-start(f32[2,128,128]{2,1,0:T(8,128)S(1)} %get-tuple-element.109), channel_id=1, source_target_pairs={{0,64},{32,96},{64,0},{96,32},{1,65},{33,97},{65,1},{97,33},{2,66}... | collective-permute-start | bytes 393224 | tf_op jit(solution)/shard_map/ppermute | solution.py:658
  91.2 8.6 %collective-permute-start.20 = (f32[2,128,128]{2,1,0:T(8,128)S(1)}, f32[2,128,128]{2,1,0:T(8,128)S(1)}, u32[]{:S(2)}, u32[]{:S(2)}) collective-permute-start(f32[2,128,128]{2,1,0:T(8,128)S(1)} %get-tuple-element.110), channel_id=1, source_target_pairs={{0,96},{32,64},{64,32},{96,0},{1,97},{33,65},{65,33},{97,1},{2,98}... | collective-permute-start | bytes 393224 | tf_op jit(solution)/shard_map/ppermute | solution.py:658
  92.4 5.8 %collective-permute-start.21 = (f32[1,128,128]{2,1,0:T(8,128)S(1)}, f32[1,128,128]{2,1,0:T(8,128)S(1)}, u32[]{:S(2)}, u32[]{:S(2)}) collective-permute-start(f32[1,128,128]{2,1,0:T(8,128)S(1)} %get-tuple-element.111), channel_id=1, source_target_pairs={{0,1},{1,2},{2,3},{3,4},{4,5},{5,6},{6,7},{7,8},{8,9},{9,10},{10,1... | collective-permute-start | bytes 196616 | tf_op jit(solution)/shard_map/ppermute | solution.py:515
  95.5 2.7 %collective-permute-start.22 = (f32[2,8,128]{2,1,0:T(8,128)S(1)}, f32[2,8,128]{2,1,0:T(8,128)S(1)}, u32[]{:S(2)}, u32[]{:S(2)}) collective-permute-start(f32[2,8,128]{2,1,0:T(8,128)S(1)} %get-tuple-element.112), channel_id=1, source_target_pairs={{0,32},{32,64},{64,96},{1,33},{33,65},{65,97},{2,34},{34,66},{66,9... | collective-permute-start | bytes 24584 | tf_op jit(solution)/shard_map/ppermute | solution.py:515

commit v2 on v1

--- a/solution.py
+++ b/solution.py
@@ -436,13 +436,17 @@
     if not other:
         lap = lax.axis_index("lap")
         for d in range(4):
-            rest[1 + d][...] = bands[lap ^ d]
-
-
-def power_kernel(g0, g1, g2, g3, own, msg):
-    g = (g0[...] + g1[...]) + (g2[...] + g3[...])
+            rest[2 + d][:, 0:128, :] = bands[lap ^ d]
+            rest[2 + d][:, 128:136, :] = rest[1][...]
+
+
+def power_kernel(g0, g1, g2, g3, own, msg, prior_y):
+    lap = lax.axis_index("lap")
+    g = (g0[:, 0:128] + g1[:, 0:128]) + (g2[:, 0:128] + g3[:, 0:128])
     own[...] = g
     msg[...] = jnp.full((128, 128), jnp.sum(g * g), jnp.float32)
+    before = jnp.where(lap == 2, g3[:, 128:136], g1[:, 128:136])
+    prior_y[...] = jnp.where(lap == 0, 0.0, before)
 
 
 def variation_kernel(slow, own_t, near_t, dual, dual_next, base, send_x, send_y):
@@ -638,11 +642,10 @@
     terms = pair_sum(msg)
 
     def gradient(other, *more):
-        bands = (4, 2, 128, 128)
-        scratch = [] if other else [pltpu.VMEM(bands, jnp.float32)]
+        scratch = [] if other else [pltpu.VMEM((4, 2, 128, 128), jnp.float32)]
         return pl.pallas_call(
             functools.partial(gradient_kernel, other),
-            out_shape=struct(*bands) if other else (struct(*bands[1:]),) * 4,
+            out_shape=struct(4, 2, 128, 128) if other else (struct(2, 136, 128),) * 4,
             in_specs=[SMEM] + [VMEM] * (8 + len(more)),
             out_specs=VMEM if other else (VMEM,) * 4,
             scratch_shapes=scratch + [pltpu.VMEM((ROWS, 128), jnp.float32)],
@@ -650,13 +653,10 @@
             name="gradient",
         )(damping, *terms, wave, u0, u1, u2, *more)
 
-    bands = gradient(False, swapped(gradient(True)))
-    slowness, dual, own_t, near_t, bands = lax.optimization_barrier(
-        (slowness, dual, own_t, near_t, bands)
+    given = gradient(True)
+    slowness, dual, own_t, near_t, given = lax.optimization_barrier(
+        (slowness, dual, own_t, near_t, given)
     )
-    arrived = [bands[0]] + [
-        lax.ppermute(bands[d], "lap", [(i, i ^ d) for i in range(4)]) for d in (1, 2, 3)
-    ]
     dual_next, base, send_x, send_y = pl.pallas_call(
         variation_kernel,
         out_shape=(
@@ -668,14 +668,18 @@
         cost_estimate=cost(1),
         name="variation",
     )(slowness, own_t, near_t, dual)
+    bands = gradient(False, swapped(given), send_y)
+    send_x, bands = lax.optimization_barrier((send_x, bands))
+    arrived = [bands[0]] + [
+        lax.ppermute(bands[d], "lap", [(i, i ^ d) for i in range(4)]) for d in (1, 2, 3)
+    ]
     prior_x = moved(send_x, ("pair", "core"), 1)
-    prior_y = moved(send_y, "lap", 1)
-    arrived, prior_x, prior_y = lax.optimization_barrier((arrived, prior_x, prior_y))
-    own_grad, power = pl.pallas_call(
+    arrived, prior_x = lax.optimization_barrier((arrived, prior_x))
+    own_grad, power, prior_y = pl.pallas_call(
         power_kernel,
-        out_shape=(struct(2, 128, 128), struct(128, 128)),
+        out_shape=(struct(2, 128, 128), struct(128, 128), struct(2, 8, 128)),
         in_specs=[VMEM] * 4,
-        out_specs=(VMEM, VMEM),
+        out_specs=(VMEM,) * 3,
         compiler_params=params(8),
         name="power",
     )(*arrived)

time: 118 us -> 116 us (0.983)
  blocking collectives: 17.5 us -> 14.5 us
  waiting for transfers between devices: 19.2 us -> 21.4 us
  starting transfers between devices: 38.3 us -> 36.5 us
    all_to_all x1, blocking collectives: 17.5 us -> 14.5 us  [on_device(): power = lax.all_to_all(power, ('lap', 'pair', 'core'), 0, 0, tiled=True)]
    ppermute x3, waiting for transfers between devices: 1.66 us -> 4.31 us  [on_device(): lax.ppermute(bands[d], 'lap', [(i, i ^ d) for i in range(4)])]
    ppermute x5 -> x4, starting transfers between devices: 11.8 us -> 9.95 us  [moved(): lax.ppermute(x, axis, [(i, i + by) for i in range(peers) if 0 <= i + by <...]
    ppermute x5 -> x4, waiting for transfers between devices: 6.76 us -> 7.29 us  [moved(): lax.ppermute(x, axis, [(i, i + by) for i in range(peers) if 0 <= i + by <...]
  transfers between devices with their start and end apart: 23 -> 22, of which waited for: 13 -> 14; matrix products, arithmetic and copies ran while one was open for 0% -> 0% of each run, Pallas kernels for 14% -> 14%
where the time goes in v2:
time: 116 us
  Pallas kernels  42.2 us (36%)
  starting transfers between devices  36.5 us (31%)
  waiting for transfers between devices  21.4 us (18%)
  blocking collectives  14.5 us (12%)
    pallas_call x5, Pallas kernels, scatter(): pl.pallas_call(kernel, out_shape=tuple((struct(*shape) for shape in shape...  15.5 us
    all_to_all x1, blocking collectives, on_device(): power = lax.all_to_all(power, ('lap', 'pair', 'core'), 0, 0, tiled=True)  14.5 us
    ppermute x12, starting transfers between devices, others(): lax.ppermute(x, 'pair', [(i, i ^ d) for i in range(16)])  14.2 us
    pallas_call x1, Pallas kernels, on_device(): pl.pallas_call(forward_kernel, out_shape=(struct(PLANES, ROWS, 128), stru...  10.1 us
    ppermute x4, starting transfers between devices, moved(): lax.ppermute(x, axis, [(i, i + by) for i in range(peers) if 0 <= i + by <...  9.95 us
    ppermute x12, waiting for transfers between devices, others(): lax.ppermute(x, 'pair', [(i, i ^ d) for i in range(16)])  9.21 us
    pallas_call x1, Pallas kernels, on_device(): pl.pallas_call(adjoint_kernel, out_shape=(struct(4, ROWS, 128), struct(13...  8.67 us
    ppermute x3, starting transfers between devices, swapped(): return lax.ppermute(x, 'core', [(0, 1), (1, 0)])  8.41 us
  transfers between devices with their start and end apart: 22, of which 14 were waited for; matrix products, arithmetic and copies ran while one was open for 0% of the time, Pallas kernels for 14%

profile of v2, /device:TPU:1, one launch (start us, length us, event | category | flops | bytes accessed | tf_op | source)
XLA Modules:
  0.0 115.6 jit_solution(16747082079579119082)
XLA Ops:
  0.6 1.1 pack.1
  1.7 1.5 %collective-permute-start = (f32[1112,128]{1,0:T(8,128)S(1)}, f32[1112,128]{1,0:T(8,128)S(1)}, u32[]{:S(2)}, u32[]{:S(2)}) collective-permute-start(f32[1112,128]{1,0:T(8,128)S(1)} %get-tuple-element.64.mine), channel_id=1, source_target_pairs={{0,1},{1,0},{2,3},{3,2},{4,5},{5,4},{6,7},{7,6},{8,9},{9,8},{10,11... | collective-permute-start | bytes 1708040 | tf_op jit(solution)/shard_map/ppermute | solution.py:523
  3.2 1.3 %collective-permute-start.2 = (f32[1112,128]{1,0:T(8,128)S(1)}, f32[1112,128]{1,0:T(8,128)S(1)}, u32[]{:S(2)}, u32[]{:S(2)}) collective-permute-start(f32[1112,128]{1,0:T(8,128)S(1)} %get-tuple-element.64.mine), channel_id=1, source_target_pairs={{2,0},{4,2},{6,4},{8,6},{10,8},{12,10},{14,12},{16,14},{18,16},{20... | collective-permute-start | bytes 1708040 | tf_op jit(solution)/shard_map/ppermute | solution.py:519
  4.5 4.3 %collective-permute-start.1 = (f32[1112,128]{1,0:T(8,128)S(1)}, f32[1112,128]{1,0:T(8,128)S(1)}, u32[]{:S(2)}, u32[]{:S(2)}) collective-permute-start(f32[1112,128]{1,0:T(8,128)S(1)} %get-tuple-element.64.mine), channel_id=1, source_target_pairs={{0,2},{2,4},{4,6},{6,8},{8,10},{10,12},{12,14},{14,16},{16,18},{18... | collective-permute-start | bytes 1708040 | tf_op jit(solution)/shard_map/ppermute | solution.py:519
  8.8 2.9 %scatter_own.1 = (f32[4,1024,128]{2,1,0:T(8,128)S(1)}, f32[4,1024,128]{2,1,0:T(8,128)S(1)}, f32[4,1024,128]{2,1,0:T(8,128)S(1)}) custom-call(f32[88,128]{1,0:T(8,128)S(1)} %get-tuple-element.65.lists), custom_call_target="tpu_custom_call" | custom-call | flops 5000000000 | bytes 1000000 | tf_op jit(solution)/shard_map/scatter_own/pallas_call | solution.py:537
  11.8 4.0 %scatter_other.1 = (f32[4,1024,128]{2,1,0:T(8,128)S(1)}, f32[4,1024,128]{2,1,0:T(8,128)S(1)}, f32[4,1024,128]{2,1,0:T(8,128)S(1)}, f32[88,128]{1,0:T(8,128)S(1)}) custom-call(f32[1112,128]{1,0:T(8,128)S(1)} %get-tuple-element.64.mine, f32[1112,128]{1,0:T(8,128)S(1)} %collective-permute-done.other.own_t, ...), custom_call_target="tpu_custom_call", output_to_operand_aliasing={{0}: (2, {}), {1}: (3, {}), {2}: (4, {})} | custom-call | flops 5000000000 | bytes 1000000 | tf_op jit(solution)/shard_map/scatter_other/pallas_call | solution.py:537
  15.8 1.3 %collective-permute-start.3 = (f32[88,128]{1,0:T(8,128)S(1)}, f32[88,128]{1,0:T(8,128)S(1)}, u32[]{:S(2)}, u32[]{:S(2)}) collective-permute-start(f32[88,128]{1,0:T(8,128)S(1)} %get-tuple-element.69), channel_id=1, source_target_pairs={{4,0},{6,2},{8,4},{10,6},{12,8},{14,10},{16,12},{18,14},{20,16},{2... | collective-permute-start | bytes 135176 | tf_op jit(solution)/shard_map/ppermute | solution.py:519
  17.1 2.4 %forward_own.1 = (f32[13,1024,128]{2,1,0:T(8,128)S(1)}, f32[13,1040,128]{2,1,0:T(8,128)S(1)}, f32[11,1040,128]{2,1,0:T(8,128)S(1)}, f32[24,128]{1,0:T(8,128)S(1)}) custom-call(f32[4]{0:T(128)S(1)} %copy-done.1, f32[1024,128]{1,0:T(8,128)S(1)} %bitcast.8, f32[1112,128]{1,0:T(8,128)S(1)} %collective-permute-done.other.own_t, ...), custom_call_target="tpu_custom_call" | custom-call | flops 4000000000 | bytes 1000000 | tf_op jit(solution)/shard_map/forward_own/pallas_call | solution.py:585
  19.6 0.5 collective-permute-done.2.high.high_m
  20.1 1.0 collective-permute-done.1.low.low_m
  21.0 4.5 %collective-permute-done.3.far = f32[88,128]{1,0:T(8,128)S(1)} collective-permute-done((f32[88,128]{1,0:T(8,128)S(1)}, f32[88,128]{1,0:T(8,128)S(1)}, u32[]{:S(2)}, u32[]{:S(2)}) %collective-permute-start.3) | collective-permute-done | bytes 45088 | tf_op jit(solution)/shard_map/ppermute | solution.py:519
  25.6 1.7 %collective-permute-start.4 = (f32[2224,128]{1,0:T(8,128)S(1)}, f32[2224,128]{1,0:T(8,128)S(1)}, u32[]{:S(2)}, u32[]{:S(2)}) collective-permute-start(f32[2224,128]{1,0:T(8,128)S(1)} %pad_maximum_fusion), channel_id=1, source_target_pairs={{0,1},{1,0},{2,3},{3,2},{4,5},{5,4},{6,7},{7,6},{8,9},{9,8},{10,11... | collective-permute-start | bytes 3416072 | tf_op jit(solution)/shard_map/ppermute | solution.py:523
  27.3 3.5 %scatter_mine.1 = (f32[9,1024,128]{2,1,0:T(8,128)S(1)}, f32[5,1024,128]{2,1,0:T(8,128)S(1)}, f32[5,1024,128]{2,1,0:T(8,128)S(1)}) custom-call(f32[1112,128]{1,0:T(8,128)S(1)} %collective-permute-done.1.low.low_m, f32[1112,128]{1,0:T(8,128)S(1)} %collective-permute-done.2.high.high_m), custom_call_target="tpu_custom_call" | custom-call | flops 6000000000 | bytes 1000000 | tf_op jit(solution)/shard_map/scatter_mine/pallas_call | solution.py:537
  30.9 2.7 %scatter_theirs.1.b_near = f32[9,1024,128]{2,1,0:T(8,128)S(1)} custom-call(f32[4]{0:T(128)S(1)} %copy-done.1, f32[88,128]{1,0:T(8,128)S(1)} %collective-permute-done.3.far, f32[2224,128]{1,0:T(8,128)S(1)} %collective-permute-done.4.near.near_t, f32[9,1024,128]{2,1,0:T(8,128)S(1)} %get-tuple-element.77.b_in), custom_call_target="tpu_custom_call", output_to_operand_aliasing={{}: (3, {})} | custom-call | flops 5000000000 | bytes 1000000 | tf_op jit(solution)/shard_map/scatter_theirs/pallas_call | solution.py:537
  33.5 10.1 %forward.1 = (f32[13,1024,128]{2,1,0:T(8,128)S(1)}, f32[13,1040,128]{2,1,0:T(8,128)S(1)}, f32[11,1040,128]{2,1,0:T(8,128)S(1)}, f32[9,1040,128]{2,1,0:T(8,128)S(1)}, f32[8,128]{1,0:T(8,128)S(1)}) custom-call(f32[4]{0:T(128)S(1)} %copy-done.1, ...), custom_call_target="tpu_custom_call", output_to_operand_aliasing={{0}: (6, {}), {1}: (7, {}), {2}: (8, {})} | custom-call | flops 20000000000 | bytes 1000000 | tf_op jit(solution)/shard_map/forward/pallas_call | solution.py:609
  43.6 3.5 %collective-permute-start.7 = (f32[8,128]{1,0:T(8,128)S(1)}, f32[8,128]{1,0:T(8,128)S(1)}, u32[]{:S(2)}, u32[]{:S(2)}) collective-permute-start(f32[8,128]{1,0:T(8,128)S(1)} %get-tuple-element.84), channel_id=1, source_target_pairs={{0,6},{2,4},{4,2},{6,0},{8,14},{10,12},{12,10},{14,8},{16,22},{18,... | collective-permute-start | bytes 12296 | tf_op jit(solution)/shard_map/ppermute | solution.py:528
  47.1 0.7 collective-permute-start.5
  47.8 0.3 collective-permute-done.7
  48.1 3.0 %collective-permute-done.6 = f32[8,128]{1,0:T(8,128)S(1)} collective-permute-done((f32[8,128]{1,0:T(8,128)S(1)}, f32[8,128]{1,0:T(8,128)S(1)}, u32[]{:S(2)}, u32[]{:S(2)}) %collective-permute-start.6) | collective-permute-done | bytes 4128 | tf_op jit(solution)/shard_map/ppermute | solution.py:528
  51.1 2.4 %collective-permute-start.10 = (f32[8,128]{1,0:T(8,128)S(1)}, f32[8,128]{1,0:T(8,128)S(1)}, u32[]{:S(2)}, u32[]{:S(2)}) collective-permute-start(f32[8,128]{1,0:T(8,128)S(1)} %add_add_fusion.1.t0), channel_id=1, source_target_pairs={{0,24},{2,26},{4,28},{6,30},{8,16},{10,18},{12,20},{14,22},{16,8},... | collective-permute-start | bytes 12296 | tf_op jit(solution)/shard_map/ppermute | solution.py:528
  53.5 0.8 collective-permute-start.9
  54.4 2.4 %scatter_late.1 = (f32[5,1024,128]{2,1,0:T(8,128)S(1)}, f32[5,1024,128]{2,1,0:T(8,128)S(1)}) custom-call(f32[1112,128]{1,0:T(8,128)S(1)} %collective-permute-done.2.high.high_m, f32[2224,128]{1,0:T(8,128)S(1)} %collective-permute-done.4.near.near_t, f32[5,1024,128]{2,1,0:T(8,128)S(1)} %get-tuple-element.91.ob_in, ...), custom_call_target="tpu_custom_call", output_to_operand_aliasing={{0}: (2, {}), {1}: (3, {})} | custom-call | flops 5000000000 | bytes 1000000 | tf_op jit(solution)/shard_map/scatter_late/pallas_call | solution.py:537
  56.8 0.6 collective-permute-done.9.t2
  57.5 8.7 %adjoint.1 = (f32[4,1024,128]{2,1,0:T(8,128)S(1)}, f32[13,1040,128]{2,1,0:T(8,128)S(1)}, f32[11,1040,128]{2,1,0:T(8,128)S(1)}, f32[9,1040,128]{2,1,0:T(8,128)S(1)}, f32[8,128]{1,0:T(8,128)S(1)}) custom-call(f32[8,128]{1,0:T(8,128)S(1)} %add_add_fusion.1.t0, ...), custom_call_target="tpu_custom_call", output_to_operand_aliasing={{1}: (5, {}), {2}: (6, {}), {3}: (7, {})} | custom-call | flops 14000000000 | bytes 1000000 | tf_op jit(solution)/shard_map/adjoint/pallas_call | solution.py:628
  66.1 2.2 %collective-permute-start.13 = (f32[8,128]{1,0:T(8,128)S(1)}, f32[8,128]{1,0:T(8,128)S(1)}, u32[]{:S(2)}, u32[]{:S(2)}) collective-permute-start(f32[8,128]{1,0:T(8,128)S(1)} %get-tuple-element.95), channel_id=1, source_target_pairs={{0,6},{2,4},{4,2},{6,0},{8,14},{10,12},{12,10},{14,8},{16,22},{18,... | collective-permute-start | bytes 12296 | tf_op jit(solution)/shard_map/ppermute | solution.py:528
  68.4 0.8 collective-permute-start.12
  69.1 0.3 collective-permute-start.11
  69.5 0.4 collective-permute-done.13
  69.9 2.4 %collective-permute-done.12 = f32[8,128]{1,0:T(8,128)S(1)} collective-permute-done((f32[8,128]{1,0:T(8,128)S(1)}, f32[8,128]{1,0:T(8,128)S(1)}, u32[]{:S(2)}, u32[]{:S(2)}) %collective-permute-start.12) | collective-permute-done | bytes 4128 | tf_op jit(solution)/shard_map/ppermute | solution.py:528
  72.3 1.8 %collective-permute-start.16 = (f32[8,128]{1,0:T(8,128)S(1)}, f32[8,128]{1,0:T(8,128)S(1)}, u32[]{:S(2)}, u32[]{:S(2)}) collective-permute-start(f32[8,128]{1,0:T(8,128)S(1)} %add_add_fusion.t0), channel_id=1, source_target_pairs={{0,24},{2,26},{4,28},{6,30},{8,16},{10,18},{12,20},{14,22},{16,8},... | collective-permute-start | bytes 12296 | tf_op jit(solution)/shard_map/ppermute | solution.py:528
  74.2 1.5 %collective-permute-start.14 = (f32[8,128]{1,0:T(8,128)S(1)}, f32[8,128]{1,0:T(8,128)S(1)}, u32[]{:S(2)}, u32[]{:S(2)}) collective-permute-start(f32[8,128]{1,0:T(8,128)S(1)} %add_add_fusion.t0), channel_id=1, source_target_pairs={{0,8},{2,10},{4,12},{6,14},{8,0},{10,2},{12,4},{14,6},{16,24},{18,... | collective-permute-start | bytes 12296 | tf_op jit(solution)/shard_map/ppermute | solution.py:528
  75.7 0.6 collective-permute-done.16.t3
  76.2 1.9 %collective-permute-done.15.t2 = f32[8,128]{1,0:T(8,128)S(1)} collective-permute-done((f32[8,128]{1,0:T(8,128)S(1)}, f32[8,128]{1,0:T(8,128)S(1)}, u32[]{:S(2)}, u32[]{:S(2)}) %collective-permute-start.15) | collective-permute-done | bytes 4128 | tf_op jit(solution)/shard_map/ppermute | solution.py:528
  78.1 1.3 %gradient.2 = f32[4,2,128,128]{3,2,1,0:T(8,128)S(1)} custom-call(f32[4]{0:T(128)S(1)} %copy-done.1, f32[8,128]{1,0:T(8,128)S(1)} %add_add_fusion.t0, f32[8,128]{1,0:T(8,128)S(1)} %collective-permute-done.14.t1, f32[8,128]{1,0:T(8,128)S(1)} %collective-permute-done.15.t2, f32[8,128]{1,0:T(8,128)S(1)} %collective-permute-done.16.t3, ...), custom_call_target="tpu_custom_call" | custom-call | tf_op jit(solution)/shard_map/gradient/pallas_call | solution.py:646
  79.4 5.2 %collective-permute-start.17 = (f32[4,2,128,128]{3,2,1,0:T(8,128)S(1)}, f32[4,2,128,128]{3,2,1,0:T(8,128)S(1)}, u32[]{:S(2)}, u32[]{:S(2)}) collective-permute-start(f32[4,2,128,128]{3,2,1,0:T(8,128)S(1)} %gradient.2), channel_id=1, source_target_pairs={{0,1},{1,0},{2,3},{3,2},{4,5},{5,4},{6,7},{7,6},{8,9},{9,8},{10,11... | collective-permute-start | bytes 1572872 | tf_op jit(solution)/shard_map/ppermute | solution.py:523
  84.6 0.9 variation.1
  85.5 0.6 collective-permute-done.17.rest_0_
  86.1 1.3 %gradient.3 = (f32[2,136,128]{2,1,0:T(8,128)S(1)}, f32[2,136,128]{2,1,0:T(8,128)S(1)}, f32[2,136,128]{2,1,0:T(8,128)S(1)}, f32[2,136,128]{2,1,0:T(8,128)S(1)}) custom-call(f32[4]{0:T(128)S(1)} %copy-done.1, f32[8,128]{1,0:T(8,128)S(1)} %add_add_fusion.t0, f32[8,128]{1,0:T(8,128)S(1)} %collective-permute-done.14.t1, f32[8,128]{1,0:T(8,128)S(1)} %collective-permute-done.15.t2, ...), custom_call_target="tpu_custom_call" | custom-call | tf_op jit(solution)/shard_map/gradient/pallas_call | solution.py:646
  87.5 1.3 %collective-permute-start.18 = (f32[2,136,128]{2,1,0:T(8,128)S(1)}, f32[2,136,128]{2,1,0:T(8,128)S(1)}, u32[]{:S(2)}, u32[]{:S(2)}) collective-permute-start(f32[2,136,128]{2,1,0:T(8,128)S(1)} %get-tuple-element.113), channel_id=1, source_target_pairs={{0,32},{32,0},{64,96},{96,64},{1,33},{33,1},{65,97},{97,65},{2,34}... | collective-permute-start | bytes 417800 | tf_op jit(solution)/shard_map/ppermute | solution.py:674
  88.7 2.5 %collective-permute-start.19 = (f32[2,136,128]{2,1,0:T(8,128)S(1)}, f32[2,136,128]{2,1,0:T(8,128)S(1)}, u32[]{:S(2)}, u32[]{:S(2)}) collective-permute-start(f32[2,136,128]{2,1,0:T(8,128)S(1)} %get-tuple-element.114), channel_id=1, source_target_pairs={{0,64},{32,96},{64,0},{96,32},{1,65},{33,97},{65,1},{97,33},{2,66}... | collective-permute-start | bytes 417800 | tf_op jit(solution)/shard_map/ppermute | solution.py:674
  91.2 0.2 collective-permute-start.20
  91.4 3.1 %collective-permute-start.21 = (f32[1,128,128]{2,1,0:T(8,128)S(1)}, f32[1,128,128]{2,1,0:T(8,128)S(1)}, u32[]{:S(2)}, u32[]{:S(2)}) collective-permute-start(f32[1,128,128]{2,1,0:T(8,128)S(1)} %get-tuple-element.116), channel_id=1, source_target_pairs={{0,1},{1,2},{2,3},{3,4},{4,5},{5,6},{6,7},{7,8},{8,9},{9,10},{10,1... | collective-permute-start | bytes 196616 | tf_op jit(solution)/shard_map/ppermute | solution.py:519
  94.5 1.3 %collective-permute-done.21.prior_x = f32[1,128,128]{2,1,0:T(8,128)S(1)} collective-permute-done((f32[1,128,128]{2,1,0:T(8,128)S(1)}, f32[1,128,128]{2,1,0:T(8,128)S(1)}, u32[]{:S(2)}, u32[]{:S(2)}) %collective-permute-start.21) | collective-permute-done | bytes 65568 | tf_op jit(solution)/shard_map/ppermute | solution.py:519
  95.8 1.8 %collective-permute-done.19.g2 = f32[2,136,128]{2,1,0:T(8,128)S(1)} collective-permute-done((f32[2,136,128]{2,1,0:T(8,128)S(1)}, f32[2,136,128]{2,1,0:T(8,128)S(1)}, u32[]{:S(2)}, u32[]{:S(2)}) %collective-permute-start.19) | collective-permute-done | bytes 139296 | tf_op jit(solution)/shard_map/ppermute | solution.py:674
  97.6 2.5 %collective-permute-done.20.g3 = f32[2,136,128]{2,1,0:T(8,128)S(1)} collective-permute-done((f32[2,136,128]{2,1,0:T(8,128)S(1)}, f32[2,136,128]{2,1,0:T(8,128)S(1)}, u32[]{:S(2)}, u32[]{:S(2)}) %collective-permute-start.20) | collective-permute-done | bytes 139296 | tf_op jit(solution)/shard_map/ppermute | solution.py:674
  100.1 0.2 power.1
  100.3 14.5 %all_to_all.9 = f32[128,1,128]{2,1,0:T(1,128)S(1)} all-to-all(f32[128,1,128]{2,1,0:T(1,128)S(1)} %bitcast.10), channel_id=1, replica_groups=mesh['lap'=4,'pair'=16,'core'=2] {'lap','pair','core'}, dimensions={0} | all-to-all | bytes 131072 | tf_op jit(solution)/shard_map/all_to_all | solution.py:686
  114.8 0.7 model.1
  (20 shorter events, 0.3 us)
Async XLA Ops:
  1.7 10.0 %collective-permute-start = (f32[1112,128]{1,0:T(8,128)S(1)}, f32[1112,128]{1,0:T(8,128)S(1)}, u32[]{:S(2)}, u32[]{:S(2)}) collective-permute-start(f32[1112,128]{1,0:T(8,128)S(1)} %get-tuple-element.64.mine), channel_id=1, source_target_pairs={{0,1},{1,0},{2,3},{3,2},{4,5},{5,4},{6,7},{7,6},{8,9},{9,8},{10,11... | collective-permute-start | bytes 1708040 | tf_op jit(solution)/shard_map/ppermute | solution.py:523
  3.2 16.8 %collective-permute-start.2 = (f32[1112,128]{1,0:T(8,128)S(1)}, f32[1112,128]{1,0:T(8,128)S(1)}, u32[]{:S(2)}, u32[]{:S(2)}) collective-permute-start(f32[1112,128]{1,0:T(8,128)S(1)} %get-tuple-element.64.mine), channel_id=1, source_target_pairs={{2,0},{4,2},{6,4},{8,6},{10,8},{12,10},{14,12},{16,14},{18,16},{20... | collective-permute-start | bytes 1708040 | tf_op jit(solution)/shard_map/ppermute | solution.py:519
  4.5 16.5 %collective-permute-start.1 = (f32[1112,128]{1,0:T(8,128)S(1)}, f32[1112,128]{1,0:T(8,128)S(1)}, u32[]{:S(2)}, u32[]{:S(2)}) collective-permute-start(f32[1112,128]{1,0:T(8,128)S(1)} %get-tuple-element.64.mine), channel_id=1, source_target_pairs={{0,2},{2,4},{4,6},{6,8},{8,10},{10,12},{12,14},{14,16},{16,18},{18... | collective-permute-start | bytes 1708040 | tf_op jit(solution)/shard_map/ppermute | solution.py:519
  11.8 5.3 %copy-start = (f32[2,512,128]{2,1,0:T(8,128)S(1)}, f32[2,512,128]{2,1,0:T(8,128)}, u32[]{:S(2)}) copy-start(f32[2,512,128]{2,1,0:T(8,128)} %slow) | copy-start | bytes 1572868
  11.8 5.3 %copy-start.1 = (f32[4]{0:T(128)S(1)}, f32[4]{0:T(128)}, u32[]{:S(2)}) copy-start(f32[4]{0:T(128)} %damp.9) | copy-start | bytes 52
  15.8 9.7 %collective-permute-start.3 = (f32[88,128]{1,0:T(8,128)S(1)}, f32[88,128]{1,0:T(8,128)S(1)}, u32[]{:S(2)}, u32[]{:S(2)}) collective-permute-start(f32[88,128]{1,0:T(8,128)S(1)} %get-tuple-element.69), channel_id=1, source_target_pairs={{4,0},{6,2},{8,4},{10,6},{12,8},{14,10},{16,12},{18,14},{20,16},{2... | collective-permute-start | bytes 135176 | tf_op jit(solution)/shard_map/ppermute | solution.py:519
  25.6 5.2 %collective-permute-start.4 = (f32[2224,128]{1,0:T(8,128)S(1)}, f32[2224,128]{1,0:T(8,128)S(1)}, u32[]{:S(2)}, u32[]{:S(2)}) collective-permute-start(f32[2224,128]{1,0:T(8,128)S(1)} %pad_maximum_fusion), channel_id=1, source_target_pairs={{0,1},{1,0},{2,3},{3,2},{4,5},{5,4},{6,7},{7,6},{8,9},{9,8},{10,11... | collective-permute-start | bytes 3416072 | tf_op jit(solution)/shard_map/ppermute | solution.py:523
  43.6 4.5 %collective-permute-start.7 = (f32[8,128]{1,0:T(8,128)S(1)}, f32[8,128]{1,0:T(8,128)S(1)}, u32[]{:S(2)}, u32[]{:S(2)}) collective-permute-start(f32[8,128]{1,0:T(8,128)S(1)} %get-tuple-element.84), channel_id=1, source_target_pairs={{0,6},{2,4},{4,2},{6,0},{8,14},{10,12},{12,10},{14,8},{16,22},{18,... | collective-permute-start | bytes 12296 | tf_op jit(solution)/shard_map/ppermute | solution.py:528
  47.1 4.0 %collective-permute-start.6 = (f32[8,128]{1,0:T(8,128)S(1)}, f32[8,128]{1,0:T(8,128)S(1)}, u32[]{:S(2)}, u32[]{:S(2)}) collective-permute-start(f32[8,128]{1,0:T(8,128)S(1)} %get-tuple-element.84), channel_id=1, source_target_pairs={{0,4},{2,6},{4,0},{6,2},{8,12},{10,14},{12,8},{14,10},{16,20},{18,... | collective-permute-start | bytes 12296 | tf_op jit(solution)/shard_map/ppermute | solution.py:528
  47.1 4.0 %collective-permute-start.5 = (f32[8,128]{1,0:T(8,128)S(1)}, f32[8,128]{1,0:T(8,128)S(1)}, u32[]{:S(2)}, u32[]{:S(2)}) collective-permute-start(f32[8,128]{1,0:T(8,128)S(1)} %get-tuple-element.84), channel_id=1, source_target_pairs={{0,2},{2,0},{4,6},{6,4},{8,10},{10,8},{12,14},{14,12},{16,18},{18,... | collective-permute-start | bytes 12296 | tf_op jit(solution)/shard_map/ppermute | solution.py:528
  51.1 5.7 %collective-permute-start.10 = (f32[8,128]{1,0:T(8,128)S(1)}, f32[8,128]{1,0:T(8,128)S(1)}, u32[]{:S(2)}, u32[]{:S(2)}) collective-permute-start(f32[8,128]{1,0:T(8,128)S(1)} %add_add_fusion.1.t0), channel_id=1, source_target_pairs={{0,24},{2,26},{4,28},{6,30},{8,16},{10,18},{12,20},{14,22},{16,8},... | collective-permute-start | bytes 12296 | tf_op jit(solution)/shard_map/ppermute | solution.py:528
  53.5 4.0 %collective-permute-start.9 = (f32[8,128]{1,0:T(8,128)S(1)}, f32[8,128]{1,0:T(8,128)S(1)}, u32[]{:S(2)}, u32[]{:S(2)}) collective-permute-start(f32[8,128]{1,0:T(8,128)S(1)} %add_add_fusion.1.t0), channel_id=1, source_target_pairs={{0,16},{2,18},{4,20},{6,22},{8,24},{10,26},{12,28},{14,30},{16,0},... | collective-permute-start | bytes 12296 | tf_op jit(solution)/shard_map/ppermute | solution.py:528
  54.2 3.2 %collective-permute-start.8 = (f32[8,128]{1,0:T(8,128)S(1)}, f32[8,128]{1,0:T(8,128)S(1)}, u32[]{:S(2)}, u32[]{:S(2)}) collective-permute-start(f32[8,128]{1,0:T(8,128)S(1)} %add_add_fusion.1.t0), channel_id=1, source_target_pairs={{0,8},{2,10},{4,12},{6,14},{8,0},{10,2},{12,4},{14,6},{16,24},{18,... | collective-permute-start | bytes 12296 | tf_op jit(solution)/shard_map/ppermute | solution.py:528
  66.1 3.7 %collective-permute-start.13 = (f32[8,128]{1,0:T(8,128)S(1)}, f32[8,128]{1,0:T(8,128)S(1)}, u32[]{:S(2)}, u32[]{:S(2)}) collective-permute-start(f32[8,128]{1,0:T(8,128)S(1)} %get-tuple-element.95), channel_id=1, source_target_pairs={{0,6},{2,4},{4,2},{6,0},{8,14},{10,12},{12,10},{14,8},{16,22},{18,... | collective-permute-start | bytes 12296 | tf_op jit(solution)/shard_map/ppermute | solution.py:528
  68.4 4.0 %collective-permute-start.12 = (f32[8,128]{1,0:T(8,128)S(1)}, f32[8,128]{1,0:T(8,128)S(1)}, u32[]{:S(2)}, u32[]{:S(2)}) collective-permute-start(f32[8,128]{1,0:T(8,128)S(1)} %get-tuple-element.95), channel_id=1, source_target_pairs={{0,4},{2,6},{4,0},{6,2},{8,12},{10,14},{12,8},{14,10},{16,20},{18,... | collective-permute-start | bytes 12296 | tf_op jit(solution)/shard_map/ppermute | solution.py:528
  69.1 3.2 %collective-permute-start.11 = (f32[8,128]{1,0:T(8,128)S(1)}, f32[8,128]{1,0:T(8,128)S(1)}, u32[]{:S(2)}, u32[]{:S(2)}) collective-permute-start(f32[8,128]{1,0:T(8,128)S(1)} %get-tuple-element.95), channel_id=1, source_target_pairs={{0,2},{2,0},{4,6},{6,4},{8,10},{10,8},{12,14},{14,12},{16,18},{18,... | collective-permute-start | bytes 12296 | tf_op jit(solution)/shard_map/ppermute | solution.py:528
  72.3 3.9 %collective-permute-start.16 = (f32[8,128]{1,0:T(8,128)S(1)}, f32[8,128]{1,0:T(8,128)S(1)}, u32[]{:S(2)}, u32[]{:S(2)}) collective-permute-start(f32[8,128]{1,0:T(8,128)S(1)} %add_add_fusion.t0), channel_id=1, source_target_pairs={{0,24},{2,26},{4,28},{6,30},{8,16},{10,18},{12,20},{14,22},{16,8},... | collective-permute-start | bytes 12296 | tf_op jit(solution)/shard_map/ppermute | solution.py:528
  74.1 4.0 %collective-permute-start.15 = (f32[8,128]{1,0:T(8,128)S(1)}, f32[8,128]{1,0:T(8,128)S(1)}, u32[]{:S(2)}, u32[]{:S(2)}) collective-permute-start(f32[8,128]{1,0:T(8,128)S(1)} %add_add_fusion.t0), channel_id=1, source_target_pairs={{0,16},{2,18},{4,20},{6,22},{8,24},{10,26},{12,28},{14,30},{16,0},... | collective-permute-start | bytes 12296 | tf_op jit(solution)/shard_map/ppermute | solution.py:528
  74.2 3.9 %collective-permute-start.14 = (f32[8,128]{1,0:T(8,128)S(1)}, f32[8,128]{1,0:T(8,128)S(1)}, u32[]{:S(2)}, u32[]{:S(2)}) collective-permute-start(f32[8,128]{1,0:T(8,128)S(1)} %add_add_fusion.t0), channel_id=1, source_target_pairs={{0,8},{2,10},{4,12},{6,14},{8,0},{10,2},{12,4},{14,6},{16,24},{18,... | collective-permute-start | bytes 12296 | tf_op jit(solution)/shard_map/ppermute | solution.py:528
  78.1 6.5 %copy-start.2 = (f32[3,2,128,128]{3,2,1,0:T(8,128)S(1)}, f32[3,2,128,128]{3,2,1,0:T(8,128)}, u32[]{:S(2)}) copy-start(f32[3,2,128,128]{3,2,1,0:T(8,128)} %dual) | copy-start | bytes 1179652
  79.4 6.8 %collective-permute-start.17 = (f32[4,2,128,128]{3,2,1,0:T(8,128)S(1)}, f32[4,2,128,128]{3,2,1,0:T(8,128)S(1)}, u32[]{:S(2)}, u32[]{:S(2)}) collective-permute-start(f32[4,2,128,128]{3,2,1,0:T(8,128)S(1)} %gradient.2), channel_id=1, source_target_pairs={{0,1},{1,0},{2,3},{3,2},{4,5},{5,4},{6,7},{7,6},{8,9},{9,8},{10,11... | collective-permute-start | bytes 1572872 | tf_op jit(solution)/shard_map/ppermute | solution.py:523
  87.5 8.3 %collective-permute-start.18 = (f32[2,136,128]{2,1,0:T(8,128)S(1)}, f32[2,136,128]{2,1,0:T(8,128)S(1)}, u32[]{:S(2)}, u32[]{:S(2)}) collective-permute-start(f32[2,136,128]{2,1,0:T(8,128)S(1)} %get-tuple-element.113), channel_id=1, source_target_pairs={{0,32},{32,0},{64,96},{96,64},{1,33},{33,1},{65,97},{97,65},{2,34}... | collective-permute-start | bytes 417800 | tf_op jit(solution)/shard_map/ppermute | solution.py:674
  88.7 8.9 %collective-permute-start.19 = (f32[2,136,128]{2,1,0:T(8,128)S(1)}, f32[2,136,128]{2,1,0:T(8,128)S(1)}, u32[]{:S(2)}, u32[]{:S(2)}) collective-permute-start(f32[2,136,128]{2,1,0:T(8,128)S(1)} %get-tuple-element.114), channel_id=1, source_target_pairs={{0,64},{32,96},{64,0},{96,32},{1,65},{33,97},{65,1},{97,33},{2,66}... | collective-permute-start | bytes 417800 | tf_op jit(solution)/shard_map/ppermute | solution.py:674
  91.2 8.9 %collective-permute-start.20 = (f32[2,136,128]{2,1,0:T(8,128)S(1)}, f32[2,136,128]{2,1,0:T(8,128)S(1)}, u32[]{:S(2)}, u32[]{:S(2)}) collective-permute-start(f32[2,136,128]{2,1,0:T(8,128)S(1)} %get-tuple-element.115), channel_id=1, source_target_pairs={{0,96},{32,64},{64,32},{96,0},{1,97},{33,65},{65,33},{97,1},{2,98}... | collective-permute-start | bytes 417800 | tf_op jit(solution)/shard_map/ppermute | solution.py:674
  91.4 4.4 %collective-permute-start.21 = (f32[1,128,128]{2,1,0:T(8,128)S(1)}, f32[1,128,128]{2,1,0:T(8,128)S(1)}, u32[]{:S(2)}, u32[]{:S(2)}) collective-permute-start(f32[1,128,128]{2,1,0:T(8,128)S(1)} %get-tuple-element.116), channel_id=1, source_target_pairs={{0,1},{1,2},{2,3},{3,4},{4,5},{5,6},{6,7},{7,8},{8,9},{9,10},{10,1... | collective-permute-start | bytes 196616 | tf_op jit(solution)/shard_map/ppermute | solution.py:519

commit v3 on v2

--- a/solution.py
+++ b/solution.py
@@ -11,9 +11,9 @@
 
 HALF = 2
 PLANES = 13
-KEPT = 9
-PAD = 8
-ROWS = 1024
+LINES = 512
+ROWS = HALF * LINES
+TURNED = 192
 LIST = 88
 SLAB = ROWS + LIST
 
@@ -29,34 +29,39 @@
     return pltpu.CompilerParams(vmem_limit_bytes=mib * 2**20)
 
 
+def line_of(row):
+    return (row & 63) * 8 + (row >> 6)
+
+
 def spread_points(index, parts, right_planes, write):
     points = index.shape[1]
     column = (index >> 16) * 128 + (index & 127)
-    row = (index >> 7) & 511
-    rows = ROWS
+    line = line_of((index >> 7) & 511)
+    lines = LINES
     if right_planes == 1:
-        rows = ROWS // 2
-        column = jnp.where(index >> 16 == 0, (row >> 8) * 128 + (index & 127), -1)
-        row = row & 255
-    row = row - lax.broadcasted_iota(jnp.int32, (8, points), 0) // HALF
+        lines = LINES // 2
+        column = jnp.where(index >> 16 == 0, (line >> 8) * 128 + (index & 127), -1)
+        line = line & 255
     lanes = lax.broadcasted_iota(jnp.int32, (256, points), 0)
     right = jnp.where(lanes == column, 1.0, 0.0).astype(jnp.bfloat16)
-    tile = lax.broadcasted_iota(jnp.int32, (rows // 8, 8, points), 0)
-    mask = row[None] == (8 // HALF) * tile
+    mask = lax.broadcasted_iota(jnp.int32, (lines, points), 0) == line
     for which, part in enumerate(parts):
         total = None
-        for piece in part:
-            left = jnp.where(mask, piece[None], 0.0).reshape(rows, points).astype(jnp.bfloat16)
+        for piece in zip(*part):
+            left = [jnp.where(mask, value, 0.0).astype(jnp.bfloat16) for value in piece]
             got = lax.dot_general(
-                left, right, (((1,), (1,)), ((), ())), preferred_element_type=jnp.float32
+                jnp.concatenate(left), right, (((1,), (1,)), ((), ())),
+                preferred_element_type=jnp.float32,
             )
             total = got if total is None else total + got
-        lower, upper = total[:, 0:128], total[:, 128:256]
-        if right_planes == 1:
-            write(which, 0, jnp.concatenate([lower, upper]))
-        else:
-            write(which, 0, lower)
-            write(which, 1, upper)
+        for c in range(len(part)):
+            rows = total[lines * c : lines * c + lines]
+            lower, upper = rows[:, 0:128], rows[:, 128:256]
+            if right_planes == 1:
+                write(which, 0, c, jnp.concatenate([lower, upper]))
+            else:
+                write(which, 0, c, lower)
+                write(which, 1, c, upper)
 
 
 def pieces_of(value, count):
@@ -73,21 +78,14 @@
     return lambda i: jnp.where(core == 0, list_row(*zero, i), list_row(*one, i))
 
 
-def by_parity(even, odd, points):
-    parity = lax.broadcasted_iota(jnp.int32, (8, points), 0) % HALF
-    return jnp.where(parity == 0, even, odd)
-
-
 def points_of(core, row, first):
-    even = jnp.where(core == 0, row(first), row(first + 2))
-    odd = jnp.where(core == 0, row(first + 1), row(first + 3))
-    return by_parity(even, odd, even.shape[1])
+    return [jnp.where(core == 0, row(first + c), row(first + HALF + c)) for c in range(HALF)]
 
 
 def writer(stores):
-    def write(which, p, value):
+    def write(which, p, c, value):
         ref, first = stores[which]
-        ref[first + p] = value
+        ref[first + p, LINES * c : LINES * c + LINES, :] = value
 
     return write
 
@@ -95,14 +93,14 @@
 def scatter_src(core, row, count, store, first, divisor=None, planes=2):
     amp = points_of(core, row, 2)
     if divisor is not None:
-        amp = amp / divisor
+        amp = [a / d for a, d in zip(amp, divisor)]
     index = row(0).astype(jnp.int32)
-    spread_points(index, [pieces_of(amp, count)], planes, writer([(store, first)]))
+    spread_points(index, [[pieces_of(a, count) for a in amp]], planes, writer([(store, first)]))
 
 
 def scatter_rec(core, row, count, planes, ob, cn, first):
     obs = points_of(core, row, 6)
-    parts = [pieces_of(obs, count), [jnp.ones_like(obs)]]
+    parts = [[pieces_of(o, count) for o in obs], [[jnp.ones_like(obs[0])]]]
     index = row(1).astype(jnp.int32)
     spread_points(index, parts, planes, writer([(ob, first), (cn, first)]))
 
@@ -115,14 +113,13 @@
 
 def diagonal_at(damp, row):
     sigma = row(10)
-    first, second = squares(damp)
-    return by_parity(6.0 + first * sigma, 6.0 + second * sigma, sigma.shape[1])
-
-
-def pack_kernel(slow_in, src_in, rec_in, amp_in, obs_in, out, far, src, rec, amp, obs, sem):
+    return [6.0 + square * sigma for square in squares(damp)]
+
+
+def pack_kernel(slow_in, src_in, rec_in, amp_in, obs_in, out, far, slow, src, rec, amp, obs, sem):
     slab = lax.axis_index("pair") * 2 + lax.axis_index("core")
     offset = slab * (2 * 512 * 128)
-    pairs = ((src_in, src), (rec_in, rec), (amp_in, amp), (obs_in, obs), (slow_in, out.at[0:ROWS]))
+    pairs = ((src_in, src), (rec_in, rec), (amp_in, amp), (obs_in, obs), (slow_in, slow))
     copies = [pltpu.make_async_copy(x, y, sem.at[k]) for k, (x, y) in enumerate(pairs)]
     for copy in copies[::-1]:
         copy.start()
@@ -140,13 +137,18 @@
     out[ROWS : ROWS + LIST, :] = far[...]
     for copy in copies[4:]:
         copy.wait()
+    for p in range(2):
+        for j in range(64):
+            at = LINES * p + 8 * j
+            out[at : at + 8, :] = slow[pl.ds(LINES * p + j, 8, stride=64), :]
 
 
 def gather_sigma(sigma, row, store):
     index = row(0).astype(jnp.int32)
     points = index.shape[1]
     rows = lax.broadcasted_iota(jnp.int32, (ROWS, points), 0)
-    pick = jnp.where(rows == index >> 7, 1.0, 0.0).astype(jnp.bfloat16)
+    line = (index >> 16) * LINES + line_of((index >> 7) & 511)
+    pick = jnp.where(rows == line, 1.0, 0.0).astype(jnp.bfloat16)
     high = sigma.astype(jnp.bfloat16)
     low = (sigma - high.astype(jnp.float32)).astype(jnp.bfloat16)
     dims = (((0,), (0,)), ((), ()))
@@ -214,60 +216,64 @@
     return jnp.where(jnp.abs(i - j) == 1, 1.0, 0.0).astype(jnp.bfloat16)
 
 
-def neighbours(ref, t):
-    ext = ref[t]
-    x = ext[PAD : PAD + ROWS]
-    total = ROWS + 2 * PAD
-    down = pltpu.roll(ext, HALF, 0)[PAD : PAD + ROWS]
-    up = pltpu.roll(ext, total - HALF, 0)[PAD : PAD + ROWS]
-    high = x.astype(jnp.bfloat16)
-    low = (x - high.astype(jnp.float32)).astype(jnp.bfloat16)
+def half(ref, t, c):
+    return ref[t, LINES * c : LINES * c + LINES, :]
+
+
+def beside(x):
+    sub = lax.broadcasted_iota(jnp.int32, (8, 128), 0)
+    before = jnp.where(sub == 0, 0.0, pltpu.roll(x[LINES - 8 :], 1, 0))
+    after = jnp.where(sub == 7, 0.0, pltpu.roll(x[:8], 7, 0))
+    across = jnp.concatenate([before, x[: LINES - 8]]) + jnp.concatenate([x[8:], after])
+    turned, rest = x[:TURNED], x[TURNED:]
+    lane = lax.broadcasted_iota(jnp.int32, turned.shape, 1)
+    low = jnp.where(lane == 0, 0.0, pltpu.roll(turned, 1, 1))
+    high = jnp.where(lane == 127, 0.0, pltpu.roll(turned, 127, 1))
     matrix = shift_matrix()
-    along = jnp.dot(high, matrix, preferred_element_type=jnp.float32)
-    along = along + jnp.dot(low, matrix, preferred_element_type=jnp.float32)
-    return x, (down + up) + along
+    coarse = rest.astype(jnp.bfloat16)
+    fine = (rest - coarse.astype(jnp.float32)).astype(jnp.bfloat16)
+    along = jnp.dot(coarse, matrix, preferred_element_type=jnp.float32)
+    along = along + jnp.dot(fine, matrix, preferred_element_type=jnp.float32)
+    return across + jnp.concatenate([low + high, along])
 
 
 def fold(x):
-    return jnp.sum(x.reshape(ROWS // 8, 8, 128), 0)
+    return jnp.sum(x.reshape(LINES // 8, 8, 128), 0)
 
 
 def walk(first, last, body, carry):
     return lax.fori_loop(first, last, body, carry)
 
 
-INNER = pl.ds(PAD, 1024)
-
-
-def advance(src, s_off, inv, i_off, dst, d_off, first, last, dots):
+def nothing():
+    return [jnp.zeros((8, 128), jnp.float32) for _ in range(HALF)]
+
+
+def advance(src, s_off, inv, dst, d_off, first, last, dots):
     def body(t, carry):
-        x, q = neighbours(src, t - s_off)
-        q = q + (src[t - s_off - 1, INNER, :] + src[t - s_off + 1, INNER, :])
-        new = inv[t - i_off] * q
-        dst[t - d_off, INNER, :] = new
-        if not dots:
-            return carry
-        return carry[0] + fold(x * q), carry[1] + fold(new * q)
-
-    zero = jnp.zeros((8, 128), jnp.float32)
-    return walk(first, last, body, (zero, zero) if dots else 0)
+        one, two = [], []
+        for c in range(HALF):
+            x = half(src, t - s_off, c)
+            q = beside(x) + (half(src, t - s_off - 1, c) + half(src, t - s_off + 1, c))
+            new = half(inv, t, c) * q
+            dst[t - d_off, LINES * c : LINES * c + LINES, :] = new
+            if dots:
+                one.append(carry[0][c] + fold(x * q))
+                two.append(carry[1][c] + fold(new * q))
+        return (one, two) if dots else carry
+
+    return walk(first, last, body, (nothing(), nothing()) if dots else 0)
 
 
 def last_moment(src, off):
     def body(t, carry):
-        x, q = neighbours(src, t - off)
-        q = q + 2.0 * src[t - off + 1, INNER, :]
-        return carry + fold(x * q)
-
-    return walk(4, 8, body, jnp.zeros((8, 128), jnp.float32))
-
-
-def clear_pads(*refs):
-    for ref in refs:
-        zero = jnp.zeros((8, 128), jnp.float32)
-        for t in range(ref.shape[0]):
-            ref[t, 0:PAD, :] = zero
-            ref[t, ref.shape[1] - PAD :, :] = zero
+        out = []
+        for c in range(HALF):
+            x = half(src, t - off, c)
+            out.append(carry[c] + fold(x * (beside(x) + 2.0 * half(src, t - off + 1, c))))
+        return out
+
+    return walk(4, 8, body, nothing())
 
 
 def message(moments):
@@ -276,7 +282,7 @@
     out = jnp.zeros((8, 128), jnp.float32)
     for k, moment in enumerate(moments):
         for c in range(HALF):
-            total = jnp.sum(jnp.where(sub % HALF == c, moment, 0.0))
+            total = jnp.sum(moment[c])
             out = out + jnp.where((sub == k) & (lane == c), total, 0.0)
     return out
 
@@ -305,16 +311,7 @@
             p = [a + new / energy * b for a, b in zip(z, p + [0.0 * one])]
             energy = new
     lane = lax.broadcasted_iota(jnp.int32, (1, 128), 1)
-    sub = lax.broadcasted_iota(jnp.int32, (8, 128), 0)
-    out = []
-    for v in x:
-        value = [jnp.sum(jnp.where(lane == c, v, 0.0)) for c in range(HALF)]
-        out.append(jnp.where(sub % HALF == 0, value[0], value[1]))
-    return out
-
-
-def times(pattern, x):
-    return (pattern[None] * x.reshape(ROWS // 8, 8, 128)).reshape(ROWS, 128)
+    return [[jnp.sum(jnp.where(lane == c, v, 0.0)) for c in range(HALF)] for v in x]
 
 
 def fill_inverse(core, square, inv, slab, mine, theirs, base, valid):
@@ -324,7 +321,7 @@
         there = theirs[pl.ds(pl.multiple_of(base + at, 8), 512), :]
         sigma = jnp.where(core == slab % 2, here, there)
         for c in range(HALF):
-            inv[2 * slab + p, pl.ds(c, 512, stride=HALF), :] = valid / (6.0 + square[c] * sigma)
+            inv[2 * slab + p, LINES * c : LINES * c + LINES, :] = valid / (6.0 + square[c] * sigma)
         return 0
 
     lax.fori_loop(0, 2, fill, 0)
@@ -333,18 +330,22 @@
 def forward_own_kernel(damp, own_m, own_t, b_own, inv, v0, v1, held):
     core = lax.axis_index("core")
     square = squares(damp)
-    clear_pads(v0, v1)
     for slab in (2, 3):
         fill_inverse(core, square, inv, slab, own_m, own_t, 0, 1.0)
 
     def start(t, carry):
-        right = b_own[t - 4]
-        new = inv[t] * right
-        v0[t, INNER, :] = new
-        return carry + fold(new * right)
-
-    held[0:8, :] = walk(4, 8, start, jnp.zeros((8, 128), jnp.float32))
-    held[8:16, :], held[16:24, :] = advance(v0, 0, inv, 0, v1, 1, 5, 7, True)
+        out = []
+        for c in range(HALF):
+            right = half(b_own, t - 4, c)
+            new = half(inv, t, c) * right
+            v0[t, LINES * c : LINES * c + LINES, :] = new
+            out.append(carry[c] + fold(new * right))
+        return out
+
+    m0 = walk(4, 8, start, nothing())
+    m1, m2 = advance(v0, 0, inv, v1, 1, 5, 7, True)
+    for k, part in enumerate(m0 + m1 + m2):
+        held[8 * k : 8 * k + 8, :] = part
 
 
 def forward_kernel(
@@ -354,7 +355,6 @@
     low = jnp.where(pair >= 1, 1.0, 0.0)
     high = jnp.where(pair + 1 < lax.axis_size("pair"), 1.0, 0.0)
     square = squares(damp)
-    clear_pads(v2)
     fill_inverse(core, square, inv, 0, low_m, near_t, 0, low)
     fill_inverse(core, square, inv, 1, low_m, near_t, 0, low)
     fill_inverse(core, square, inv, 4, high_m, near_t, SLAB, high)
@@ -362,25 +362,26 @@
 
     def start(off):
         def body(t, carry):
-            v0[t, INNER, :] = inv[t] * b_near[t - off]
+            v0[t] = inv[t] * b_near[t - off]
             return carry
 
         return body
 
-    v0[12, INNER, :] = b_near[8]
+    v0[12] = b_near[8]
     walk(0, 4, start(0), 0)
     walk(8, 12, start(4), 0)
-    advance(v0, 0, inv, 0, v1, 1, 1, 4, False)
-    m1, m2 = advance(v0, 0, inv, 0, v1, 1, 4, 5, True)
-    more1, more2 = advance(v0, 0, inv, 0, v1, 1, 7, 8, True)
-    advance(v0, 0, inv, 0, v1, 1, 8, 12, False)
-    m1 = m1 + more1 + held[8:16, :]
-    m2 = m2 + more2 + held[16:24, :]
-    advance(v1, 1, inv, 0, v2, 2, 2, 4, False)
-    m3, m4 = advance(v1, 1, inv, 0, v2, 2, 4, 8, True)
-    advance(v1, 1, inv, 0, v2, 2, 8, 11, False)
+    kept = [held[8 * k : 8 * k + 8, :] for k in range(3 * HALF)]
+    advance(v0, 0, inv, v1, 1, 1, 4, False)
+    lower = advance(v0, 0, inv, v1, 1, 4, 5, True)
+    upper = advance(v0, 0, inv, v1, 1, 7, 8, True)
+    advance(v0, 0, inv, v1, 1, 8, 12, False)
+    m1 = [a + b + c for a, b, c in zip(lower[0], upper[0], kept[HALF : 2 * HALF])]
+    m2 = [a + b + c for a, b, c in zip(lower[1], upper[1], kept[2 * HALF :])]
+    advance(v1, 1, inv, v2, 2, 2, 4, False)
+    m3, m4 = advance(v1, 1, inv, v2, 2, 4, 8, True)
+    advance(v1, 1, inv, v2, 2, 8, 11, False)
     m5 = last_moment(v2, 2)
-    msg[...] = message([held[0:8, :], m1, m2, m3, m4, m5])
+    msg[...] = message([kept[:HALF], m1, m2, m3, m4, m5])
 
 
 def adjoint_kernel(
@@ -390,27 +391,30 @@
 
     def start(ob, cn, off, own):
         def body(t, carry):
-            w = times(a[0], v0[t, INNER, :]) + times(a[1], v1[t - 1, INNER, :])
-            w = w + times(a[2], v2[t - 2, INNER, :])
-            right = cn[t - off] * w - ob[t - off]
-            new = inv[t] * right
-            u0[t, INNER, :] = new
-            if not own:
-                return carry
-            wave[t - 4] = w
-            return carry + fold(new * right)
+            out = []
+            count = cn[t - off]
+            for c in range(HALF):
+                lines = slice(LINES * c, LINES * c + LINES)
+                w = a[0][c] * half(v0, t, c) + a[1][c] * half(v1, t - 1, c)
+                w = w + a[2][c] * half(v2, t - 2, c)
+                right = count * w - half(ob, t - off, c)
+                new = half(inv, t, c) * right
+                u0[t, lines, :] = new
+                if own:
+                    wave[t - 4, lines, :] = w
+                    out.append(carry[c] + fold(new * right))
+            return out if own else carry
 
         return body
 
-    zero = jnp.zeros((8, 128), jnp.float32)
     walk(2, 4, start(ob_near, cn_near, 2, False), 0)
-    m0 = walk(4, 8, start(ob_own, cn_own, 4, True), zero)
+    m0 = walk(4, 8, start(ob_own, cn_own, 4, True), nothing())
     walk(8, 11, start(ob_near, cn_near, 6, False), 0)
-    advance(u0, 0, inv, 0, u1, 1, 3, 4, False)
-    m1, m2 = advance(u0, 0, inv, 0, u1, 1, 4, 8, True)
-    advance(u0, 0, inv, 0, u1, 1, 8, 10, False)
-    m3, m4 = advance(u1, 1, inv, 0, u2, 2, 4, 8, True)
-    advance(u1, 1, inv, 0, u2, 2, 8, 9, False)
+    advance(u0, 0, inv, u1, 1, 3, 4, False)
+    m1, m2 = advance(u0, 0, inv, u1, 1, 4, 8, True)
+    advance(u0, 0, inv, u1, 1, 8, 10, False)
+    m3, m4 = advance(u1, 1, inv, u2, 2, 4, 8, True)
+    advance(u1, 1, inv, u2, 2, 8, 9, False)
     m5 = last_moment(u2, 2)
     msg[...] = message([m0, m1, m2, m3, m4, m5])
 
@@ -418,21 +422,21 @@
 def gradient_kernel(other, damp, t0, t1, t2, t3, wave, u0, u1, u2, *rest):
     held = rest[-1]
     a = coefficients((t0, t1, t2, t3))
-    sub = lax.broadcasted_iota(jnp.int32, (8, 128), 0)
-    square = jnp.where(sub % HALF == 0, *squares(damp))
-    a = [-square * v for v in a]
+    a = [[-square * v for square, v in zip(squares(damp), one)] for one in a]
     core = lax.axis_index("core")
     core = 1 - core if other else core
     bands = rest[0] if other else rest[-2]
     for p in range(2):
         t = 4 + 2 * core + p
-        x = times(a[0], u0[t, INNER, :]) + times(a[1], u1[t - 1, INNER, :])
-        x = x + times(a[2], u2[t - 2, INNER, :])
-        held[...] = x * wave[t - 4]
-        for band in range(4):
-            at = band * 256
-            both = held[pl.ds(at, 128, stride=HALF), :] + held[pl.ds(at + 1, 128, stride=HALF), :]
-            bands[band, p] = both if other else both + rest[0][band, p]
+        total = 0.0
+        for c in range(HALF):
+            x = a[0][c] * half(u0, t, c) + a[1][c] * half(u1, t - 1, c) + a[2][c] * half(u2, t - 2, c)
+            total = total + x * half(wave, t - 4, c)
+        held[...] = total
+        for s in range(8):
+            band, rows = s // 2, slice(64 * (s % 2), 64 * (s % 2) + 64)
+            part = held[pl.ds(s, 64, stride=8), :]
+            bands[band, p, rows, :] = part if other else part + rest[0][band, p, rows, :]
     if not other:
         lap = lax.axis_index("lap")
         for d in range(4):
@@ -447,6 +451,15 @@
     msg[...] = jnp.full((128, 128), jnp.sum(g * g), jnp.float32)
     before = jnp.where(lap == 2, g3[:, 128:136], g1[:, 128:136])
     prior_y[...] = jnp.where(lap == 0, 0.0, before)
+
+
+def band_of(ref, base, lap):
+    out = None
+    for k in range(4):
+        parts = [ref[pl.ds(base + 2 * k + i, 64, stride=8), :] for i in range(2)]
+        band = jnp.concatenate(parts)
+        out = band if out is None else jnp.where(lap == k, band, out)
+    return out
 
 
 def variation_kernel(slow, own_t, near_t, dual, dual_next, base, send_x, send_y):
@@ -464,8 +477,8 @@
         if p == 0:
             step_x = slow[1, band, :] - here
         else:
-            beyond = near_t[pl.ds(pl.multiple_of(SLAB + start, 8), 128), :]
-            step_x = jnp.where(core == 0, own_t[band, :], beyond) - here
+            beyond = jnp.where(core == 0, band_of(own_t, 0, lap), band_of(near_t, SLAB, lap))
+            step_x = beyond - here
             step_x = jnp.where((core == 1) & (pair == 15), 0.0, step_x)
         rolled = pltpu.roll(here, 127, 0)
         step_y = jnp.where(row == 127, slow[p, after, :][0:1], rolled) - here
@@ -557,7 +570,7 @@
         in_specs=[pl.BlockSpec(memory_space=pltpu.HBM)] * 5,
         out_specs=(VMEM,) * 2,
         scratch_shapes=[
-            pltpu.VMEM((8, 128), jnp.int32), pltpu.VMEM((8, 128), jnp.int32),
+            pltpu.VMEM((ROWS, 128), jnp.float32), pltpu.VMEM((8, 128), jnp.int32), pltpu.VMEM((8, 128), jnp.int32),
             pltpu.VMEM(src_amp.shape, jnp.float32), pltpu.VMEM(observed.shape, jnp.float32),
             pltpu.SemaphoreType.DMA((5,)),
         ],
@@ -576,29 +589,29 @@
     own_t = swapped(packed)
 
     block, near_block = (4, ROWS, 128), (5, ROWS, 128)
-    own = scatter(scatter_own_kernel, "scatter_own", 5, (lists,), [block] * 3)
+    count, near_count = (4, LINES, 128), (5, LINES, 128)
+    own = scatter(scatter_own_kernel, "scatter_own", 5, (lists,), [block, block, count])
     b_own, ob_own, cn_own, first = scatter(
-        scatter_other_kernel, "scatter_other", 5, (packed, own_t), [block] * 3 + [(LIST, 128)], own
+        scatter_other_kernel, "scatter_other", 5, (packed, own_t), [block, block, count, (LIST, 128)], own
     )
     far_m = moved(first, "pair", -2)
-    padded = ROWS + 2 * PAD
     inv, v0, v1, held = pl.pallas_call(
         forward_own_kernel,
         out_shape=(
-            struct(PLANES, ROWS, 128), struct(13, padded, 128), struct(11, padded, 128),
-            struct(24, 128),
+            struct(PLANES, ROWS, 128), struct(13, ROWS, 128), struct(11, ROWS, 128),
+            struct(48, 128),
         ),
         in_specs=[SMEM] + [VMEM] * 3,
         out_specs=(VMEM,) * 4,
         compiler_params=params(2),
         cost_estimate=cost(4),
         name="forward_own",
-    )(damping, slowness.reshape(ROWS, 128), own_t, b_own)
+    )(damping, packed, own_t, b_own)
     low_m, high_m, far_m, held = lax.optimization_barrier((low_m, high_m, far_m, held))
     near_t = swapped(jnp.concatenate([low_m, high_m]))
     b_near, ob_near, cn_near = scatter(
         scatter_mine_kernel, "scatter_mine", 6, (low_m, high_m),
-        [(9, ROWS, 128), near_block, near_block],
+        [(9, ROWS, 128), near_block, near_count],
     )
     near_t, b_near = lax.optimization_barrier((near_t, b_near))
     b_near, = scatter(
@@ -609,8 +622,8 @@
     inv, v0, v1, v2, msg = pl.pallas_call(
         forward_kernel,
         out_shape=(
-            struct(PLANES, ROWS, 128), struct(13, padded, 128), struct(11, padded, 128),
-            struct(9, padded, 128), struct(8, 128),
+            struct(PLANES, ROWS, 128), struct(13, ROWS, 128), struct(11, ROWS, 128),
+            struct(9, ROWS, 128), struct(8, 128),
         ),
         in_specs=[SMEM] + [VMEM] * 8,
         out_specs=(VMEM,) * 5,
@@ -622,14 +635,14 @@
 
     near_t, msg = lax.optimization_barrier((near_t, msg))
     ob_near, cn_near = scatter(
-        scatter_late_kernel, "scatter_late", 5, (high_m, near_t), [near_block] * 2,
+        scatter_late_kernel, "scatter_late", 5, (high_m, near_t), [near_block, near_count],
         (ob_near, cn_near),
     )
     wave, u0, u1, u2, msg = pl.pallas_call(
         adjoint_kernel,
         out_shape=(
-            struct(4, ROWS, 128), struct(13, padded, 128), struct(11, padded, 128),
-            struct(9, padded, 128), struct(8, 128),
+            struct(4, ROWS, 128), struct(13, ROWS, 128), struct(11, ROWS, 128),
+            struct(9, ROWS, 128), struct(8, 128),
         ),
         in_specs=[VMEM] * 12,
         out_specs=(VMEM,) * 5,
@@ -648,7 +661,7 @@
             out_shape=struct(4, 2, 128, 128) if other else (struct(2, 136, 128),) * 4,
             in_specs=[SMEM] + [VMEM] * (8 + len(more)),
             out_specs=VMEM if other else (VMEM,) * 4,
-            scratch_shapes=scratch + [pltpu.VMEM((ROWS, 128), jnp.float32)],
+            scratch_shapes=scratch + [pltpu.VMEM((LINES, 128), jnp.float32)],
             compiler_params=params(8),
             name="gradient",
         )(damping, *terms, wave, u0, u1, u2, *more)

time: 116 us -> 114 us (0.983)
  Pallas kernels: 42.2 us -> 38.9 us
  waiting for transfers between devices: 21.4 us -> 22.6 us
    pallas_call x1, Pallas kernels: 10.1 us -> 8.42 us  [on_device(): pl.pallas_call(forward_kernel, out_shape=(struct(PLANES, ROWS, 128), stru...]
    pallas_call x5, Pallas kernels: 15.5 us -> 14.4 us  [scatter(): pl.pallas_call(kernel, out_shape=tuple((struct(*shape) for shape in shape...]
  transfers between devices with their start and end apart: 22 -> 22, of which waited for: 14 -> 14; matrix products, arithmetic and copies ran while one was open for 0% -> 0% of each run, Pallas kernels for 14% -> 13%
where the time goes in v3:
time: 114 us; the launch traced here: 113 us
  Pallas kernels  38.9 us (34%)
  starting transfers between devices  36.1 us (32%)
  waiting for transfers between devices  22.6 us (20%)
  blocking collectives  14.7 us (13%)
    all_to_all x1, blocking collectives, on_device(): power = lax.all_to_all(power, ('lap', 'pair', 'core'), 0, 0, tiled=True)  14.7 us
    pallas_call x5, Pallas kernels, scatter(): pl.pallas_call(kernel, out_shape=tuple((struct(*shape) for shape in shape...  14.4 us
    ppermute x12, starting transfers between devices, others(): lax.ppermute(x, 'pair', [(i, i ^ d) for i in range(16)])  13.9 us
    ppermute x4, starting transfers between devices, moved(): lax.ppermute(x, axis, [(i, i + by) for i in range(peers) if 0 <= i + by <...  9.87 us
    ppermute x12, waiting for transfers between devices, others(): lax.ppermute(x, 'pair', [(i, i ^ d) for i in range(16)])  9.47 us
    pallas_call x1, Pallas kernels, on_device(): pl.pallas_call(forward_kernel, out_shape=(struct(PLANES, ROWS, 128), stru...  8.42 us
    ppermute x3, starting transfers between devices, swapped(): return lax.ppermute(x, 'core', [(0, 1), (1, 0)])  8.41 us
    pallas_call x1, Pallas kernels, on_device(): pl.pallas_call(adjoint_kernel, out_shape=(struct(4, ROWS, 128), struct(13...  8.26 us
  transfers between devices with their start and end apart: 22, of which 14 were waited for; matrix products, arithmetic and copies ran while one was open for 0% of the time, Pallas kernels for 13%

profile of v3, /device:TPU:1, one launch (start us, length us, event | category | flops | bytes accessed | tf_op | source)
XLA Modules:
  0.0 113.3 jit_solution(13816856686872854005)
XLA Ops:
  0.6 1.4 %pack.1 = (f32[1112,128]{1,0:T(8,128)S(1)}, f32[88,128]{1,0:T(8,128)S(1)}) custom-call(f32[1024,128]{1,0:T(8,128)} %bitcast.7, s32[8,128]{1,0:T(8,128)} %bitcast.10, s32[8,128]{1,0:T(8,128)} %bitcast.11, f32[4,1024]{1,0:T(4,128)} %amp_in.1, f32[4,1024]{1,0:T(4,128)} %obs_in.1), custom_call_target="tpu_custom_call" | custom-call | tf_op jit(solution)/shard_map/pack/pallas_call | solution.py:567
  2.0 1.5 %collective-permute-start = (f32[1112,128]{1,0:T(8,128)S(1)}, f32[1112,128]{1,0:T(8,128)S(1)}, u32[]{:S(2)}, u32[]{:S(2)}) collective-permute-start(f32[1112,128]{1,0:T(8,128)S(1)} %get-tuple-element.64.mine.own_m), channel_id=1, source_target_pairs={{0,1},{1,0},{2,3},{3,2},{4,5},{5,4},{6,7},{7,6},{8,9},{9,8},{10,11... | collective-permute-start | bytes 1708040 | tf_op jit(solution)/shard_map/ppermute | solution.py:536
  3.5 1.3 %collective-permute-start.2 = (f32[1112,128]{1,0:T(8,128)S(1)}, f32[1112,128]{1,0:T(8,128)S(1)}, u32[]{:S(2)}, u32[]{:S(2)}) collective-permute-start(f32[1112,128]{1,0:T(8,128)S(1)} %get-tuple-element.64.mine.own_m), channel_id=1, source_target_pairs={{2,0},{4,2},{6,4},{8,6},{10,8},{12,10},{14,12},{16,14},{18,16},{20... | collective-permute-start | bytes 1708040 | tf_op jit(solution)/shard_map/ppermute | solution.py:532
  4.8 4.3 %collective-permute-start.1 = (f32[1112,128]{1,0:T(8,128)S(1)}, f32[1112,128]{1,0:T(8,128)S(1)}, u32[]{:S(2)}, u32[]{:S(2)}) collective-permute-start(f32[1112,128]{1,0:T(8,128)S(1)} %get-tuple-element.64.mine.own_m), channel_id=1, source_target_pairs={{0,2},{2,4},{4,6},{6,8},{8,10},{10,12},{12,14},{14,16},{16,18},{18... | collective-permute-start | bytes 1708040 | tf_op jit(solution)/shard_map/ppermute | solution.py:532
  9.1 2.7 %scatter_own.1 = (f32[4,1024,128]{2,1,0:T(8,128)S(1)}, f32[4,1024,128]{2,1,0:T(8,128)S(1)}, f32[4,512,128]{2,1,0:T(8,128)S(1)}) custom-call(f32[88,128]{1,0:T(8,128)S(1)} %get-tuple-element.65.lists), custom_call_target="tpu_custom_call" | custom-call | flops 5000000000 | bytes 1000000 | tf_op jit(solution)/shard_map/scatter_own/pallas_call | solution.py:550
  11.8 3.8 %scatter_other.1 = (f32[4,1024,128]{2,1,0:T(8,128)S(1)}, f32[4,1024,128]{2,1,0:T(8,128)S(1)}, f32[4,512,128]{2,1,0:T(8,128)S(1)}, f32[88,128]{1,0:T(8,128)S(1)}) custom-call(f32[1112,128]{1,0:T(8,128)S(1)} %get-tuple-element.64.mine.own_m, ...), custom_call_target="tpu_custom_call", output_to_operand_aliasing={{0}: (2, {}), {1}: (3, {}), {2}: (4, {})} | custom-call | flops 5000000000 | bytes 1000000 | tf_op jit(solution)/shard_map/scatter_other/pallas_call | solution.py:550
  15.6 1.3 %collective-permute-start.3 = (f32[88,128]{1,0:T(8,128)S(1)}, f32[88,128]{1,0:T(8,128)S(1)}, u32[]{:S(2)}, u32[]{:S(2)}) collective-permute-start(f32[88,128]{1,0:T(8,128)S(1)} %get-tuple-element.69), channel_id=1, source_target_pairs={{4,0},{6,2},{8,4},{10,6},{12,8},{14,10},{16,12},{18,14},{20,16},{2... | collective-permute-start | bytes 135176 | tf_op jit(solution)/shard_map/ppermute | solution.py:532
  16.9 2.0 %forward_own.1 = (f32[13,1024,128]{2,1,0:T(8,128)S(1)}, f32[13,1024,128]{2,1,0:T(8,128)S(1)}, f32[11,1024,128]{2,1,0:T(8,128)S(1)}, f32[48,128]{1,0:T(8,128)S(1)}) custom-call(f32[4]{0:T(128)S(1)} %copy-done.1, f32[1112,128]{1,0:T(8,128)S(1)} %get-tuple-element.64.mine.own_m, f32[1112,128]{1,0:T(8,128)S(1)} %collective-permute-done.other.own_t, ...), custom_call_target="tpu_custom_call" | custom-call | flops 4000000000 | bytes 1000000 | tf_op jit(solution)/shard_map/forward_own/pallas_call | solution.py:598
  18.9 1.4 %collective-permute-done.2.high.high_m = f32[1112,128]{1,0:T(8,128)S(1)} collective-permute-done((f32[1112,128]{1,0:T(8,128)S(1)}, f32[1112,128]{1,0:T(8,128)S(1)}, u32[]{:S(2)}, u32[]{:S(2)}) %collective-permute-start.2) | collective-permute-done | bytes 569376 | tf_op jit(solution)/shard_map/ppermute | solution.py:532
  20.4 1.0 collective-permute-done.1.low.low_m
  21.3 4.5 %collective-permute-done.3.far = f32[88,128]{1,0:T(8,128)S(1)} collective-permute-done((f32[88,128]{1,0:T(8,128)S(1)}, f32[88,128]{1,0:T(8,128)S(1)}, u32[]{:S(2)}, u32[]{:S(2)}) %collective-permute-start.3) | collective-permute-done | bytes 45088 | tf_op jit(solution)/shard_map/ppermute | solution.py:532
  25.9 1.7 %collective-permute-start.4 = (f32[2224,128]{1,0:T(8,128)S(1)}, f32[2224,128]{1,0:T(8,128)S(1)}, u32[]{:S(2)}, u32[]{:S(2)}) collective-permute-start(f32[2224,128]{1,0:T(8,128)S(1)} %pad_maximum_fusion), channel_id=1, source_target_pairs={{0,1},{1,0},{2,3},{3,2},{4,5},{5,4},{6,7},{7,6},{8,9},{9,8},{10,11... | collective-permute-start | bytes 3416072 | tf_op jit(solution)/shard_map/ppermute | solution.py:536
  27.6 3.2 %scatter_mine.1 = (f32[9,1024,128]{2,1,0:T(8,128)S(1)}, f32[5,1024,128]{2,1,0:T(8,128)S(1)}, f32[5,512,128]{2,1,0:T(8,128)S(1)}) custom-call(f32[1112,128]{1,0:T(8,128)S(1)} %collective-permute-done.1.low.low_m, f32[1112,128]{1,0:T(8,128)S(1)} %collective-permute-done.2.high.high_m), custom_call_target="tpu_custom_call" | custom-call | flops 6000000000 | bytes 1000000 | tf_op jit(solution)/shard_map/scatter_mine/pallas_call | solution.py:550
  30.9 2.7 %scatter_theirs.1.b_near = f32[9,1024,128]{2,1,0:T(8,128)S(1)} custom-call(f32[4]{0:T(128)S(1)} %copy-done.1, f32[88,128]{1,0:T(8,128)S(1)} %collective-permute-done.3.far, f32[2224,128]{1,0:T(8,128)S(1)} %collective-permute-done.4.near.near_t, f32[9,1024,128]{2,1,0:T(8,128)S(1)} %get-tuple-element.77.b_in), custom_call_target="tpu_custom_call", output_to_operand_aliasing={{}: (3, {})} | custom-call | flops 5000000000 | bytes 1000000 | tf_op jit(solution)/shard_map/scatter_theirs/pallas_call | solution.py:550
  33.6 8.4 %forward.1 = (f32[13,1024,128]{2,1,0:T(8,128)S(1)}, f32[13,1024,128]{2,1,0:T(8,128)S(1)}, f32[11,1024,128]{2,1,0:T(8,128)S(1)}, f32[9,1024,128]{2,1,0:T(8,128)S(1)}, f32[8,128]{1,0:T(8,128)S(1)}) custom-call(f32[4]{0:T(128)S(1)} %copy-done.1, ...), custom_call_target="tpu_custom_call", output_to_operand_aliasing={{0}: (6, {}), {1}: (7, {}), {2}: (8, {})} | custom-call | flops 20000000000 | bytes 1000000 | tf_op jit(solution)/shard_map/forward/pallas_call | solution.py:622
  42.0 3.0 %collective-permute-start.7 = (f32[8,128]{1,0:T(8,128)S(1)}, f32[8,128]{1,0:T(8,128)S(1)}, u32[]{:S(2)}, u32[]{:S(2)}) collective-permute-start(f32[8,128]{1,0:T(8,128)S(1)} %get-tuple-element.84), channel_id=1, source_target_pairs={{0,6},{2,4},{4,2},{6,0},{8,14},{10,12},{12,10},{14,8},{16,22},{18,... | collective-permute-start | bytes 12296 | tf_op jit(solution)/shard_map/ppermute | solution.py:541
  45.0 0.7 collective-permute-start.5
  45.7 0.3 collective-permute-done.7
  46.0 3.0 %collective-permute-done.6 = f32[8,128]{1,0:T(8,128)S(1)} collective-permute-done((f32[8,128]{1,0:T(8,128)S(1)}, f32[8,128]{1,0:T(8,128)S(1)}, u32[]{:S(2)}, u32[]{:S(2)}) %collective-permute-start.6) | collective-permute-done | bytes 4128 | tf_op jit(solution)/shard_map/ppermute | solution.py:541
  49.0 2.9 %collective-permute-start.10 = (f32[8,128]{1,0:T(8,128)S(1)}, f32[8,128]{1,0:T(8,128)S(1)}, u32[]{:S(2)}, u32[]{:S(2)}) collective-permute-start(f32[8,128]{1,0:T(8,128)S(1)} %add_add_fusion.1.t0), channel_id=1, source_target_pairs={{0,24},{2,26},{4,28},{6,30},{8,16},{10,18},{12,20},{14,22},{16,8},... | collective-permute-start | bytes 12296 | tf_op jit(solution)/shard_map/ppermute | solution.py:541
  51.9 0.3 collective-permute-start.9
  52.1 0.4 collective-permute-start.8
  52.5 2.0 %scatter_late.1 = (f32[5,1024,128]{2,1,0:T(8,128)S(1)}, f32[5,512,128]{2,1,0:T(8,128)S(1)}) custom-call(f32[1112,128]{1,0:T(8,128)S(1)} %collective-permute-done.2.high.high_m, f32[2224,128]{1,0:T(8,128)S(1)} %collective-permute-done.4.near.near_t, f32[5,1024,128]{2,1,0:T(8,128)S(1)} %get-tuple-element.91.ob_in, ...), custom_call_target="tpu_custom_call", output_to_operand_aliasing={{0}: (2, {}), {1}: (3, {})} | custom-call | flops 5000000000 | bytes 1000000 | tf_op jit(solution)/shard_map/scatter_late/pallas_call | solution.py:550
  54.5 1.3 %collective-permute-done.9.t2 = f32[8,128]{1,0:T(8,128)S(1)} collective-permute-done((f32[8,128]{1,0:T(8,128)S(1)}, f32[8,128]{1,0:T(8,128)S(1)}, u32[]{:S(2)}, u32[]{:S(2)}) %collective-permute-start.9) | collective-permute-done | bytes 4128 | tf_op jit(solution)/shard_map/ppermute | solution.py:541
  55.8 8.3 %adjoint.1 = (f32[4,1024,128]{2,1,0:T(8,128)S(1)}, f32[13,1024,128]{2,1,0:T(8,128)S(1)}, f32[11,1024,128]{2,1,0:T(8,128)S(1)}, f32[9,1024,128]{2,1,0:T(8,128)S(1)}, f32[8,128]{1,0:T(8,128)S(1)}) custom-call(f32[8,128]{1,0:T(8,128)S(1)} %add_add_fusion.1.t0, ...), custom_call_target="tpu_custom_call", output_to_operand_aliasing={{1}: (5, {}), {2}: (6, {}), {3}: (7, {})} | custom-call | flops 14000000000 | bytes 1000000 | tf_op jit(solution)/shard_map/adjoint/pallas_call | solution.py:641
  64.1 2.2 %collective-permute-start.13 = (f32[8,128]{1,0:T(8,128)S(1)}, f32[8,128]{1,0:T(8,128)S(1)}, u32[]{:S(2)}, u32[]{:S(2)}) collective-permute-start(f32[8,128]{1,0:T(8,128)S(1)} %get-tuple-element.95), channel_id=1, source_target_pairs={{0,6},{2,4},{4,2},{6,0},{8,14},{10,12},{12,10},{14,8},{16,22},{18,... | collective-permute-start | bytes 12296 | tf_op jit(solution)/shard_map/ppermute | solution.py:541
  66.3 0.8 collective-permute-start.12
  67.1 0.3 collective-permute-start.11
  67.4 0.4 collective-permute-done.13
  67.9 2.4 %collective-permute-done.12 = f32[8,128]{1,0:T(8,128)S(1)} collective-permute-done((f32[8,128]{1,0:T(8,128)S(1)}, f32[8,128]{1,0:T(8,128)S(1)}, u32[]{:S(2)}, u32[]{:S(2)}) %collective-permute-start.12) | collective-permute-done | bytes 4128 | tf_op jit(solution)/shard_map/ppermute | solution.py:541
  70.3 1.4 %collective-permute-start.16 = (f32[8,128]{1,0:T(8,128)S(1)}, f32[8,128]{1,0:T(8,128)S(1)}, u32[]{:S(2)}, u32[]{:S(2)}) collective-permute-start(f32[8,128]{1,0:T(8,128)S(1)} %add_add_fusion.t0), channel_id=1, source_target_pairs={{0,24},{2,26},{4,28},{6,30},{8,16},{10,18},{12,20},{14,22},{16,8},... | collective-permute-start | bytes 12296 | tf_op jit(solution)/shard_map/ppermute | solution.py:541
  71.7 0.2 collective-permute-start.15
  71.9 1.7 %collective-permute-start.14 = (f32[8,128]{1,0:T(8,128)S(1)}, f32[8,128]{1,0:T(8,128)S(1)}, u32[]{:S(2)}, u32[]{:S(2)}) collective-permute-start(f32[8,128]{1,0:T(8,128)S(1)} %add_add_fusion.t0), channel_id=1, source_target_pairs={{0,8},{2,10},{4,12},{6,14},{8,0},{10,2},{12,4},{14,6},{16,24},{18,... | collective-permute-start | bytes 12296 | tf_op jit(solution)/shard_map/ppermute | solution.py:541
  73.6 0.6 collective-permute-done.16.t3
  74.2 1.5 %collective-permute-done.15.t2 = f32[8,128]{1,0:T(8,128)S(1)} collective-permute-done((f32[8,128]{1,0:T(8,128)S(1)}, f32[8,128]{1,0:T(8,128)S(1)}, u32[]{:S(2)}, u32[]{:S(2)}) %collective-permute-start.15) | collective-permute-done | bytes 4128 | tf_op jit(solution)/shard_map/ppermute | solution.py:541
  75.7 1.2 %gradient.2 = f32[4,2,128,128]{3,2,1,0:T(8,128)S(1)} custom-call(f32[4]{0:T(128)S(1)} %copy-done.1, f32[8,128]{1,0:T(8,128)S(1)} %add_add_fusion.t0, f32[8,128]{1,0:T(8,128)S(1)} %collective-permute-done.14.t1, f32[8,128]{1,0:T(8,128)S(1)} %collective-permute-done.15.t2, f32[8,128]{1,0:T(8,128)S(1)} %collective-permute-done.16.t3, ...), custom_call_target="tpu_custom_call" | custom-call | tf_op jit(solution)/shard_map/gradient/pallas_call | solution.py:659
  76.9 5.2 %collective-permute-start.17 = (f32[4,2,128,128]{3,2,1,0:T(8,128)S(1)}, f32[4,2,128,128]{3,2,1,0:T(8,128)S(1)}, u32[]{:S(2)}, u32[]{:S(2)}) collective-permute-start(f32[4,2,128,128]{3,2,1,0:T(8,128)S(1)} %gradient.2), channel_id=1, source_target_pairs={{0,1},{1,0},{2,3},{3,2},{4,5},{5,4},{6,7},{7,6},{8,9},{9,8},{10,11... | collective-permute-start | bytes 1572872 | tf_op jit(solution)/shard_map/ppermute | solution.py:536
  82.1 1.0 variation.1
  83.1 0.5 collective-permute-done.17.rest_0_
  83.7 1.3 %gradient.3 = (f32[2,136,128]{2,1,0:T(8,128)S(1)}, f32[2,136,128]{2,1,0:T(8,128)S(1)}, f32[2,136,128]{2,1,0:T(8,128)S(1)}, f32[2,136,128]{2,1,0:T(8,128)S(1)}) custom-call(f32[4]{0:T(128)S(1)} %copy-done.1, f32[8,128]{1,0:T(8,128)S(1)} %add_add_fusion.t0, f32[8,128]{1,0:T(8,128)S(1)} %collective-permute-done.14.t1, f32[8,128]{1,0:T(8,128)S(1)} %collective-permute-done.15.t2, ...), custom_call_target="tpu_custom_call" | custom-call | tf_op jit(solution)/shard_map/gradient/pallas_call | solution.py:659
  85.0 1.3 %collective-permute-start.18 = (f32[2,136,128]{2,1,0:T(8,128)S(1)}, f32[2,136,128]{2,1,0:T(8,128)S(1)}, u32[]{:S(2)}, u32[]{:S(2)}) collective-permute-start(f32[2,136,128]{2,1,0:T(8,128)S(1)} %get-tuple-element.113), channel_id=1, source_target_pairs={{0,32},{32,0},{64,96},{96,64},{1,33},{33,1},{65,97},{97,65},{2,34}... | collective-permute-start | bytes 417800 | tf_op jit(solution)/shard_map/ppermute | solution.py:687
  86.3 2.4 %collective-permute-start.19 = (f32[2,136,128]{2,1,0:T(8,128)S(1)}, f32[2,136,128]{2,1,0:T(8,128)S(1)}, u32[]{:S(2)}, u32[]{:S(2)}) collective-permute-start(f32[2,136,128]{2,1,0:T(8,128)S(1)} %get-tuple-element.114), channel_id=1, source_target_pairs={{0,64},{32,96},{64,0},{96,32},{1,65},{33,97},{65,1},{97,33},{2,66}... | collective-permute-start | bytes 417800 | tf_op jit(solution)/shard_map/ppermute | solution.py:687
  88.9 3.0 %collective-permute-start.21 = (f32[1,128,128]{2,1,0:T(8,128)S(1)}, f32[1,128,128]{2,1,0:T(8,128)S(1)}, u32[]{:S(2)}, u32[]{:S(2)}) collective-permute-start(f32[1,128,128]{2,1,0:T(8,128)S(1)} %get-tuple-element.116), channel_id=1, source_target_pairs={{0,1},{1,2},{2,3},{3,4},{4,5},{5,6},{6,7},{7,8},{8,9},{9,10},{10,1... | collective-permute-start | bytes 196616 | tf_op jit(solution)/shard_map/ppermute | solution.py:532
  91.9 1.3 %collective-permute-done.21.prior_x = f32[1,128,128]{2,1,0:T(8,128)S(1)} collective-permute-done((f32[1,128,128]{2,1,0:T(8,128)S(1)}, f32[1,128,128]{2,1,0:T(8,128)S(1)}, u32[]{:S(2)}, u32[]{:S(2)}) %collective-permute-start.21) | collective-permute-done | bytes 65568 | tf_op jit(solution)/shard_map/ppermute | solution.py:532
  93.3 1.9 %collective-permute-done.19.g2 = f32[2,136,128]{2,1,0:T(8,128)S(1)} collective-permute-done((f32[2,136,128]{2,1,0:T(8,128)S(1)}, f32[2,136,128]{2,1,0:T(8,128)S(1)}, u32[]{:S(2)}, u32[]{:S(2)}) %collective-permute-start.19) | collective-permute-done | bytes 139296 | tf_op jit(solution)/shard_map/ppermute | solution.py:687
  95.2 2.5 %collective-permute-done.20.g3 = f32[2,136,128]{2,1,0:T(8,128)S(1)} collective-permute-done((f32[2,136,128]{2,1,0:T(8,128)S(1)}, f32[2,136,128]{2,1,0:T(8,128)S(1)}, u32[]{:S(2)}, u32[]{:S(2)}) %collective-permute-start.20) | collective-permute-done | bytes 139296 | tf_op jit(solution)/shard_map/ppermute | solution.py:687
  97.9 14.7 %all_to_all.9 = f32[128,1,128]{2,1,0:T(1,128)S(1)} all-to-all(f32[128,1,128]{2,1,0:T(1,128)S(1)} %bitcast.9), channel_id=1, replica_groups=mesh['lap'=4,'pair'=16,'core'=2] {'lap','pair','core'}, dimensions={0} | all-to-all | bytes 131072 | tf_op jit(solution)/shard_map/all_to_all | solution.py:699
  112.6 0.7 model.1
  (20 shorter events, 0.5 us)
Async XLA Ops:
  2.0 9.8 %collective-permute-start = (f32[1112,128]{1,0:T(8,128)S(1)}, f32[1112,128]{1,0:T(8,128)S(1)}, u32[]{:S(2)}, u32[]{:S(2)}) collective-permute-start(f32[1112,128]{1,0:T(8,128)S(1)} %get-tuple-element.64.mine.own_m), channel_id=1, source_target_pairs={{0,1},{1,0},{2,3},{3,2},{4,5},{5,4},{6,7},{7,6},{8,9},{9,8},{10,11... | collective-permute-start | bytes 1708040 | tf_op jit(solution)/shard_map/ppermute | solution.py:536
  3.5 16.8 %collective-permute-start.2 = (f32[1112,128]{1,0:T(8,128)S(1)}, f32[1112,128]{1,0:T(8,128)S(1)}, u32[]{:S(2)}, u32[]{:S(2)}) collective-permute-start(f32[1112,128]{1,0:T(8,128)S(1)} %get-tuple-element.64.mine.own_m), channel_id=1, source_target_pairs={{2,0},{4,2},{6,4},{8,6},{10,8},{12,10},{14,12},{16,14},{18,16},{20... | collective-permute-start | bytes 1708040 | tf_op jit(solution)/shard_map/ppermute | solution.py:532
  4.8 16.5 %collective-permute-start.1 = (f32[1112,128]{1,0:T(8,128)S(1)}, f32[1112,128]{1,0:T(8,128)S(1)}, u32[]{:S(2)}, u32[]{:S(2)}) collective-permute-start(f32[1112,128]{1,0:T(8,128)S(1)} %get-tuple-element.64.mine.own_m), channel_id=1, source_target_pairs={{0,2},{2,4},{4,6},{6,8},{8,10},{10,12},{12,14},{14,16},{16,18},{18... | collective-permute-start | bytes 1708040 | tf_op jit(solution)/shard_map/ppermute | solution.py:532
  11.8 5.1 %copy-start.1 = (f32[4]{0:T(128)S(1)}, f32[4]{0:T(128)}, u32[]{:S(2)}) copy-start(f32[4]{0:T(128)} %damp.9) | copy-start | bytes 52
  15.6 10.3 %collective-permute-start.3 = (f32[88,128]{1,0:T(8,128)S(1)}, f32[88,128]{1,0:T(8,128)S(1)}, u32[]{:S(2)}, u32[]{:S(2)}) collective-permute-start(f32[88,128]{1,0:T(8,128)S(1)} %get-tuple-element.69), channel_id=1, source_target_pairs={{4,0},{6,2},{8,4},{10,6},{12,8},{14,10},{16,12},{18,14},{20,16},{2... | collective-permute-start | bytes 135176 | tf_op jit(solution)/shard_map/ppermute | solution.py:532
  25.9 4.9 %collective-permute-start.4 = (f32[2224,128]{1,0:T(8,128)S(1)}, f32[2224,128]{1,0:T(8,128)S(1)}, u32[]{:S(2)}, u32[]{:S(2)}) collective-permute-start(f32[2224,128]{1,0:T(8,128)S(1)} %pad_maximum_fusion), channel_id=1, source_target_pairs={{0,1},{1,0},{2,3},{3,2},{4,5},{5,4},{6,7},{7,6},{8,9},{9,8},{10,11... | collective-permute-start | bytes 3416072 | tf_op jit(solution)/shard_map/ppermute | solution.py:536
  42.0 4.0 %collective-permute-start.7 = (f32[8,128]{1,0:T(8,128)S(1)}, f32[8,128]{1,0:T(8,128)S(1)}, u32[]{:S(2)}, u32[]{:S(2)}) collective-permute-start(f32[8,128]{1,0:T(8,128)S(1)} %get-tuple-element.84), channel_id=1, source_target_pairs={{0,6},{2,4},{4,2},{6,0},{8,14},{10,12},{12,10},{14,8},{16,22},{18,... | collective-permute-start | bytes 12296 | tf_op jit(solution)/shard_map/ppermute | solution.py:541
  45.0 4.0 %collective-permute-start.6 = (f32[8,128]{1,0:T(8,128)S(1)}, f32[8,128]{1,0:T(8,128)S(1)}, u32[]{:S(2)}, u32[]{:S(2)}) collective-permute-start(f32[8,128]{1,0:T(8,128)S(1)} %get-tuple-element.84), channel_id=1, source_target_pairs={{0,4},{2,6},{4,0},{6,2},{8,12},{10,14},{12,8},{14,10},{16,20},{18,... | collective-permute-start | bytes 12296 | tf_op jit(solution)/shard_map/ppermute | solution.py:541
  45.0 4.0 %collective-permute-start.5 = (f32[8,128]{1,0:T(8,128)S(1)}, f32[8,128]{1,0:T(8,128)S(1)}, u32[]{:S(2)}, u32[]{:S(2)}) collective-permute-start(f32[8,128]{1,0:T(8,128)S(1)} %get-tuple-element.84), channel_id=1, source_target_pairs={{0,2},{2,0},{4,6},{6,4},{8,10},{10,8},{12,14},{14,12},{16,18},{18,... | collective-permute-start | bytes 12296 | tf_op jit(solution)/shard_map/ppermute | solution.py:541
  49.0 5.6 %collective-permute-start.10 = (f32[8,128]{1,0:T(8,128)S(1)}, f32[8,128]{1,0:T(8,128)S(1)}, u32[]{:S(2)}, u32[]{:S(2)}) collective-permute-start(f32[8,128]{1,0:T(8,128)S(1)} %add_add_fusion.1.t0), channel_id=1, source_target_pairs={{0,24},{2,26},{4,28},{6,30},{8,16},{10,18},{12,20},{14,22},{16,8},... | collective-permute-start | bytes 12296 | tf_op jit(solution)/shard_map/ppermute | solution.py:541
  51.9 4.0 %collective-permute-start.9 = (f32[8,128]{1,0:T(8,128)S(1)}, f32[8,128]{1,0:T(8,128)S(1)}, u32[]{:S(2)}, u32[]{:S(2)}) collective-permute-start(f32[8,128]{1,0:T(8,128)S(1)} %add_add_fusion.1.t0), channel_id=1, source_target_pairs={{0,16},{2,18},{4,20},{6,22},{8,24},{10,26},{12,28},{14,30},{16,0},... | collective-permute-start | bytes 12296 | tf_op jit(solution)/shard_map/ppermute | solution.py:541
  52.1 3.7 %collective-permute-start.8 = (f32[8,128]{1,0:T(8,128)S(1)}, f32[8,128]{1,0:T(8,128)S(1)}, u32[]{:S(2)}, u32[]{:S(2)}) collective-permute-start(f32[8,128]{1,0:T(8,128)S(1)} %add_add_fusion.1.t0), channel_id=1, source_target_pairs={{0,8},{2,10},{4,12},{6,14},{8,0},{10,2},{12,4},{14,6},{16,24},{18,... | collective-permute-start | bytes 12296 | tf_op jit(solution)/shard_map/ppermute | solution.py:541
  64.1 3.7 %collective-permute-start.13 = (f32[8,128]{1,0:T(8,128)S(1)}, f32[8,128]{1,0:T(8,128)S(1)}, u32[]{:S(2)}, u32[]{:S(2)}) collective-permute-start(f32[8,128]{1,0:T(8,128)S(1)} %get-tuple-element.95), channel_id=1, source_target_pairs={{0,6},{2,4},{4,2},{6,0},{8,14},{10,12},{12,10},{14,8},{16,22},{18,... | collective-permute-start | bytes 12296 | tf_op jit(solution)/shard_map/ppermute | solution.py:541
  66.3 4.0 %collective-permute-start.12 = (f32[8,128]{1,0:T(8,128)S(1)}, f32[8,128]{1,0:T(8,128)S(1)}, u32[]{:S(2)}, u32[]{:S(2)}) collective-permute-start(f32[8,128]{1,0:T(8,128)S(1)} %get-tuple-element.95), channel_id=1, source_target_pairs={{0,4},{2,6},{4,0},{6,2},{8,12},{10,14},{12,8},{14,10},{16,20},{18,... | collective-permute-start | bytes 12296 | tf_op jit(solution)/shard_map/ppermute | solution.py:541
  67.1 3.2 %collective-permute-start.11 = (f32[8,128]{1,0:T(8,128)S(1)}, f32[8,128]{1,0:T(8,128)S(1)}, u32[]{:S(2)}, u32[]{:S(2)}) collective-permute-start(f32[8,128]{1,0:T(8,128)S(1)} %get-tuple-element.95), channel_id=1, source_target_pairs={{0,2},{2,0},{4,6},{6,4},{8,10},{10,8},{12,14},{14,12},{16,18},{18,... | collective-permute-start | bytes 12296 | tf_op jit(solution)/shard_map/ppermute | solution.py:541
  70.3 3.9 %collective-permute-start.16 = (f32[8,128]{1,0:T(8,128)S(1)}, f32[8,128]{1,0:T(8,128)S(1)}, u32[]{:S(2)}, u32[]{:S(2)}) collective-permute-start(f32[8,128]{1,0:T(8,128)S(1)} %add_add_fusion.t0), channel_id=1, source_target_pairs={{0,24},{2,26},{4,28},{6,30},{8,16},{10,18},{12,20},{14,22},{16,8},... | collective-permute-start | bytes 12296 | tf_op jit(solution)/shard_map/ppermute | solution.py:541
  71.7 4.0 %collective-permute-start.15 = (f32[8,128]{1,0:T(8,128)S(1)}, f32[8,128]{1,0:T(8,128)S(1)}, u32[]{:S(2)}, u32[]{:S(2)}) collective-permute-start(f32[8,128]{1,0:T(8,128)S(1)} %add_add_fusion.t0), channel_id=1, source_target_pairs={{0,16},{2,18},{4,20},{6,22},{8,24},{10,26},{12,28},{14,30},{16,0},... | collective-permute-start | bytes 12296 | tf_op jit(solution)/shard_map/ppermute | solution.py:541
  71.9 3.7 %collective-permute-start.14 = (f32[8,128]{1,0:T(8,128)S(1)}, f32[8,128]{1,0:T(8,128)S(1)}, u32[]{:S(2)}, u32[]{:S(2)}) collective-permute-start(f32[8,128]{1,0:T(8,128)S(1)} %add_add_fusion.t0), channel_id=1, source_target_pairs={{0,8},{2,10},{4,12},{6,14},{8,0},{10,2},{12,4},{14,6},{16,24},{18,... | collective-permute-start | bytes 12296 | tf_op jit(solution)/shard_map/ppermute | solution.py:541
  75.7 6.5 %copy-start = (f32[2,512,128]{2,1,0:T(8,128)S(1)}, f32[2,512,128]{2,1,0:T(8,128)}, u32[]{:S(2)}) copy-start(f32[2,512,128]{2,1,0:T(8,128)} %slow) | copy-start | bytes 1572868
  75.7 6.5 %copy-start.2 = (f32[3,2,128,128]{3,2,1,0:T(8,128)S(1)}, f32[3,2,128,128]{3,2,1,0:T(8,128)}, u32[]{:S(2)}) copy-start(f32[3,2,128,128]{3,2,1,0:T(8,128)} %dual) | copy-start | bytes 1179652
  76.9 6.8 %collective-permute-start.17 = (f32[4,2,128,128]{3,2,1,0:T(8,128)S(1)}, f32[4,2,128,128]{3,2,1,0:T(8,128)S(1)}, u32[]{:S(2)}, u32[]{:S(2)}) collective-permute-start(f32[4,2,128,128]{3,2,1,0:T(8,128)S(1)} %gradient.2), channel_id=1, source_target_pairs={{0,1},{1,0},{2,3},{3,2},{4,5},{5,4},{6,7},{7,6},{8,9},{9,8},{10,11... | collective-permute-start | bytes 1572872 | tf_op jit(solution)/shard_map/ppermute | solution.py:536
  85.0 8.3 %collective-permute-start.18 = (f32[2,136,128]{2,1,0:T(8,128)S(1)}, f32[2,136,128]{2,1,0:T(8,128)S(1)}, u32[]{:S(2)}, u32[]{:S(2)}) collective-permute-start(f32[2,136,128]{2,1,0:T(8,128)S(1)} %get-tuple-element.113), channel_id=1, source_target_pairs={{0,32},{32,0},{64,96},{96,64},{1,33},{33,1},{65,97},{97,65},{2,34}... | collective-permute-start | bytes 417800 | tf_op jit(solution)/shard_map/ppermute | solution.py:687
  86.3 8.9 %collective-permute-start.19 = (f32[2,136,128]{2,1,0:T(8,128)S(1)}, f32[2,136,128]{2,1,0:T(8,128)S(1)}, u32[]{:S(2)}, u32[]{:S(2)}) collective-permute-start(f32[2,136,128]{2,1,0:T(8,128)S(1)} %get-tuple-element.114), channel_id=1, source_target_pairs={{0,64},{32,96},{64,0},{96,32},{1,65},{33,97},{65,1},{97,33},{2,66}... | collective-permute-start | bytes 417800 | tf_op jit(solution)/shard_map/ppermute | solution.py:687
  88.7 8.9 %collective-permute-start.20 = (f32[2,136,128]{2,1,0:T(8,128)S(1)}, f32[2,136,128]{2,1,0:T(8,128)S(1)}, u32[]{:S(2)}, u32[]{:S(2)}) collective-permute-start(f32[2,136,128]{2,1,0:T(8,128)S(1)} %get-tuple-element.115), channel_id=1, source_target_pairs={{0,96},{32,64},{64,32},{96,0},{1,97},{33,65},{65,33},{97,1},{2,98}... | collective-permute-start | bytes 417800 | tf_op jit(solution)/shard_map/ppermute | solution.py:687
  88.9 4.3 %collective-permute-start.21 = (f32[1,128,128]{2,1,0:T(8,128)S(1)}, f32[1,128,128]{2,1,0:T(8,128)S(1)}, u32[]{:S(2)}, u32[]{:S(2)}) collective-permute-start(f32[1,128,128]{2,1,0:T(8,128)S(1)} %get-tuple-element.116), channel_id=1, source_target_pairs={{0,1},{1,2},{2,3},{3,4},{4,5},{5,6},{6,7},{7,8},{8,9},{9,10},{10,1... | collective-permute-start | bytes 196616 | tf_op jit(solution)/shard_map/ppermute | solution.py:532

commit v4 on v3

--- a/solution.py
+++ b/solution.py
@@ -166,11 +166,7 @@
     scatter_rec(core, row, 2, 2, ob, cn, 2 * h)
 
 
-def scatter_own_kernel(lists, b, ob, cn):
-    scatter_slab(lax.axis_index("core"), functools.partial(list_row, lists, 0), b, ob, cn)
-
-
-def scatter_other_kernel(mine, other, b_in, ob_in, cn_in, b, ob, cn, first):
+def scatter_other_kernel(mine, other, b, ob, cn, first):
     core = lax.axis_index("core")
     whole = jnp.where(core == 0, mine[...], other[...])
     first[...] = whole[ROWS:SLAB]
@@ -179,35 +175,38 @@
     scatter_slab(1 - lax.axis_index("core"), row, b, ob, cn)
 
 
-def scatter_near(core, heavy, heavy_low, light, light_low, b):
-    scatter_src(core, heavy, 2, b, jnp.where(heavy_low, 2, 4))
-    scatter_src(core, light, 1, b, jnp.where(light_low, 0, 6))
-
-
-def scatter_mine_kernel(low, high, b, ob, cn):
-    core = lax.axis_index("core")
-    heavy = either(core, (high, ROWS), (low, ROWS))
-    light = either(core, (low, ROWS), (high, ROWS))
-    scatter_near(core, heavy, core == 1, light, core == 0, b)
-    scatter_rec(core, heavy, 2, 2, ob, cn, jnp.where(core == 1, 0, 2))
-
-
-def scatter_theirs_kernel(damp, far, near, b_in, b):
-    core = lax.axis_index("core")
-    low_at, high_at = ROWS, SLAB + ROWS
-    heavy = either(core, (near, low_at), (near, high_at))
-    light = either(core, (near, high_at), (near, low_at))
-    scatter_near(core, heavy, core == 0, light, core == 1, b)
+def scatter_own_kernel(lists, first_in, b_in, ob_in, cn_in, b, ob, cn):
+    scatter_slab(lax.axis_index("core"), functools.partial(list_row, lists, 0), b, ob, cn)
+
+
+def lists_of(ref):
+    return functools.partial(list_row, ref, ROWS)
+
+
+def scatter_mine_kernel(damp, touch, beyond, far, b):
+    core = lax.axis_index("core")
+    scatter_src(core, lists_of(touch), 2, b, jnp.where(core == 0, 4, 2))
+    scatter_src(core, lists_of(beyond), 1, b, jnp.where(core == 0, 0, 6))
     last = functools.partial(list_row, far, 0)
     scatter_src(core, last, 1, b, 8, diagonal_at(damp, last), 1)
 
 
-def scatter_late_kernel(high, near, ob_in, cn_in, ob, cn):
-    core = lax.axis_index("core")
-    low_at, high_at = ROWS, SLAB + ROWS
-    heavy = either(core, (near, low_at), (near, high_at))
-    scatter_rec(core, heavy, 2, 2, ob, cn, jnp.where(core == 0, 0, 2))
-    scatter_rec(core, either(core, (near, high_at), (high, ROWS)), 1, 1, ob, cn, 4)
+def scatter_theirs_kernel(touch, beyond, b_in, b):
+    core = lax.axis_index("core")
+    scatter_src(core, lists_of(touch), 2, b, jnp.where(core == 0, 2, 4))
+    scatter_src(core, lists_of(beyond), 1, b, jnp.where(core == 0, 6, 0))
+
+
+def scatter_later_kernel(mine, ob, cn):
+    core = lax.axis_index("core")
+    scatter_rec(core, lists_of(mine), 2, 2, ob, cn, jnp.where(core == 0, 2, 0))
+
+
+def scatter_late_kernel(theirs, beyond_m, beyond_t, ob_in, cn_in, ob, cn):
+    core = lax.axis_index("core")
+    scatter_rec(core, lists_of(theirs), 2, 2, ob, cn, jnp.where(core == 0, 0, 2))
+    upper = either(core, (beyond_t, ROWS), (beyond_m, ROWS))
+    scatter_rec(core, upper, 1, 1, ob, cn, 4)
 
 
 def shift_matrix():
@@ -220,11 +219,16 @@
     return ref[t, LINES * c : LINES * c + LINES, :]
 
 
+def next_line(x):
+    sub = lax.broadcasted_iota(jnp.int32, (8, 128), 0)
+    after = jnp.where(sub == 7, 0.0, pltpu.roll(x[:8], 7, 0))
+    return jnp.concatenate([x[8:], after])
+
+
 def beside(x):
     sub = lax.broadcasted_iota(jnp.int32, (8, 128), 0)
     before = jnp.where(sub == 0, 0.0, pltpu.roll(x[LINES - 8 :], 1, 0))
-    after = jnp.where(sub == 7, 0.0, pltpu.roll(x[:8], 7, 0))
-    across = jnp.concatenate([before, x[: LINES - 8]]) + jnp.concatenate([x[8:], after])
+    across = jnp.concatenate([before, x[: LINES - 8]]) + next_line(x)
     turned, rest = x[:TURNED], x[TURNED:]
     lane = lax.broadcasted_iota(jnp.int32, turned.shape, 1)
     low = jnp.where(lane == 0, 0.0, pltpu.roll(turned, 1, 1))
@@ -270,10 +274,13 @@
         out = []
         for c in range(HALF):
             x = half(src, t - off, c)
-            out.append(carry[c] + fold(x * (beside(x) + 2.0 * half(src, t - off + 1, c))))
+            lane = lax.broadcasted_iota(jnp.int32, x.shape, 1)
+            along = jnp.where(lane == 127, 0.0, pltpu.roll(x, 127, 1))
+            q = (next_line(x) + along) + half(src, t - off + 1, c)
+            out.append(carry[c] + fold(x * q))
         return out
 
-    return walk(4, 8, body, nothing())
+    return [2.0 * m for m in walk(4, 8, body, nothing())]
 
 
 def message(moments):
@@ -314,11 +321,11 @@
     return [[jnp.sum(jnp.where(lane == c, v, 0.0)) for c in range(HALF)] for v in x]
 
 
-def fill_inverse(core, square, inv, slab, mine, theirs, base, valid):
+def fill_inverse(core, square, inv, slab, mine, theirs, valid):
     def fill(p, _):
         at = pl.multiple_of(p * 512, 512)
         here = mine[pl.ds(at, 512), :]
-        there = theirs[pl.ds(pl.multiple_of(base + at, 8), 512), :]
+        there = theirs[pl.ds(at, 512), :]
         sigma = jnp.where(core == slab % 2, here, there)
         for c in range(HALF):
             inv[2 * slab + p, LINES * c : LINES * c + LINES, :] = valid / (6.0 + square[c] * sigma)
@@ -331,7 +338,7 @@
     core = lax.axis_index("core")
     square = squares(damp)
     for slab in (2, 3):
-        fill_inverse(core, square, inv, slab, own_m, own_t, 0, 1.0)
+        fill_inverse(core, square, inv, slab, own_m, own_t, 1.0)
 
     def start(t, carry):
         out = []
@@ -349,16 +356,17 @@
 
 
 def forward_kernel(
-    damp, low_m, high_m, near_t, b_near, held, inv_in, v0_in, v1_in, inv, v0, v1, v2, msg
+    damp, touch_m, touch_t, beyond_m, beyond_t, b_near, held, inv_in, v0_in, v1_in,
+    inv, v0, v1, v2, msg,
 ):
     pair, core = lax.axis_index("pair"), lax.axis_index("core")
     low = jnp.where(pair >= 1, 1.0, 0.0)
     high = jnp.where(pair + 1 < lax.axis_size("pair"), 1.0, 0.0)
     square = squares(damp)
-    fill_inverse(core, square, inv, 0, low_m, near_t, 0, low)
-    fill_inverse(core, square, inv, 1, low_m, near_t, 0, low)
-    fill_inverse(core, square, inv, 4, high_m, near_t, SLAB, high)
-    fill_inverse(core, square, inv, 5, high_m, near_t, SLAB, high)
+    fill_inverse(core, square, inv, 0, beyond_m, beyond_t, low)
+    fill_inverse(core, square, inv, 1, touch_m, touch_t, low)
+    fill_inverse(core, square, inv, 4, touch_m, touch_t, high)
+    fill_inverse(core, square, inv, 5, beyond_m, beyond_t, high)
 
     def start(off):
         def body(t, carry):
@@ -453,16 +461,16 @@
     prior_y[...] = jnp.where(lap == 0, 0.0, before)
 
 
-def band_of(ref, base, lap):
+def band_of(ref, lap):
     out = None
     for k in range(4):
-        parts = [ref[pl.ds(base + 2 * k + i, 64, stride=8), :] for i in range(2)]
+        parts = [ref[pl.ds(2 * k + i, 64, stride=8), :] for i in range(2)]
         band = jnp.concatenate(parts)
         out = band if out is None else jnp.where(lap == k, band, out)
     return out
 
 
-def variation_kernel(slow, own_t, near_t, dual, dual_next, base, send_x, send_y):
+def variation_kernel(slow, own_t, touch_t, dual, dual_next, base, send_x, send_y):
     lap, pair, core = (lax.axis_index(name) for name in ("lap", "pair", "core"))
     start = pl.multiple_of(lap * 128, 128)
     band = pl.ds(start, 128)
@@ -477,7 +485,7 @@
         if p == 0:
             step_x = slow[1, band, :] - here
         else:
-            beyond = jnp.where(core == 0, band_of(own_t, 0, lap), band_of(near_t, SLAB, lap))
+            beyond = jnp.where(core == 0, band_of(own_t, lap), band_of(touch_t, lap))
             step_x = beyond - here
             step_x = jnp.where((core == 1) & (pair == 15), 0.0, step_x)
         rolled = pltpu.roll(here, 127, 0)
@@ -520,7 +528,7 @@
 
 
 def cost(work):
-    return pl.CostEstimate(flops=work * 10**9, bytes_accessed=10**6, transcendentals=0)
+    return pl.CostEstimate(flops=work * 10**7, bytes_accessed=10**4, transcendentals=0)
 
 
 def struct(*shape):
@@ -536,11 +544,15 @@
     return lax.ppermute(x, "core", [(0, 1), (1, 0)])
 
 
-def pair_sum(x):
-    def others(x, masks):
-        return [lax.ppermute(x, "pair", [(i, i ^ d) for i in range(16)]) for d in masks]
-
-    x = x + sum(others(x, (1, 2, 3)))
+def others(x, masks):
+    return [lax.ppermute(x, "pair", [(i, i ^ d) for i in range(16)]) for d in masks]
+
+
+def stage_sum(x):
+    return x + sum(others(x, (1, 2, 3)))
+
+
+def stage_terms(x):
     return [x] + others(x, (4, 8, 12))
 
 
@@ -585,16 +597,22 @@
             )
         )
     )
-    low_m, high_m = moved(packed, "pair", 1), moved(packed, "pair", -1)
+    space, last = ("pair", "core"), 2 * pairs
+    inward = [(i, i - 2) for i in range(2, last, 2)] + [(i, i + 2) for i in range(1, last - 2, 2)]
+    outward = [(i, i + 2) for i in range(0, last - 2, 2)] + [(i, i - 2) for i in range(3, last, 2)]
+    touch_m = lax.ppermute(packed, space, inward)
+    beyond_m = lax.ppermute(packed, space, outward)
     own_t = swapped(packed)
 
     block, near_block = (4, ROWS, 128), (5, ROWS, 128)
     count, near_count = (4, LINES, 128), (5, LINES, 128)
-    own = scatter(scatter_own_kernel, "scatter_own", 5, (lists,), [block, block, count])
-    b_own, ob_own, cn_own, first = scatter(
-        scatter_other_kernel, "scatter_other", 5, (packed, own_t), [block, block, count, (LIST, 128)], own
+    *own, first = scatter(
+        scatter_other_kernel, "scatter_other", 5, (packed, own_t), [block, block, count, (LIST, 128)]
     )
     far_m = moved(first, "pair", -2)
+    b_own, ob_own, cn_own = scatter(
+        scatter_own_kernel, "scatter_own", 5, (lists, first), [block, block, count], own
+    )
     inv, v0, v1, held = pl.pallas_call(
         forward_own_kernel,
         out_shape=(
@@ -607,16 +625,15 @@
         cost_estimate=cost(4),
         name="forward_own",
     )(damping, packed, own_t, b_own)
-    low_m, high_m, far_m, held = lax.optimization_barrier((low_m, high_m, far_m, held))
-    near_t = swapped(jnp.concatenate([low_m, high_m]))
-    b_near, ob_near, cn_near = scatter(
-        scatter_mine_kernel, "scatter_mine", 6, (low_m, high_m),
-        [(9, ROWS, 128), near_block, near_count],
-    )
-    near_t, b_near = lax.optimization_barrier((near_t, b_near))
+    touch_m, beyond_m, far_m, held = lax.optimization_barrier((touch_m, beyond_m, far_m, held))
+    touch_t, beyond_t = swapped(touch_m), swapped(beyond_m)
+    near_shape = [(9, ROWS, 128)]
     b_near, = scatter(
-        scatter_theirs_kernel, "scatter_theirs", 5, (damping, far_m, near_t), [(9, ROWS, 128)],
-        (b_near,),
+        scatter_mine_kernel, "scatter_mine", 4, (damping, touch_m, beyond_m, far_m), near_shape
+    )
+    touch_t, beyond_t, b_near = lax.optimization_barrier((touch_t, beyond_t, b_near))
+    b_near, = scatter(
+        scatter_theirs_kernel, "scatter_theirs", 3, (touch_t, beyond_t), near_shape, (b_near,)
     )
 
     inv, v0, v1, v2, msg = pl.pallas_call(
@@ -625,18 +642,21 @@
             struct(PLANES, ROWS, 128), struct(13, ROWS, 128), struct(11, ROWS, 128),
             struct(9, ROWS, 128), struct(8, 128),
         ),
-        in_specs=[SMEM] + [VMEM] * 8,
+        in_specs=[SMEM] + [VMEM] * 9,
         out_specs=(VMEM,) * 5,
-        input_output_aliases={6: 0, 7: 1, 8: 2},
+        input_output_aliases={7: 0, 8: 1, 9: 2},
         compiler_params=params(2),
         cost_estimate=cost(20),
         name="forward",
-    )(damping, low_m, high_m, near_t, b_near, held, inv, v0, v1)
-
-    near_t, msg = lax.optimization_barrier((near_t, msg))
+    )(damping, touch_m, touch_t, beyond_m, beyond_t, b_near, held, inv, v0, v1)
+
+    touch_m, msg = lax.optimization_barrier((touch_m, msg))
+    near = scatter(scatter_later_kernel, "scatter_later", 3, (touch_m,), [near_block, near_count])
+    half_sum = stage_sum(msg)
+    half_sum, near, touch_t = lax.optimization_barrier((half_sum, near, touch_t))
     ob_near, cn_near = scatter(
-        scatter_late_kernel, "scatter_late", 5, (high_m, near_t), [near_block, near_count],
-        (ob_near, cn_near),
+        scatter_late_kernel, "scatter_late", 4, (touch_t, beyond_m, beyond_t),
+        [near_block, near_count], near,
     )
     wave, u0, u1, u2, msg = pl.pallas_call(
         adjoint_kernel,
@@ -650,9 +670,9 @@
         compiler_params=params(2),
         cost_estimate=cost(14),
         name="adjoint",
-    )(*pair_sum(msg), inv, v0, v1, v2, ob_own, cn_own, ob_near, cn_near)
-
-    terms = pair_sum(msg)
+    )(*stage_terms(half_sum), inv, v0, v1, v2, ob_own, cn_own, ob_near, cn_near)
+
+    terms = stage_terms(stage_sum(msg))
 
     def gradient(other, *more):
         scratch = [] if other else [pltpu.VMEM((4, 2, 128, 128), jnp.float32)]
@@ -667,8 +687,8 @@
         )(damping, *terms, wave, u0, u1, u2, *more)
 
     given = gradient(True)
-    slowness, dual, own_t, near_t, given = lax.optimization_barrier(
-        (slowness, dual, own_t, near_t, given)
+    slowness, dual, own_t, touch_t, given = lax.optimization_barrier(
+        (slowness, dual, own_t, touch_t, given)
     )
     dual_next, base, send_x, send_y = pl.pallas_call(
         variation_kernel,
@@ -680,7 +700,7 @@
         compiler_params=params(8),
         cost_estimate=cost(1),
         name="variation",
-    )(slowness, own_t, near_t, dual)
+    )(slowness, own_t, touch_t, dual)
     bands = gradient(False, swapped(given), send_y)
     send_x, bands = lax.optimization_barrier((send_x, bands))
     arrived = [bands[0]] + [

time: 114 us -> 109 us (0.956)
  waiting for transfers between devices: 22.6 us -> 18.3 us
    ppermute x0 -> x2, starting transfers between devices: none -> 5.57 us  [the longest x1 4.29 us: on_device(): touch_m = lax.ppermute(packed, space, inward)]
    ppermute x4 -> x2, starting transfers between devices: 9.87 us -> 4.85 us  [moved(): lax.ppermute(x, axis, [(i, i + by) for i in range(peers) if 0 <= i + by <...]
    ppermute x12, waiting for transfers between devices: 9.47 us -> 6.44 us  [others(): lax.ppermute(x, 'pair', [(i, i ^ d) for i in range(16)])]
    ppermute x4 -> x2, waiting for transfers between devices: 8.23 us -> 6.02 us  [moved(): lax.ppermute(x, axis, [(i, i + by) for i in range(peers) if 0 <= i + by <...]
    ppermute x0 -> x2, waiting for transfers between devices: none -> 1.44 us  [the longest x1 1.43 us: on_device(): touch_m = lax.ppermute(packed, space, inward)]
    pallas_call x5 -> x6, Pallas kernels: 14.4 us -> 14.6 us  [scatter(): pl.pallas_call(kernel, out_shape=tuple((struct(*shape) for shape in shape...]
    ppermute x3 -> x4, starting transfers between devices: 8.41 us -> 8.6 us  [swapped(): return lax.ppermute(x, 'core', [(0, 1), (1, 0)])]
  transfers between devices with their start and end apart: 22 -> 23, of which waited for: 14 -> 13; matrix products, arithmetic and copies ran while one was open for 0% -> 0% of each run, Pallas kernels for 13% -> 14%
where the time goes in v4:
time: 109 us
  Pallas kernels  38.8 us (36%)
  starting transfers between devices  36.4 us (33%)
  waiting for transfers between devices  18.3 us (17%)
  blocking collectives  14.5 us (13%)
    pallas_call x6, Pallas kernels, scatter(): pl.pallas_call(kernel, out_shape=tuple((struct(*shape) for shape in shape...  14.6 us
    all_to_all x1, blocking collectives, on_device(): power = lax.all_to_all(power, ('lap', 'pair', 'core'), 0, 0, tiled=True)  14.5 us
    ppermute x12, starting transfers between devices, others(): lax.ppermute(x, 'pair', [(i, i ^ d) for i in range(16)])  13.4 us
    ppermute x4, starting transfers between devices, swapped(): return lax.ppermute(x, 'core', [(0, 1), (1, 0)])  8.6 us
    pallas_call x1, Pallas kernels, on_device(): pl.pallas_call(forward_kernel, out_shape=(struct(PLANES, ROWS, 128), stru...  8.28 us
    pallas_call x1, Pallas kernels, on_device(): pl.pallas_call(adjoint_kernel, out_shape=(struct(4, ROWS, 128), struct(13...  8.14 us
    ppermute x12, waiting for transfers between devices, others(): lax.ppermute(x, 'pair', [(i, i ^ d) for i in range(16)])  6.44 us
    ppermute x2, waiting for transfers between devices, moved(): lax.ppermute(x, axis, [(i, i + by) for i in range(peers) if 0 <= i + by <...  6.02 us
  transfers between devices with their start and end apart: 23, of which 13 were waited for; matrix products, arithmetic and copies ran while one was open for 0% of the time, Pallas kernels for 14%

profile of v4, /device:TPU:1, one launch (start us, length us, event | category | flops | bytes accessed | tf_op | source)
XLA Modules:
  0.0 108.9 jit_solution(4271239915208576681)
XLA Ops:
  0.6 1.4 %pack.1 = (f32[1112,128]{1,0:T(8,128)S(1)}, f32[88,128]{1,0:T(8,128)S(1)}) custom-call(f32[1024,128]{1,0:T(8,128)} %bitcast.7, s32[8,128]{1,0:T(8,128)} %bitcast.10, s32[8,128]{1,0:T(8,128)} %bitcast.11, f32[4,1024]{1,0:T(4,128)} %amp_in.1, f32[4,1024]{1,0:T(4,128)} %obs_in.1), custom_call_target="tpu_custom_call" | custom-call | tf_op jit(solution)/shard_map/pack/pallas_call | solution.py:579
  2.0 1.5 %collective-permute-start = (f32[1112,128]{1,0:T(8,128)S(1)}, f32[1112,128]{1,0:T(8,128)S(1)}, u32[]{:S(2)}, u32[]{:S(2)}) collective-permute-start(f32[1112,128]{1,0:T(8,128)S(1)} %get-tuple-element.68.mine.own_m), channel_id=1, source_target_pairs={{0,1},{1,0},{2,3},{3,2},{4,5},{5,4},{6,7},{7,6},{8,9},{9,8},{10,11... | collective-permute-start | bytes 1708040 | tf_op jit(solution)/shard_map/ppermute | solution.py:544
  3.5 1.3 %collective-permute-start.2 = (f32[1112,128]{1,0:T(8,128)S(1)}, f32[1112,128]{1,0:T(8,128)S(1)}, u32[]{:S(2)}, u32[]{:S(2)}) collective-permute-start(f32[1112,128]{1,0:T(8,128)S(1)} %get-tuple-element.68.mine.own_m), channel_id=1, source_target_pairs={{0,2},{2,4},{4,6},{6,8},{8,10},{10,12},{12,14},{14,16},{16,18},{18... | collective-permute-start | bytes 1708040 | tf_op jit(solution)/shard_map/ppermute | solution.py:604
  4.8 4.3 %collective-permute-start.1 = (f32[1112,128]{1,0:T(8,128)S(1)}, f32[1112,128]{1,0:T(8,128)S(1)}, u32[]{:S(2)}, u32[]{:S(2)}) collective-permute-start(f32[1112,128]{1,0:T(8,128)S(1)} %get-tuple-element.68.mine.own_m), channel_id=1, source_target_pairs={{2,0},{4,2},{6,4},{8,6},{10,8},{12,10},{14,12},{16,14},{18,16},{20... | collective-permute-start | bytes 1708040 | tf_op jit(solution)/shard_map/ppermute | solution.py:603
  9.1 3.8 %scatter_other.1 = (f32[4,1024,128]{2,1,0:T(8,128)S(1)}, f32[4,1024,128]{2,1,0:T(8,128)S(1)}, f32[4,512,128]{2,1,0:T(8,128)S(1)}, f32[88,128]{1,0:T(8,128)S(1)}) custom-call(f32[1112,128]{1,0:T(8,128)S(1)} %get-tuple-element.68.mine.own_m, f32[1112,128]{1,0:T(8,128)S(1)} %collective-permute-done.other.own_t), custom_call_target="tpu_custom_call" | custom-call | flops 50000000 | bytes 10000 | tf_op jit(solution)/shard_map/scatter_other/pallas_call | solution.py:562
  12.9 1.3 %collective-permute-start.3 = (f32[88,128]{1,0:T(8,128)S(1)}, f32[88,128]{1,0:T(8,128)S(1)}, u32[]{:S(2)}, u32[]{:S(2)}) collective-permute-start(f32[88,128]{1,0:T(8,128)S(1)} %get-tuple-element.69.first_in), channel_id=1, source_target_pairs={{4,0},{6,2},{8,4},{10,6},{12,8},{14,10},{16,12},{18,14},{20,16},{2... | collective-permute-start | bytes 135176 | tf_op jit(solution)/shard_map/ppermute | solution.py:540
  14.2 2.7 %scatter_own.1 = (f32[4,1024,128]{2,1,0:T(8,128)S(1)}, f32[4,1024,128]{2,1,0:T(8,128)S(1)}, f32[4,512,128]{2,1,0:T(8,128)S(1)}) custom-call(f32[88,128]{1,0:T(8,128)S(1)} %get-tuple-element.70.lists, f32[88,128]{1,0:T(8,128)S(1)} %get-tuple-element.69.first_in, ...), custom_call_target="tpu_custom_call", output_to_operand_aliasing={{0}: (2, {}), {1}: (3, {}), {2}: (4, {})} | custom-call | flops 50000000 | bytes 10000 | tf_op jit(solution)/shard_map/scatter_own/pallas_call | solution.py:562
  16.9 2.0 %forward_own.1 = (f32[13,1024,128]{2,1,0:T(8,128)S(1)}, f32[13,1024,128]{2,1,0:T(8,128)S(1)}, f32[11,1024,128]{2,1,0:T(8,128)S(1)}, f32[48,128]{1,0:T(8,128)S(1)}) custom-call(f32[4]{0:T(128)S(1)} %copy-done.2, f32[1112,128]{1,0:T(8,128)S(1)} %get-tuple-element.68.mine.own_m, f32[1112,128]{1,0:T(8,128)S(1)} %collective-permute-done.other.own_t, ...), custom_call_target="tpu_custom_call" | custom-call | flops 40000000 | bytes 10000 | tf_op jit(solution)/shard_map/forward_own/pallas_call | solution.py:616
  18.9 1.4 %collective-permute-done.1.touch.touch_m.mine = f32[1112,128]{1,0:T(8,128)S(1)} collective-permute-done((f32[1112,128]{1,0:T(8,128)S(1)}, f32[1112,128]{1,0:T(8,128)S(1)}, u32[]{:S(2)}, u32[]{:S(2)}) %collective-permute-start.1) | collective-permute-done | bytes 569376 | tf_op jit(solution)/shard_map/ppermute | solution.py:603
  20.3 4.7 %collective-permute-done.3.far = f32[88,128]{1,0:T(8,128)S(1)} collective-permute-done((f32[88,128]{1,0:T(8,128)S(1)}, f32[88,128]{1,0:T(8,128)S(1)}, u32[]{:S(2)}, u32[]{:S(2)}) %collective-permute-start.3) | collective-permute-done | bytes 45088 | tf_op jit(solution)/shard_map/ppermute | solution.py:540
  25.1 0.5 collective-permute-start.5
  25.6 2.7 %scatter_mine.1.b_in = f32[9,1024,128]{2,1,0:T(8,128)S(1)} custom-call(f32[4]{0:T(128)S(1)} %copy-done.2, f32[1112,128]{1,0:T(8,128)S(1)} %collective-permute-done.1.touch.touch_m.mine, f32[1112,128]{1,0:T(8,128)S(1)} %collective-permute-done.2.beyond.beyond_m, f32[88,128]{1,0:T(8,128)S(1)} %collective-permute-done.3.far), custom_call_target="tpu_custom_call" | custom-call | flops 40000000 | bytes 10000 | tf_op jit(solution)/shard_map/scatter_mine/pallas_call | solution.py:562
  28.3 1.9 %scatter_theirs.1.b_near = f32[9,1024,128]{2,1,0:T(8,128)S(1)} custom-call(f32[1112,128]{1,0:T(8,128)S(1)} %collective-permute-done.4.touch.touch_t.theirs, f32[1112,128]{1,0:T(8,128)S(1)} %collective-permute-done.5.beyond.beyond_t, f32[9,1024,128]{2,1,0:T(8,128)S(1)} %scatter_mine.1.b_in), custom_call_target="tpu_custom_call", output_to_operand_aliasing={{}: (2, {})} | custom-call | flops 30000000 | bytes 10000 | tf_op jit(solution)/shard_map/scatter_theirs/pallas_call | solution.py:562
  30.2 8.3 %forward.1 = (f32[13,1024,128]{2,1,0:T(8,128)S(1)}, f32[13,1024,128]{2,1,0:T(8,128)S(1)}, f32[11,1024,128]{2,1,0:T(8,128)S(1)}, f32[9,1024,128]{2,1,0:T(8,128)S(1)}, f32[8,128]{1,0:T(8,128)S(1)}) custom-call(f32[4]{0:T(128)S(1)} %copy-done.2, ...), custom_call_target="tpu_custom_call", output_to_operand_aliasing={{0}: (7, {}), {1}: (8, {}), {2}: (9, {})} | custom-call | flops 200000000 | bytes 10000 | tf_op jit(solution)/shard_map/forward/pallas_call | solution.py:639
  38.4 2.6 %collective-permute-start.8 = (f32[8,128]{1,0:T(8,128)S(1)}, f32[8,128]{1,0:T(8,128)S(1)}, u32[]{:S(2)}, u32[]{:S(2)}) collective-permute-start(f32[8,128]{1,0:T(8,128)S(1)} %get-tuple-element.87), channel_id=1, source_target_pairs={{0,6},{2,4},{4,2},{6,0},{8,14},{10,12},{12,10},{14,8},{16,22},{18,... | collective-permute-start | bytes 12296 | tf_op jit(solution)/shard_map/ppermute | solution.py:548
  41.1 0.8 collective-permute-start.7
  41.9 1.6 %scatter_later.1 = (f32[5,1024,128]{2,1,0:T(8,128)S(1)}, f32[5,512,128]{2,1,0:T(8,128)S(1)}) custom-call(f32[1112,128]{1,0:T(8,128)S(1)} %collective-permute-done.1.touch.touch_m.mine), custom_call_target="tpu_custom_call" | custom-call | flops 30000000 | bytes 10000 | tf_op jit(solution)/shard_map/scatter_later/pallas_call | solution.py:562
  43.5 1.5 %collective-permute-done.7 = f32[8,128]{1,0:T(8,128)S(1)} collective-permute-done((f32[8,128]{1,0:T(8,128)S(1)}, f32[8,128]{1,0:T(8,128)S(1)}, u32[]{:S(2)}, u32[]{:S(2)}) %collective-permute-start.7) | collective-permute-done | bytes 4128 | tf_op jit(solution)/shard_map/ppermute | solution.py:548
  45.0 1.4 %collective-permute-start.11 = (f32[8,128]{1,0:T(8,128)S(1)}, f32[8,128]{1,0:T(8,128)S(1)}, u32[]{:S(2)}, u32[]{:S(2)}) collective-permute-start(f32[8,128]{1,0:T(8,128)S(1)} %add_add_fusion.1.t0), channel_id=1, source_target_pairs={{0,24},{2,26},{4,28},{6,30},{8,16},{10,18},{12,20},{14,22},{16,8},... | collective-permute-start | bytes 12296 | tf_op jit(solution)/shard_map/ppermute | solution.py:548
  46.5 1.7 %collective-permute-start.10 = (f32[8,128]{1,0:T(8,128)S(1)}, f32[8,128]{1,0:T(8,128)S(1)}, u32[]{:S(2)}, u32[]{:S(2)}) collective-permute-start(f32[8,128]{1,0:T(8,128)S(1)} %add_add_fusion.1.t0), channel_id=1, source_target_pairs={{0,16},{2,18},{4,20},{6,22},{8,24},{10,26},{12,28},{14,30},{16,0},... | collective-permute-start | bytes 12296 | tf_op jit(solution)/shard_map/ppermute | solution.py:548
  48.4 2.0 %scatter_late.1 = (f32[5,1024,128]{2,1,0:T(8,128)S(1)}, f32[5,512,128]{2,1,0:T(8,128)S(1)}) custom-call(f32[1112,128]{1,0:T(8,128)S(1)} %collective-permute-done.4.touch.touch_t.theirs, f32[1112,128]{1,0:T(8,128)S(1)} %collective-permute-done.2.beyond.beyond_m, ...), custom_call_target="tpu_custom_call", output_to_operand_aliasing={{0}: (3, {}), {1}: (4, {})} | custom-call | flops 40000000 | bytes 10000 | tf_op jit(solution)/shard_map/scatter_late/pallas_call | solution.py:562
  50.5 0.5 collective-permute-done.9.t1
  51.0 8.1 %adjoint.1 = (f32[4,1024,128]{2,1,0:T(8,128)S(1)}, f32[13,1024,128]{2,1,0:T(8,128)S(1)}, f32[11,1024,128]{2,1,0:T(8,128)S(1)}, f32[9,1024,128]{2,1,0:T(8,128)S(1)}, f32[8,128]{1,0:T(8,128)S(1)}) custom-call(f32[8,128]{1,0:T(8,128)S(1)} %add_add_fusion.1.t0, ...), custom_call_target="tpu_custom_call", output_to_operand_aliasing={{1}: (5, {}), {2}: (6, {}), {3}: (7, {})} | custom-call | flops 140000000 | bytes 10000 | tf_op jit(solution)/shard_map/adjoint/pallas_call | solution.py:661
  59.1 1.1 collective-permute-start.14
  60.2 1.2 %collective-permute-start.13 = (f32[8,128]{1,0:T(8,128)S(1)}, f32[8,128]{1,0:T(8,128)S(1)}, u32[]{:S(2)}, u32[]{:S(2)}) collective-permute-start(f32[8,128]{1,0:T(8,128)S(1)} %get-tuple-element.103), channel_id=1, source_target_pairs={{0,4},{2,6},{4,0},{6,2},{8,12},{10,14},{12,8},{14,10},{16,20},{18,... | collective-permute-start | bytes 12296 | tf_op jit(solution)/shard_map/ppermute | solution.py:548
  61.4 1.1 collective-permute-start.12
  62.4 0.4 collective-permute-done.14
  62.9 1.3 %collective-permute-done.13 = f32[8,128]{1,0:T(8,128)S(1)} collective-permute-done((f32[8,128]{1,0:T(8,128)S(1)}, f32[8,128]{1,0:T(8,128)S(1)}, u32[]{:S(2)}, u32[]{:S(2)}) %collective-permute-start.13) | collective-permute-done | bytes 4128 | tf_op jit(solution)/shard_map/ppermute | solution.py:548
  64.2 2.0 %collective-permute-start.17 = (f32[8,128]{1,0:T(8,128)S(1)}, f32[8,128]{1,0:T(8,128)S(1)}, u32[]{:S(2)}, u32[]{:S(2)}) collective-permute-start(f32[8,128]{1,0:T(8,128)S(1)} %add_add_fusion.t0), channel_id=1, source_target_pairs={{0,24},{2,26},{4,28},{6,30},{8,16},{10,18},{12,20},{14,22},{16,8},... | collective-permute-start | bytes 12296 | tf_op jit(solution)/shard_map/ppermute | solution.py:548
  66.1 0.9 collective-permute-start.16
  67.0 0.5 collective-permute-start.15
  67.5 0.4 collective-permute-done.17.t3
  67.9 2.2 %collective-permute-done.16.t2 = f32[8,128]{1,0:T(8,128)S(1)} collective-permute-done((f32[8,128]{1,0:T(8,128)S(1)}, f32[8,128]{1,0:T(8,128)S(1)}, u32[]{:S(2)}, u32[]{:S(2)}) %collective-permute-start.16) | collective-permute-done | bytes 4128 | tf_op jit(solution)/shard_map/ppermute | solution.py:548
  70.1 1.2 %gradient.2 = f32[4,2,128,128]{3,2,1,0:T(8,128)S(1)} custom-call(f32[4]{0:T(128)S(1)} %copy-done.2, f32[8,128]{1,0:T(8,128)S(1)} %add_add_fusion.t0, f32[8,128]{1,0:T(8,128)S(1)} %collective-permute-done.15.t1, f32[8,128]{1,0:T(8,128)S(1)} %collective-permute-done.16.t2, f32[8,128]{1,0:T(8,128)S(1)} %collective-permute-done.17.t3, ...), custom_call_target="tpu_custom_call" | custom-call | tf_op jit(solution)/shard_map/gradient/pallas_call | solution.py:679
  71.3 6.6 %collective-permute-start.18 = (f32[4,2,128,128]{3,2,1,0:T(8,128)S(1)}, f32[4,2,128,128]{3,2,1,0:T(8,128)S(1)}, u32[]{:S(2)}, u32[]{:S(2)}) collective-permute-start(f32[4,2,128,128]{3,2,1,0:T(8,128)S(1)} %gradient.2), channel_id=1, source_target_pairs={{0,1},{1,0},{2,3},{3,2},{4,5},{5,4},{6,7},{7,6},{8,9},{9,8},{10,11... | collective-permute-start | bytes 1572872 | tf_op jit(solution)/shard_map/ppermute | solution.py:544
  77.9 1.0 variation.1
  78.9 0.5 collective-permute-done.18.rest_0_
  79.5 1.3 %gradient.3 = (f32[2,136,128]{2,1,0:T(8,128)S(1)}, f32[2,136,128]{2,1,0:T(8,128)S(1)}, f32[2,136,128]{2,1,0:T(8,128)S(1)}, f32[2,136,128]{2,1,0:T(8,128)S(1)}) custom-call(f32[4]{0:T(128)S(1)} %copy-done.2, f32[8,128]{1,0:T(8,128)S(1)} %add_add_fusion.t0, f32[8,128]{1,0:T(8,128)S(1)} %collective-permute-done.15.t1, f32[8,128]{1,0:T(8,128)S(1)} %collective-permute-done.16.t2, ...), custom_call_target="tpu_custom_call" | custom-call | tf_op jit(solution)/shard_map/gradient/pallas_call | solution.py:679
  80.8 1.3 %collective-permute-start.19 = (f32[2,136,128]{2,1,0:T(8,128)S(1)}, f32[2,136,128]{2,1,0:T(8,128)S(1)}, u32[]{:S(2)}, u32[]{:S(2)}) collective-permute-start(f32[2,136,128]{2,1,0:T(8,128)S(1)} %get-tuple-element.121), channel_id=1, source_target_pairs={{0,32},{32,0},{64,96},{96,64},{1,33},{33,1},{65,97},{97,65},{2,34}... | collective-permute-start | bytes 417800 | tf_op jit(solution)/shard_map/ppermute | solution.py:707
  82.1 2.5 %collective-permute-start.20 = (f32[2,136,128]{2,1,0:T(8,128)S(1)}, f32[2,136,128]{2,1,0:T(8,128)S(1)}, u32[]{:S(2)}, u32[]{:S(2)}) collective-permute-start(f32[2,136,128]{2,1,0:T(8,128)S(1)} %get-tuple-element.122), channel_id=1, source_target_pairs={{0,64},{32,96},{64,0},{96,32},{1,65},{33,97},{65,1},{97,33},{2,66}... | collective-permute-start | bytes 417800 | tf_op jit(solution)/shard_map/ppermute | solution.py:707
  84.5 0.2 collective-permute-start.21
  84.7 3.6 %collective-permute-start.22 = (f32[1,128,128]{2,1,0:T(8,128)S(1)}, f32[1,128,128]{2,1,0:T(8,128)S(1)}, u32[]{:S(2)}, u32[]{:S(2)}) collective-permute-start(f32[1,128,128]{2,1,0:T(8,128)S(1)} %get-tuple-element.124), channel_id=1, source_target_pairs={{0,1},{1,2},{2,3},{3,4},{4,5},{5,6},{6,7},{7,8},{8,9},{9,10},{10,1... | collective-permute-start | bytes 196616 | tf_op jit(solution)/shard_map/ppermute | solution.py:540
  88.3 1.3 %collective-permute-done.22.prior_x = f32[1,128,128]{2,1,0:T(8,128)S(1)} collective-permute-done((f32[1,128,128]{2,1,0:T(8,128)S(1)}, f32[1,128,128]{2,1,0:T(8,128)S(1)}, u32[]{:S(2)}, u32[]{:S(2)}) %collective-permute-start.22) | collective-permute-done | bytes 65568 | tf_op jit(solution)/shard_map/ppermute | solution.py:540
  89.6 1.4 %collective-permute-done.20.g2 = f32[2,136,128]{2,1,0:T(8,128)S(1)} collective-permute-done((f32[2,136,128]{2,1,0:T(8,128)S(1)}, f32[2,136,128]{2,1,0:T(8,128)S(1)}, u32[]{:S(2)}, u32[]{:S(2)}) %collective-permute-start.20) | collective-permute-done | bytes 139296 | tf_op jit(solution)/shard_map/ppermute | solution.py:707
  91.0 2.5 %collective-permute-done.21.g3 = f32[2,136,128]{2,1,0:T(8,128)S(1)} collective-permute-done((f32[2,136,128]{2,1,0:T(8,128)S(1)}, f32[2,136,128]{2,1,0:T(8,128)S(1)}, u32[]{:S(2)}, u32[]{:S(2)}) %collective-permute-start.21) | collective-permute-done | bytes 139296 | tf_op jit(solution)/shard_map/ppermute | solution.py:707
  93.5 0.2 power.1
  93.7 14.5 %all_to_all.9 = f32[128,1,128]{2,1,0:T(1,128)S(1)} all-to-all(f32[128,1,128]{2,1,0:T(1,128)S(1)} %bitcast.9), channel_id=1, replica_groups=mesh['lap'=4,'pair'=16,'core'=2] {'lap','pair','core'}, dimensions={0} | all-to-all | bytes 131072 | tf_op jit(solution)/shard_map/all_to_all | solution.py:719
  108.2 0.7 model.1
  (22 shorter events, 0.3 us)
Async XLA Ops:
  0.6 16.3 %copy-start.2 = (f32[4]{0:T(128)S(1)}, f32[4]{0:T(128)}, u32[]{:S(2)}) copy-start(f32[4]{0:T(128)} %damp.9) | copy-start | bytes 52
  2.0 7.1 %collective-permute-start = (f32[1112,128]{1,0:T(8,128)S(1)}, f32[1112,128]{1,0:T(8,128)S(1)}, u32[]{:S(2)}, u32[]{:S(2)}) collective-permute-start(f32[1112,128]{1,0:T(8,128)S(1)} %get-tuple-element.68.mine.own_m), channel_id=1, source_target_pairs={{0,1},{1,0},{2,3},{3,2},{4,5},{5,4},{6,7},{7,6},{8,9},{9,8},{10,11... | collective-permute-start | bytes 1708040 | tf_op jit(solution)/shard_map/ppermute | solution.py:544
  3.5 15.4 %collective-permute-start.2 = (f32[1112,128]{1,0:T(8,128)S(1)}, f32[1112,128]{1,0:T(8,128)S(1)}, u32[]{:S(2)}, u32[]{:S(2)}) collective-permute-start(f32[1112,128]{1,0:T(8,128)S(1)} %get-tuple-element.68.mine.own_m), channel_id=1, source_target_pairs={{0,2},{2,4},{4,6},{6,8},{8,10},{10,12},{12,14},{14,16},{16,18},{18... | collective-permute-start | bytes 1708040 | tf_op jit(solution)/shard_map/ppermute | solution.py:604
  4.8 15.5 %collective-permute-start.1 = (f32[1112,128]{1,0:T(8,128)S(1)}, f32[1112,128]{1,0:T(8,128)S(1)}, u32[]{:S(2)}, u32[]{:S(2)}) collective-permute-start(f32[1112,128]{1,0:T(8,128)S(1)} %get-tuple-element.68.mine.own_m), channel_id=1, source_target_pairs={{2,0},{4,2},{6,4},{8,6},{10,8},{12,10},{14,12},{16,14},{18,16},{20... | collective-permute-start | bytes 1708040 | tf_op jit(solution)/shard_map/ppermute | solution.py:603
  12.9 12.1 %collective-permute-start.3 = (f32[88,128]{1,0:T(8,128)S(1)}, f32[88,128]{1,0:T(8,128)S(1)}, u32[]{:S(2)}, u32[]{:S(2)}) collective-permute-start(f32[88,128]{1,0:T(8,128)S(1)} %get-tuple-element.69.first_in), channel_id=1, source_target_pairs={{4,0},{6,2},{8,4},{10,6},{12,8},{14,10},{16,12},{18,14},{20,16},{2... | collective-permute-start | bytes 135176 | tf_op jit(solution)/shard_map/ppermute | solution.py:540
  25.1 3.2 %collective-permute-start.4 = (f32[1112,128]{1,0:T(8,128)S(1)}, f32[1112,128]{1,0:T(8,128)S(1)}, u32[]{:S(2)}, u32[]{:S(2)}) collective-permute-start(f32[1112,128]{1,0:T(8,128)S(1)} %collective-permute-done.1.touch.touch_m.mine), channel_id=1, source_target_pairs={{0,1},{1,0},{2,3},{3,2},{4,5},{5,4},{6,7},{7,6},{8,9},{9,8},{10,11... | collective-permute-start | bytes 1708040 | tf_op jit(solution)/shard_map/ppermute | solution.py:544
  25.1 3.2 %collective-permute-start.5 = (f32[1112,128]{1,0:T(8,128)S(1)}, f32[1112,128]{1,0:T(8,128)S(1)}, u32[]{:S(2)}, u32[]{:S(2)}) collective-permute-start(f32[1112,128]{1,0:T(8,128)S(1)} %collective-permute-done.2.beyond.beyond_m), channel_id=1, source_target_pairs={{0,1},{1,0},{2,3},{3,2},{4,5},{5,4},{6,7},{7,6},{8,9},{9,8},{10,11... | collective-permute-start | bytes 1708040 | tf_op jit(solution)/shard_map/ppermute | solution.py:544
  38.4 5.0 %collective-permute-start.8 = (f32[8,128]{1,0:T(8,128)S(1)}, f32[8,128]{1,0:T(8,128)S(1)}, u32[]{:S(2)}, u32[]{:S(2)}) collective-permute-start(f32[8,128]{1,0:T(8,128)S(1)} %get-tuple-element.87), channel_id=1, source_target_pairs={{0,6},{2,4},{4,2},{6,0},{8,14},{10,12},{12,10},{14,8},{16,22},{18,... | collective-permute-start | bytes 12296 | tf_op jit(solution)/shard_map/ppermute | solution.py:548
  41.1 4.0 %collective-permute-start.7 = (f32[8,128]{1,0:T(8,128)S(1)}, f32[8,128]{1,0:T(8,128)S(1)}, u32[]{:S(2)}, u32[]{:S(2)}) collective-permute-start(f32[8,128]{1,0:T(8,128)S(1)} %get-tuple-element.87), channel_id=1, source_target_pairs={{0,4},{2,6},{4,0},{6,2},{8,12},{10,14},{12,8},{14,10},{16,20},{18,... | collective-permute-start | bytes 12296 | tf_op jit(solution)/shard_map/ppermute | solution.py:548
  41.9 3.2 %collective-permute-start.6 = (f32[8,128]{1,0:T(8,128)S(1)}, f32[8,128]{1,0:T(8,128)S(1)}, u32[]{:S(2)}, u32[]{:S(2)}) collective-permute-start(f32[8,128]{1,0:T(8,128)S(1)} %get-tuple-element.87), channel_id=1, source_target_pairs={{0,2},{2,0},{4,6},{6,4},{8,10},{10,8},{12,14},{14,12},{16,18},{18,... | collective-permute-start | bytes 12296 | tf_op jit(solution)/shard_map/ppermute | solution.py:548
  45.0 5.3 %collective-permute-start.11 = (f32[8,128]{1,0:T(8,128)S(1)}, f32[8,128]{1,0:T(8,128)S(1)}, u32[]{:S(2)}, u32[]{:S(2)}) collective-permute-start(f32[8,128]{1,0:T(8,128)S(1)} %add_add_fusion.1.t0), channel_id=1, source_target_pairs={{0,24},{2,26},{4,28},{6,30},{8,16},{10,18},{12,20},{14,22},{16,8},... | collective-permute-start | bytes 12296 | tf_op jit(solution)/shard_map/ppermute | solution.py:548
  46.5 4.0 %collective-permute-start.10 = (f32[8,128]{1,0:T(8,128)S(1)}, f32[8,128]{1,0:T(8,128)S(1)}, u32[]{:S(2)}, u32[]{:S(2)}) collective-permute-start(f32[8,128]{1,0:T(8,128)S(1)} %add_add_fusion.1.t0), channel_id=1, source_target_pairs={{0,16},{2,18},{4,20},{6,22},{8,24},{10,26},{12,28},{14,30},{16,0},... | collective-permute-start | bytes 12296 | tf_op jit(solution)/shard_map/ppermute | solution.py:548
  48.2 2.8 %collective-permute-start.9 = (f32[8,128]{1,0:T(8,128)S(1)}, f32[8,128]{1,0:T(8,128)S(1)}, u32[]{:S(2)}, u32[]{:S(2)}) collective-permute-start(f32[8,128]{1,0:T(8,128)S(1)} %add_add_fusion.1.t0), channel_id=1, source_target_pairs={{0,8},{2,10},{4,12},{6,14},{8,0},{10,2},{12,4},{14,6},{16,24},{18,... | collective-permute-start | bytes 12296 | tf_op jit(solution)/shard_map/ppermute | solution.py:548
  59.1 3.7 %collective-permute-start.14 = (f32[8,128]{1,0:T(8,128)S(1)}, f32[8,128]{1,0:T(8,128)S(1)}, u32[]{:S(2)}, u32[]{:S(2)}) collective-permute-start(f32[8,128]{1,0:T(8,128)S(1)} %get-tuple-element.103), channel_id=1, source_target_pairs={{0,6},{2,4},{4,2},{6,0},{8,14},{10,12},{12,10},{14,8},{16,22},{18,... | collective-permute-start | bytes 12296 | tf_op jit(solution)/shard_map/ppermute | solution.py:548
  60.2 4.0 %collective-permute-start.13 = (f32[8,128]{1,0:T(8,128)S(1)}, f32[8,128]{1,0:T(8,128)S(1)}, u32[]{:S(2)}, u32[]{:S(2)}) collective-permute-start(f32[8,128]{1,0:T(8,128)S(1)} %get-tuple-element.103), channel_id=1, source_target_pairs={{0,4},{2,6},{4,0},{6,2},{8,12},{10,14},{12,8},{14,10},{16,20},{18,... | collective-permute-start | bytes 12296 | tf_op jit(solution)/shard_map/ppermute | solution.py:548
  61.4 2.8 %collective-permute-start.12 = (f32[8,128]{1,0:T(8,128)S(1)}, f32[8,128]{1,0:T(8,128)S(1)}, u32[]{:S(2)}, u32[]{:S(2)}) collective-permute-start(f32[8,128]{1,0:T(8,128)S(1)} %get-tuple-element.103), channel_id=1, source_target_pairs={{0,2},{2,0},{4,6},{6,4},{8,10},{10,8},{12,14},{14,12},{16,18},{18,... | collective-permute-start | bytes 12296 | tf_op jit(solution)/shard_map/ppermute | solution.py:548
  64.2 3.7 %collective-permute-start.17 = (f32[8,128]{1,0:T(8,128)S(1)}, f32[8,128]{1,0:T(8,128)S(1)}, u32[]{:S(2)}, u32[]{:S(2)}) collective-permute-start(f32[8,128]{1,0:T(8,128)S(1)} %add_add_fusion.t0), channel_id=1, source_target_pairs={{0,24},{2,26},{4,28},{6,30},{8,16},{10,18},{12,20},{14,22},{16,8},... | collective-permute-start | bytes 12296 | tf_op jit(solution)/shard_map/ppermute | solution.py:548
  66.1 4.0 %collective-permute-start.16 = (f32[8,128]{1,0:T(8,128)S(1)}, f32[8,128]{1,0:T(8,128)S(1)}, u32[]{:S(2)}, u32[]{:S(2)}) collective-permute-start(f32[8,128]{1,0:T(8,128)S(1)} %add_add_fusion.t0), channel_id=1, source_target_pairs={{0,16},{2,18},{4,20},{6,22},{8,24},{10,26},{12,28},{14,30},{16,0},... | collective-permute-start | bytes 12296 | tf_op jit(solution)/shard_map/ppermute | solution.py:548
  67.0 3.1 %collective-permute-start.15 = (f32[8,128]{1,0:T(8,128)S(1)}, f32[8,128]{1,0:T(8,128)S(1)}, u32[]{:S(2)}, u32[]{:S(2)}) collective-permute-start(f32[8,128]{1,0:T(8,128)S(1)} %add_add_fusion.t0), channel_id=1, source_target_pairs={{0,8},{2,10},{4,12},{6,14},{8,0},{10,2},{12,4},{14,6},{16,24},{18,... | collective-permute-start | bytes 12296 | tf_op jit(solution)/shard_map/ppermute | solution.py:548
  70.1 7.9 %copy-start = (f32[2,512,128]{2,1,0:T(8,128)S(1)}, f32[2,512,128]{2,1,0:T(8,128)}, u32[]{:S(2)}) copy-start(f32[2,512,128]{2,1,0:T(8,128)} %slow) | copy-start | bytes 1572868
  70.1 7.9 %copy-start.1 = (f32[3,2,128,128]{3,2,1,0:T(8,128)S(1)}, f32[3,2,128,128]{3,2,1,0:T(8,128)}, u32[]{:S(2)}) copy-start(f32[3,2,128,128]{3,2,1,0:T(8,128)} %dual) | copy-start | bytes 1179652
  71.3 8.1 %collective-permute-start.18 = (f32[4,2,128,128]{3,2,1,0:T(8,128)S(1)}, f32[4,2,128,128]{3,2,1,0:T(8,128)S(1)}, u32[]{:S(2)}, u32[]{:S(2)}) collective-permute-start(f32[4,2,128,128]{3,2,1,0:T(8,128)S(1)} %gradient.2), channel_id=1, source_target_pairs={{0,1},{1,0},{2,3},{3,2},{4,5},{5,4},{6,7},{7,6},{8,9},{9,8},{10,11... | collective-permute-start | bytes 1572872 | tf_op jit(solution)/shard_map/ppermute | solution.py:544
  80.8 8.8 %collective-permute-start.19 = (f32[2,136,128]{2,1,0:T(8,128)S(1)}, f32[2,136,128]{2,1,0:T(8,128)S(1)}, u32[]{:S(2)}, u32[]{:S(2)}) collective-permute-start(f32[2,136,128]{2,1,0:T(8,128)S(1)} %get-tuple-element.121), channel_id=1, source_target_pairs={{0,32},{32,0},{64,96},{96,64},{1,33},{33,1},{65,97},{97,65},{2,34}... | collective-permute-start | bytes 417800 | tf_op jit(solution)/shard_map/ppermute | solution.py:707
  82.1 8.9 %collective-permute-start.20 = (f32[2,136,128]{2,1,0:T(8,128)S(1)}, f32[2,136,128]{2,1,0:T(8,128)S(1)}, u32[]{:S(2)}, u32[]{:S(2)}) collective-permute-start(f32[2,136,128]{2,1,0:T(8,128)S(1)} %get-tuple-element.122), channel_id=1, source_target_pairs={{0,64},{32,96},{64,0},{96,32},{1,65},{33,97},{65,1},{97,33},{2,66}... | collective-permute-start | bytes 417800 | tf_op jit(solution)/shard_map/ppermute | solution.py:707
  84.5 8.9 %collective-permute-start.21 = (f32[2,136,128]{2,1,0:T(8,128)S(1)}, f32[2,136,128]{2,1,0:T(8,128)S(1)}, u32[]{:S(2)}, u32[]{:S(2)}) collective-permute-start(f32[2,136,128]{2,1,0:T(8,128)S(1)} %get-tuple-element.123), channel_id=1, source_target_pairs={{0,96},{32,64},{64,32},{96,0},{1,97},{33,65},{65,33},{97,1},{2,98}... | collective-permute-start | bytes 417800 | tf_op jit(solution)/shard_map/ppermute | solution.py:707
  84.7 4.9 %collective-permute-start.22 = (f32[1,128,128]{2,1,0:T(8,128)S(1)}, f32[1,128,128]{2,1,0:T(8,128)S(1)}, u32[]{:S(2)}, u32[]{:S(2)}) collective-permute-start(f32[1,128,128]{2,1,0:T(8,128)S(1)} %get-tuple-element.124), channel_id=1, source_target_pairs={{0,1},{1,2},{2,3},{3,4},{4,5},{5,6},{6,7},{7,8},{8,9},{9,10},{10,1... | collective-permute-start | bytes 196616 | tf_op jit(solution)/shard_map/ppermute | solution.py:540

commit v5 on v4

--- a/solution.py
+++ b/solution.py
@@ -245,15 +245,15 @@
     return jnp.sum(x.reshape(LINES // 8, 8, 128), 0)
 
 
-def walk(first, last, body, carry):
-    return lax.fori_loop(first, last, body, carry)
+def walk(first, last, body, carry, unroll=False):
+    return lax.fori_loop(first, last, body, carry, unroll=unroll)
 
 
 def nothing():
     return [jnp.zeros((8, 128), jnp.float32) for _ in range(HALF)]
 
 
-def advance(src, s_off, inv, dst, d_off, first, last, dots):
+def advance(src, s_off, inv, dst, d_off, first, last, dots, unroll=False):
     def body(t, carry):
         one, two = [], []
         for c in range(HALF):
@@ -266,7 +266,7 @@
                 two.append(carry[1][c] + fold(new * q))
         return (one, two) if dots else carry
 
-    return walk(first, last, body, (nothing(), nothing()) if dots else 0)
+    return walk(first, last, body, (nothing(), nothing()) if dots else 0, unroll)
 
 
 def last_moment(src, off):
@@ -375,19 +375,19 @@
 
         return body
 
-    v0[12] = b_near[8]
+    v0[12] = b_near[8] * jnp.where(pair + 2 < lax.axis_size("pair"), 1.0, 0.0)
     walk(0, 4, start(0), 0)
     walk(8, 12, start(4), 0)
     kept = [held[8 * k : 8 * k + 8, :] for k in range(3 * HALF)]
-    advance(v0, 0, inv, v1, 1, 1, 4, False)
-    lower = advance(v0, 0, inv, v1, 1, 4, 5, True)
-    upper = advance(v0, 0, inv, v1, 1, 7, 8, True)
-    advance(v0, 0, inv, v1, 1, 8, 12, False)
+    advance(v0, 0, inv, v1, 1, 1, 4, False, True)
+    lower = advance(v0, 0, inv, v1, 1, 4, 5, True, True)
+    upper = advance(v0, 0, inv, v1, 1, 7, 8, True, True)
+    advance(v0, 0, inv, v1, 1, 8, 12, False, True)
     m1 = [a + b + c for a, b, c in zip(lower[0], upper[0], kept[HALF : 2 * HALF])]
     m2 = [a + b + c for a, b, c in zip(lower[1], upper[1], kept[2 * HALF :])]
-    advance(v1, 1, inv, v2, 2, 2, 4, False)
-    m3, m4 = advance(v1, 1, inv, v2, 2, 4, 8, True)
-    advance(v1, 1, inv, v2, 2, 8, 11, False)
+    advance(v1, 1, inv, v2, 2, 2, 4, False, True)
+    m3, m4 = advance(v1, 1, inv, v2, 2, 4, 8, True, True)
+    advance(v1, 1, inv, v2, 2, 8, 11, False, True)
     m5 = last_moment(v2, 2)
     msg[...] = message([kept[:HALF], m1, m2, m3, m4, m5])
 
@@ -418,11 +418,11 @@
     walk(2, 4, start(ob_near, cn_near, 2, False), 0)
     m0 = walk(4, 8, start(ob_own, cn_own, 4, True), nothing())
     walk(8, 11, start(ob_near, cn_near, 6, False), 0)
-    advance(u0, 0, inv, u1, 1, 3, 4, False)
-    m1, m2 = advance(u0, 0, inv, u1, 1, 4, 8, True)
-    advance(u0, 0, inv, u1, 1, 8, 10, False)
-    m3, m4 = advance(u1, 1, inv, u2, 2, 4, 8, True)
-    advance(u1, 1, inv, u2, 2, 8, 9, False)
+    advance(u0, 0, inv, u1, 1, 3, 4, False, True)
+    m1, m2 = advance(u0, 0, inv, u1, 1, 4, 8, True, True)
+    advance(u0, 0, inv, u1, 1, 8, 10, False, True)
+    m3, m4 = advance(u1, 1, inv, u2, 2, 4, 8, True, True)
+    advance(u1, 1, inv, u2, 2, 8, 9, False, True)
     m5 = last_moment(u2, 2)
     msg[...] = message([m0, m1, m2, m3, m4, m5])
 
@@ -523,7 +523,8 @@
     for p in range(2):
         back = jnp.where(row == 0, prior_y[p][7:8], 0.0)
         if p == 0:
-            back = back + prior_x[0]
+            first = (lax.axis_index("pair") == 0) & (lax.axis_index("core") == 0)
+            back = back + jnp.where(first, 0.0, prior_x[0])
         model[p] = base[p] - primal_step * (grad[p] * scale + back)
 
 
@@ -537,7 +538,7 @@
 
 def moved(x, axis, by):
     peers = lax.axis_size(axis)
-    return lax.ppermute(x, axis, [(i, i + by) for i in range(peers) if 0 <= i + by < peers])
+    return lax.ppermute(x, axis, [(i, (i + by) % peers) for i in range(peers)])
 
 
 def swapped(x):
@@ -598,8 +599,8 @@
         )
     )
     space, last = ("pair", "core"), 2 * pairs
-    inward = [(i, i - 2) for i in range(2, last, 2)] + [(i, i + 2) for i in range(1, last - 2, 2)]
-    outward = [(i, i + 2) for i in range(0, last - 2, 2)] + [(i, i - 2) for i in range(3, last, 2)]
+    inward = [(i, (i + 2 * (-1, 1)[i % 2]) % last) for i in range(last)]
+    outward = [(i, (i + 2 * (1, -1)[i % 2]) % last) for i in range(last)]
     touch_m = lax.ppermute(packed, space, inward)
     beyond_m = lax.ppermute(packed, space, outward)
     own_t = swapped(packed)

time: 109 us -> 107 us (0.982)
  Pallas kernels: 38.8 us -> 37.2 us
    ppermute x1, starting transfers between devices: 1.28 us -> 6.29 us  [on_device(): beyond_m = lax.ppermute(packed, space, outward)]
    ppermute x2, waiting for transfers between devices: 6.02 us -> 1.33 us  [moved(): return lax.ppermute(x, axis, [(i, (i + by) % peers) for i in range(peers)])]
    ppermute x1, starting transfers between devices: 4.29 us -> 0.01 us  [on_device(): touch_m = lax.ppermute(packed, space, inward)]
    ppermute x1, waiting for transfers between devices: 0.01 us -> 3.09 us  [on_device(): beyond_m = lax.ppermute(packed, space, outward)]
    ppermute x3, waiting for transfers between devices: 3.86 us -> 5.89 us  [on_device(): lax.ppermute(bands[d], 'lap', [(i, i ^ d) for i in range(4)])]
    ppermute x2, starting transfers between devices: 4.85 us -> 3.01 us  [moved(): return lax.ppermute(x, axis, [(i, (i + by) % peers) for i in range(peers)])]
    ppermute x12, starting transfers between devices: 13.4 us -> 14.7 us  [others(): lax.ppermute(x, 'pair', [(i, i ^ d) for i in range(16)])]
  transfers between devices with their start and end apart: 23 -> 23, of which waited for: 13 -> 12; matrix products, arithmetic and copies ran while one was open for 0% -> 0% of each run, Pallas kernels for 14% -> 15%
where the time goes in v5:
time: 107 us
  Pallas kernels  37.2 us (35%)
  starting transfers between devices  36 us (34%)
  waiting for transfers between devices  18 us (17%)
  blocking collectives  14.7 us (14%)
    all_to_all x1, blocking collectives, on_device(): power = lax.all_to_all(power, ('lap', 'pair', 'core'), 0, 0, tiled=True)  14.7 us
    ppermute x12, starting transfers between devices, others(): lax.ppermute(x, 'pair', [(i, i ^ d) for i in range(16)])  14.7 us
    pallas_call x6, Pallas kernels, scatter(): pl.pallas_call(kernel, out_shape=tuple((struct(*shape) for shape in shape...  14.6 us
    ppermute x4, starting transfers between devices, swapped(): return lax.ppermute(x, 'core', [(0, 1), (1, 0)])  8.08 us
    pallas_call x1, Pallas kernels, on_device(): pl.pallas_call(adjoint_kernel, out_shape=(struct(4, ROWS, 128), struct(13...  7.58 us
    pallas_call x1, Pallas kernels, on_device(): pl.pallas_call(forward_kernel, out_shape=(struct(PLANES, ROWS, 128), stru...  7.21 us
    ppermute x1, starting transfers between devices, on_device(): beyond_m = lax.ppermute(packed, space, outward)  6.29 us
    ppermute x3, waiting for transfers between devices, on_device(): lax.ppermute(bands[d], 'lap', [(i, i ^ d) for i in range(4)])  5.89 us
  transfers between devices with their start and end apart: 23, of which 12 were waited for; matrix products, arithmetic and copies ran while one was open for 0% of the time, Pallas kernels for 15%

profile of v5, /device:TPU:1, one launch (start us, length us, event | category | flops | bytes accessed | tf_op | source)
XLA Modules:
  0.0 106.8 jit_solution(586875543886926515)
XLA Ops:
  0.6 1.4 %pack.1 = (f32[1112,128]{1,0:T(8,128)S(1)}, f32[88,128]{1,0:T(8,128)S(1)}) custom-call(f32[1024,128]{1,0:T(8,128)} %bitcast.7, s32[8,128]{1,0:T(8,128)} %bitcast.10, s32[8,128]{1,0:T(8,128)} %bitcast.11, f32[4,1024]{1,0:T(4,128)} %amp_in.1, f32[4,1024]{1,0:T(4,128)} %obs_in.1), custom_call_target="tpu_custom_call" | custom-call | tf_op jit(solution)/shard_map/pack/pallas_call | solution.py:580
  2.0 1.5 %collective-permute-start = (f32[1112,128]{1,0:T(8,128)S(1)}, f32[1112,128]{1,0:T(8,128)S(1)}, u32[]{:S(2)}, u32[]{:S(2)}) collective-permute-start(f32[1112,128]{1,0:T(8,128)S(1)} %get-tuple-element.68.mine.own_m), channel_id=1, source_target_pairs={{0,1},{1,0},{2,3},{3,2},{4,5},{5,4},{6,7},{7,6},{8,9},{9,8},{10,11... | collective-permute-start | bytes 1708040 | tf_op jit(solution)/shard_map/ppermute | solution.py:545
  3.5 6.3 %collective-permute-start.2 = (f32[1112,128]{1,0:T(8,128)S(1)}, f32[1112,128]{1,0:T(8,128)S(1)}, u32[]{:S(2)}, u32[]{:S(2)}) collective-permute-start(f32[1112,128]{1,0:T(8,128)S(1)} %get-tuple-element.68.mine.own_m), channel_id=1, source_target_pairs={{0,2},{1,31},{2,4},{3,1},{4,6},{5,3},{6,8},{7,5},{8,10},{9,7},{10,... | collective-permute-start | bytes 1708040 | tf_op jit(solution)/shard_map/ppermute | solution.py:605
  9.8 3.8 %scatter_other.1 = (f32[4,1024,128]{2,1,0:T(8,128)S(1)}, f32[4,1024,128]{2,1,0:T(8,128)S(1)}, f32[4,512,128]{2,1,0:T(8,128)S(1)}, f32[88,128]{1,0:T(8,128)S(1)}) custom-call(f32[1112,128]{1,0:T(8,128)S(1)} %get-tuple-element.68.mine.own_m, f32[1112,128]{1,0:T(8,128)S(1)} %collective-permute-done.other.own_t), custom_call_target="tpu_custom_call" | custom-call | flops 50000000 | bytes 10000 | tf_op jit(solution)/shard_map/scatter_other/pallas_call | solution.py:563
  13.6 1.5 %collective-permute-start.3 = (f32[88,128]{1,0:T(8,128)S(1)}, f32[88,128]{1,0:T(8,128)S(1)}, u32[]{:S(2)}, u32[]{:S(2)}) collective-permute-start(f32[88,128]{1,0:T(8,128)S(1)} %get-tuple-element.69.first_in), channel_id=1, source_target_pairs={{0,28},{2,30},{4,0},{6,2},{8,4},{10,6},{12,8},{14,10},{16,12},{18,... | collective-permute-start | bytes 135176 | tf_op jit(solution)/shard_map/ppermute | solution.py:541
  15.1 2.7 %scatter_own.1 = (f32[4,1024,128]{2,1,0:T(8,128)S(1)}, f32[4,1024,128]{2,1,0:T(8,128)S(1)}, f32[4,512,128]{2,1,0:T(8,128)S(1)}) custom-call(f32[88,128]{1,0:T(8,128)S(1)} %get-tuple-element.70.lists, f32[88,128]{1,0:T(8,128)S(1)} %get-tuple-element.69.first_in, ...), custom_call_target="tpu_custom_call", output_to_operand_aliasing={{0}: (2, {}), {1}: (3, {}), {2}: (4, {})} | custom-call | flops 50000000 | bytes 10000 | tf_op jit(solution)/shard_map/scatter_own/pallas_call | solution.py:563
  17.8 2.0 %forward_own.1 = (f32[13,1024,128]{2,1,0:T(8,128)S(1)}, f32[13,1024,128]{2,1,0:T(8,128)S(1)}, f32[11,1024,128]{2,1,0:T(8,128)S(1)}, f32[48,128]{1,0:T(8,128)S(1)}) custom-call(f32[4]{0:T(128)S(1)} %copy-done.2, f32[1112,128]{1,0:T(8,128)S(1)} %get-tuple-element.68.mine.own_m, f32[1112,128]{1,0:T(8,128)S(1)} %collective-permute-done.other.own_t, ...), custom_call_target="tpu_custom_call" | custom-call | flops 40000000 | bytes 10000 | tf_op jit(solution)/shard_map/forward_own/pallas_call | solution.py:617
  19.8 3.1 %collective-permute-done.2.beyond.beyond_m = f32[1112,128]{1,0:T(8,128)S(1)} collective-permute-done((f32[1112,128]{1,0:T(8,128)S(1)}, f32[1112,128]{1,0:T(8,128)S(1)}, u32[]{:S(2)}, u32[]{:S(2)}) %collective-permute-start.2) | collective-permute-done | bytes 569376 | tf_op jit(solution)/shard_map/ppermute | solution.py:605
  22.9 1.3 %collective-permute-done.1.touch.touch_m.mine = f32[1112,128]{1,0:T(8,128)S(1)} collective-permute-done((f32[1112,128]{1,0:T(8,128)S(1)}, f32[1112,128]{1,0:T(8,128)S(1)}, u32[]{:S(2)}, u32[]{:S(2)}) %collective-permute-start.1) | collective-permute-done | bytes 569376 | tf_op jit(solution)/shard_map/ppermute | solution.py:604
  24.2 0.6 collective-permute-start.4
  24.8 2.7 %scatter_mine.1.b_in = f32[9,1024,128]{2,1,0:T(8,128)S(1)} custom-call(f32[4]{0:T(128)S(1)} %copy-done.2, f32[1112,128]{1,0:T(8,128)S(1)} %collective-permute-done.1.touch.touch_m.mine, f32[1112,128]{1,0:T(8,128)S(1)} %collective-permute-done.2.beyond.beyond_m, f32[88,128]{1,0:T(8,128)S(1)} %collective-permute-done.3.far), custom_call_target="tpu_custom_call" | custom-call | flops 40000000 | bytes 10000 | tf_op jit(solution)/shard_map/scatter_mine/pallas_call | solution.py:563
  27.6 1.9 %scatter_theirs.1.b_near = f32[9,1024,128]{2,1,0:T(8,128)S(1)} custom-call(f32[1112,128]{1,0:T(8,128)S(1)} %collective-permute-done.4.touch.touch_t.theirs, f32[1112,128]{1,0:T(8,128)S(1)} %collective-permute-done.5.beyond.beyond_t, f32[9,1024,128]{2,1,0:T(8,128)S(1)} %scatter_mine.1.b_in), custom_call_target="tpu_custom_call", output_to_operand_aliasing={{}: (2, {})} | custom-call | flops 30000000 | bytes 10000 | tf_op jit(solution)/shard_map/scatter_theirs/pallas_call | solution.py:563
  29.4 7.2 %forward.1 = (f32[13,1024,128]{2,1,0:T(8,128)S(1)}, f32[13,1024,128]{2,1,0:T(8,128)S(1)}, f32[11,1024,128]{2,1,0:T(8,128)S(1)}, f32[9,1024,128]{2,1,0:T(8,128)S(1)}, f32[8,128]{1,0:T(8,128)S(1)}) custom-call(f32[4]{0:T(128)S(1)} %copy-done.2, ...), custom_call_target="tpu_custom_call", output_to_operand_aliasing={{0}: (7, {}), {1}: (8, {}), {2}: (9, {})} | custom-call | flops 200000000 | bytes 10000 | tf_op jit(solution)/shard_map/forward/pallas_call | solution.py:640
  36.6 1.5 %collective-permute-start.8 = (f32[8,128]{1,0:T(8,128)S(1)}, f32[8,128]{1,0:T(8,128)S(1)}, u32[]{:S(2)}, u32[]{:S(2)}) collective-permute-start(f32[8,128]{1,0:T(8,128)S(1)} %get-tuple-element.87), channel_id=1, source_target_pairs={{0,6},{2,4},{4,2},{6,0},{8,14},{10,12},{12,10},{14,8},{16,22},{18,... | collective-permute-start | bytes 12296 | tf_op jit(solution)/shard_map/ppermute | solution.py:549
  38.1 0.9 collective-permute-start.7
  39.0 1.0 collective-permute-start.6
  40.0 1.6 %scatter_later.1 = (f32[5,1024,128]{2,1,0:T(8,128)S(1)}, f32[5,512,128]{2,1,0:T(8,128)S(1)}) custom-call(f32[1112,128]{1,0:T(8,128)S(1)} %collective-permute-done.1.touch.touch_m.mine), custom_call_target="tpu_custom_call" | custom-call | flops 30000000 | bytes 10000 | tf_op jit(solution)/shard_map/scatter_later/pallas_call | solution.py:563
  41.6 0.5 collective-permute-done.7
  42.1 4.0 %collective-permute-start.11 = (f32[8,128]{1,0:T(8,128)S(1)}, f32[8,128]{1,0:T(8,128)S(1)}, u32[]{:S(2)}, u32[]{:S(2)}) collective-permute-start(f32[8,128]{1,0:T(8,128)S(1)} %add_add_fusion.1.t0), channel_id=1, source_target_pairs={{0,24},{2,26},{4,28},{6,30},{8,16},{10,18},{12,20},{14,22},{16,8},... | collective-permute-start | bytes 12296 | tf_op jit(solution)/shard_map/ppermute | solution.py:549
  46.1 0.7 collective-permute-start.9
  46.8 2.0 %scatter_late.1 = (f32[5,1024,128]{2,1,0:T(8,128)S(1)}, f32[5,512,128]{2,1,0:T(8,128)S(1)}) custom-call(f32[1112,128]{1,0:T(8,128)S(1)} %collective-permute-done.4.touch.touch_t.theirs, f32[1112,128]{1,0:T(8,128)S(1)} %collective-permute-done.2.beyond.beyond_m, ...), custom_call_target="tpu_custom_call", output_to_operand_aliasing={{0}: (3, {}), {1}: (4, {})} | custom-call | flops 40000000 | bytes 10000 | tf_op jit(solution)/shard_map/scatter_late/pallas_call | solution.py:563
  48.8 1.3 %collective-permute-done.10.t2 = f32[8,128]{1,0:T(8,128)S(1)} collective-permute-done((f32[8,128]{1,0:T(8,128)S(1)}, f32[8,128]{1,0:T(8,128)S(1)}, u32[]{:S(2)}, u32[]{:S(2)}) %collective-permute-start.10) | collective-permute-done | bytes 4128 | tf_op jit(solution)/shard_map/ppermute | solution.py:549
  50.1 7.6 %adjoint.1 = (f32[4,1024,128]{2,1,0:T(8,128)S(1)}, f32[13,1024,128]{2,1,0:T(8,128)S(1)}, f32[11,1024,128]{2,1,0:T(8,128)S(1)}, f32[9,1024,128]{2,1,0:T(8,128)S(1)}, f32[8,128]{1,0:T(8,128)S(1)}) custom-call(f32[8,128]{1,0:T(8,128)S(1)} %add_add_fusion.1.t0, ...), custom_call_target="tpu_custom_call", output_to_operand_aliasing={{1}: (5, {}), {2}: (6, {}), {3}: (7, {})} | custom-call | flops 140000000 | bytes 10000 | tf_op jit(solution)/shard_map/adjoint/pallas_call | solution.py:662
  57.7 1.3 %collective-permute-start.14 = (f32[8,128]{1,0:T(8,128)S(1)}, f32[8,128]{1,0:T(8,128)S(1)}, u32[]{:S(2)}, u32[]{:S(2)}) collective-permute-start(f32[8,128]{1,0:T(8,128)S(1)} %get-tuple-element.103), channel_id=1, source_target_pairs={{0,6},{2,4},{4,2},{6,0},{8,14},{10,12},{12,10},{14,8},{16,22},{18,... | collective-permute-start | bytes 12296 | tf_op jit(solution)/shard_map/ppermute | solution.py:549
  59.0 1.0 collective-permute-start.13
  60.0 1.0 collective-permute-start.12
  61.0 0.4 collective-permute-done.14
  61.4 1.6 %collective-permute-done.13 = f32[8,128]{1,0:T(8,128)S(1)} collective-permute-done((f32[8,128]{1,0:T(8,128)S(1)}, f32[8,128]{1,0:T(8,128)S(1)}, u32[]{:S(2)}, u32[]{:S(2)}) %collective-permute-start.13) | collective-permute-done | bytes 4128 | tf_op jit(solution)/shard_map/ppermute | solution.py:549
  63.0 1.4 %collective-permute-start.17 = (f32[8,128]{1,0:T(8,128)S(1)}, f32[8,128]{1,0:T(8,128)S(1)}, u32[]{:S(2)}, u32[]{:S(2)}) collective-permute-start(f32[8,128]{1,0:T(8,128)S(1)} %add_add_fusion.t0), channel_id=1, source_target_pairs={{0,24},{2,26},{4,28},{6,30},{8,16},{10,18},{12,20},{14,22},{16,8},... | collective-permute-start | bytes 12296 | tf_op jit(solution)/shard_map/ppermute | solution.py:549
  64.4 0.2 collective-permute-start.16
  64.6 1.7 %collective-permute-start.15 = (f32[8,128]{1,0:T(8,128)S(1)}, f32[8,128]{1,0:T(8,128)S(1)}, u32[]{:S(2)}, u32[]{:S(2)}) collective-permute-start(f32[8,128]{1,0:T(8,128)S(1)} %add_add_fusion.t0), channel_id=1, source_target_pairs={{0,8},{2,10},{4,12},{6,14},{8,0},{10,2},{12,4},{14,6},{16,24},{18,... | collective-permute-start | bytes 12296 | tf_op jit(solution)/shard_map/ppermute | solution.py:549
  66.3 0.4 collective-permute-done.17.t3
  66.7 1.6 %collective-permute-done.16.t2 = f32[8,128]{1,0:T(8,128)S(1)} collective-permute-done((f32[8,128]{1,0:T(8,128)S(1)}, f32[8,128]{1,0:T(8,128)S(1)}, u32[]{:S(2)}, u32[]{:S(2)}) %collective-permute-start.16) | collective-permute-done | bytes 4128 | tf_op jit(solution)/shard_map/ppermute | solution.py:549
  68.3 1.2 %gradient.2 = f32[4,2,128,128]{3,2,1,0:T(8,128)S(1)} custom-call(f32[4]{0:T(128)S(1)} %copy-done.2, f32[8,128]{1,0:T(8,128)S(1)} %add_add_fusion.t0, f32[8,128]{1,0:T(8,128)S(1)} %collective-permute-done.15.t1, f32[8,128]{1,0:T(8,128)S(1)} %collective-permute-done.16.t2, f32[8,128]{1,0:T(8,128)S(1)} %collective-permute-done.17.t3, ...), custom_call_target="tpu_custom_call" | custom-call | tf_op jit(solution)/shard_map/gradient/pallas_call | solution.py:680
  69.6 6.0 %collective-permute-start.18 = (f32[4,2,128,128]{3,2,1,0:T(8,128)S(1)}, f32[4,2,128,128]{3,2,1,0:T(8,128)S(1)}, u32[]{:S(2)}, u32[]{:S(2)}) collective-permute-start(f32[4,2,128,128]{3,2,1,0:T(8,128)S(1)} %gradient.2), channel_id=1, source_target_pairs={{0,1},{1,0},{2,3},{3,2},{4,5},{5,4},{6,7},{7,6},{8,9},{9,8},{10,11... | collective-permute-start | bytes 1572872 | tf_op jit(solution)/shard_map/ppermute | solution.py:545
  75.6 1.0 variation.1
  76.6 0.5 collective-permute-done.18.rest_0_
  77.1 1.3 %gradient.3 = (f32[2,136,128]{2,1,0:T(8,128)S(1)}, f32[2,136,128]{2,1,0:T(8,128)S(1)}, f32[2,136,128]{2,1,0:T(8,128)S(1)}, f32[2,136,128]{2,1,0:T(8,128)S(1)}) custom-call(f32[4]{0:T(128)S(1)} %copy-done.2, f32[8,128]{1,0:T(8,128)S(1)} %add_add_fusion.t0, f32[8,128]{1,0:T(8,128)S(1)} %collective-permute-done.15.t1, f32[8,128]{1,0:T(8,128)S(1)} %collective-permute-done.16.t2, ...), custom_call_target="tpu_custom_call" | custom-call | tf_op jit(solution)/shard_map/gradient/pallas_call | solution.py:680
  78.4 1.3 %collective-permute-start.19 = (f32[2,136,128]{2,1,0:T(8,128)S(1)}, f32[2,136,128]{2,1,0:T(8,128)S(1)}, u32[]{:S(2)}, u32[]{:S(2)}) collective-permute-start(f32[2,136,128]{2,1,0:T(8,128)S(1)} %get-tuple-element.121), channel_id=1, source_target_pairs={{0,32},{32,0},{64,96},{96,64},{1,33},{33,1},{65,97},{97,65},{2,34}... | collective-permute-start | bytes 417800 | tf_op jit(solution)/shard_map/ppermute | solution.py:708
  79.7 2.5 %collective-permute-start.20 = (f32[2,136,128]{2,1,0:T(8,128)S(1)}, f32[2,136,128]{2,1,0:T(8,128)S(1)}, u32[]{:S(2)}, u32[]{:S(2)}) collective-permute-start(f32[2,136,128]{2,1,0:T(8,128)S(1)} %get-tuple-element.122), channel_id=1, source_target_pairs={{0,64},{32,96},{64,0},{96,32},{1,65},{33,97},{65,1},{97,33},{2,66}... | collective-permute-start | bytes 417800 | tf_op jit(solution)/shard_map/ppermute | solution.py:708
  82.2 0.2 collective-permute-start.21
  82.4 1.5 %collective-permute-start.22 = (f32[1,128,128]{2,1,0:T(8,128)S(1)}, f32[1,128,128]{2,1,0:T(8,128)S(1)}, u32[]{:S(2)}, u32[]{:S(2)}) collective-permute-start(f32[1,128,128]{2,1,0:T(8,128)S(1)} %get-tuple-element.124), channel_id=1, source_target_pairs={{0,1},{1,2},{2,3},{3,4},{4,5},{5,6},{6,7},{7,8},{8,9},{9,10},{10,1... | collective-permute-start | bytes 196616 | tf_op jit(solution)/shard_map/ppermute | solution.py:541
  83.9 1.3 %collective-permute-done.22.prior_x = f32[1,128,128]{2,1,0:T(8,128)S(1)} collective-permute-done((f32[1,128,128]{2,1,0:T(8,128)S(1)}, f32[1,128,128]{2,1,0:T(8,128)S(1)}, u32[]{:S(2)}, u32[]{:S(2)}) %collective-permute-start.22) | collective-permute-done | bytes 65568 | tf_op jit(solution)/shard_map/ppermute | solution.py:541
  85.2 3.4 %collective-permute-done.20.g2 = f32[2,136,128]{2,1,0:T(8,128)S(1)} collective-permute-done((f32[2,136,128]{2,1,0:T(8,128)S(1)}, f32[2,136,128]{2,1,0:T(8,128)S(1)}, u32[]{:S(2)}, u32[]{:S(2)}) %collective-permute-start.20) | collective-permute-done | bytes 139296 | tf_op jit(solution)/shard_map/ppermute | solution.py:708
  88.6 2.5 %collective-permute-done.21.g3 = f32[2,136,128]{2,1,0:T(8,128)S(1)} collective-permute-done((f32[2,136,128]{2,1,0:T(8,128)S(1)}, f32[2,136,128]{2,1,0:T(8,128)S(1)}, u32[]{:S(2)}, u32[]{:S(2)}) %collective-permute-start.21) | collective-permute-done | bytes 139296 | tf_op jit(solution)/shard_map/ppermute | solution.py:708
  91.1 0.2 power.1
  91.3 14.7 %all_to_all.9 = f32[128,1,128]{2,1,0:T(1,128)S(1)} all-to-all(f32[128,1,128]{2,1,0:T(1,128)S(1)} %bitcast.9), channel_id=1, replica_groups=mesh['lap'=4,'pair'=16,'core'=2] {'lap','pair','core'}, dimensions={0} | all-to-all | bytes 131072 | tf_op jit(solution)/shard_map/all_to_all | solution.py:720
  106.0 0.7 model.1
  (22 shorter events, 0.1 us)
Async XLA Ops:
  0.6 17.2 %copy-start.2 = (f32[4]{0:T(128)S(1)}, f32[4]{0:T(128)}, u32[]{:S(2)}) copy-start(f32[4]{0:T(128)} %damp.9) | copy-start | bytes 52
  2.0 7.8 %collective-permute-start = (f32[1112,128]{1,0:T(8,128)S(1)}, f32[1112,128]{1,0:T(8,128)S(1)}, u32[]{:S(2)}, u32[]{:S(2)}) collective-permute-start(f32[1112,128]{1,0:T(8,128)S(1)} %get-tuple-element.68.mine.own_m), channel_id=1, source_target_pairs={{0,1},{1,0},{2,3},{3,2},{4,5},{5,4},{6,7},{7,6},{8,9},{9,8},{10,11... | collective-permute-start | bytes 1708040 | tf_op jit(solution)/shard_map/ppermute | solution.py:545
  3.5 19.3 %collective-permute-start.2 = (f32[1112,128]{1,0:T(8,128)S(1)}, f32[1112,128]{1,0:T(8,128)S(1)}, u32[]{:S(2)}, u32[]{:S(2)}) collective-permute-start(f32[1112,128]{1,0:T(8,128)S(1)} %get-tuple-element.68.mine.own_m), channel_id=1, source_target_pairs={{0,2},{1,31},{2,4},{3,1},{4,6},{5,3},{6,8},{7,5},{8,10},{9,7},{10,... | collective-permute-start | bytes 1708040 | tf_op jit(solution)/shard_map/ppermute | solution.py:605
  9.8 14.4 %collective-permute-start.1 = (f32[1112,128]{1,0:T(8,128)S(1)}, f32[1112,128]{1,0:T(8,128)S(1)}, u32[]{:S(2)}, u32[]{:S(2)}) collective-permute-start(f32[1112,128]{1,0:T(8,128)S(1)} %get-tuple-element.68.mine.own_m), channel_id=1, source_target_pairs={{0,30},{1,3},{2,0},{3,5},{4,2},{5,7},{6,4},{7,9},{8,6},{9,11},{10,... | collective-permute-start | bytes 1708040 | tf_op jit(solution)/shard_map/ppermute | solution.py:604
  13.6 10.6 %collective-permute-start.3 = (f32[88,128]{1,0:T(8,128)S(1)}, f32[88,128]{1,0:T(8,128)S(1)}, u32[]{:S(2)}, u32[]{:S(2)}) collective-permute-start(f32[88,128]{1,0:T(8,128)S(1)} %get-tuple-element.69.first_in), channel_id=1, source_target_pairs={{0,28},{2,30},{4,0},{6,2},{8,4},{10,6},{12,8},{14,10},{16,12},{18,... | collective-permute-start | bytes 135176 | tf_op jit(solution)/shard_map/ppermute | solution.py:541
  24.2 3.3 %collective-permute-start.4 = (f32[1112,128]{1,0:T(8,128)S(1)}, f32[1112,128]{1,0:T(8,128)S(1)}, u32[]{:S(2)}, u32[]{:S(2)}) collective-permute-start(f32[1112,128]{1,0:T(8,128)S(1)} %collective-permute-done.1.touch.touch_m.mine), channel_id=1, source_target_pairs={{0,1},{1,0},{2,3},{3,2},{4,5},{5,4},{6,7},{7,6},{8,9},{9,8},{10,11... | collective-permute-start | bytes 1708040 | tf_op jit(solution)/shard_map/ppermute | solution.py:545
  24.8 2.7 %collective-permute-start.5 = (f32[1112,128]{1,0:T(8,128)S(1)}, f32[1112,128]{1,0:T(8,128)S(1)}, u32[]{:S(2)}, u32[]{:S(2)}) collective-permute-start(f32[1112,128]{1,0:T(8,128)S(1)} %collective-permute-done.2.beyond.beyond_m), channel_id=1, source_target_pairs={{0,1},{1,0},{2,3},{3,2},{4,5},{5,4},{6,7},{7,6},{8,9},{9,8},{10,11... | collective-permute-start | bytes 1708040 | tf_op jit(solution)/shard_map/ppermute | solution.py:545
  36.6 4.9 %collective-permute-start.8 = (f32[8,128]{1,0:T(8,128)S(1)}, f32[8,128]{1,0:T(8,128)S(1)}, u32[]{:S(2)}, u32[]{:S(2)}) collective-permute-start(f32[8,128]{1,0:T(8,128)S(1)} %get-tuple-element.87), channel_id=1, source_target_pairs={{0,6},{2,4},{4,2},{6,0},{8,14},{10,12},{12,10},{14,8},{16,22},{18,... | collective-permute-start | bytes 12296 | tf_op jit(solution)/shard_map/ppermute | solution.py:549
  38.1 4.0 %collective-permute-start.7 = (f32[8,128]{1,0:T(8,128)S(1)}, f32[8,128]{1,0:T(8,128)S(1)}, u32[]{:S(2)}, u32[]{:S(2)}) collective-permute-start(f32[8,128]{1,0:T(8,128)S(1)} %get-tuple-element.87), channel_id=1, source_target_pairs={{0,4},{2,6},{4,0},{6,2},{8,12},{10,14},{12,8},{14,10},{16,20},{18,... | collective-permute-start | bytes 12296 | tf_op jit(solution)/shard_map/ppermute | solution.py:549
  39.0 3.1 %collective-permute-start.6 = (f32[8,128]{1,0:T(8,128)S(1)}, f32[8,128]{1,0:T(8,128)S(1)}, u32[]{:S(2)}, u32[]{:S(2)}) collective-permute-start(f32[8,128]{1,0:T(8,128)S(1)} %get-tuple-element.87), channel_id=1, source_target_pairs={{0,2},{2,0},{4,6},{6,4},{8,10},{10,8},{12,14},{14,12},{16,18},{18,... | collective-permute-start | bytes 12296 | tf_op jit(solution)/shard_map/ppermute | solution.py:549
  42.1 6.7 %collective-permute-start.11 = (f32[8,128]{1,0:T(8,128)S(1)}, f32[8,128]{1,0:T(8,128)S(1)}, u32[]{:S(2)}, u32[]{:S(2)}) collective-permute-start(f32[8,128]{1,0:T(8,128)S(1)} %add_add_fusion.1.t0), channel_id=1, source_target_pairs={{0,24},{2,26},{4,28},{6,30},{8,16},{10,18},{12,20},{14,22},{16,8},... | collective-permute-start | bytes 12296 | tf_op jit(solution)/shard_map/ppermute | solution.py:549
  46.1 4.0 %collective-permute-start.10 = (f32[8,128]{1,0:T(8,128)S(1)}, f32[8,128]{1,0:T(8,128)S(1)}, u32[]{:S(2)}, u32[]{:S(2)}) collective-permute-start(f32[8,128]{1,0:T(8,128)S(1)} %add_add_fusion.1.t0), channel_id=1, source_target_pairs={{0,16},{2,18},{4,20},{6,22},{8,24},{10,26},{12,28},{14,30},{16,0},... | collective-permute-start | bytes 12296 | tf_op jit(solution)/shard_map/ppermute | solution.py:549
  46.1 4.0 %collective-permute-start.9 = (f32[8,128]{1,0:T(8,128)S(1)}, f32[8,128]{1,0:T(8,128)S(1)}, u32[]{:S(2)}, u32[]{:S(2)}) collective-permute-start(f32[8,128]{1,0:T(8,128)S(1)} %add_add_fusion.1.t0), channel_id=1, source_target_pairs={{0,8},{2,10},{4,12},{6,14},{8,0},{10,2},{12,4},{14,6},{16,24},{18,... | collective-permute-start | bytes 12296 | tf_op jit(solution)/shard_map/ppermute | solution.py:549
  57.7 3.7 %collective-permute-start.14 = (f32[8,128]{1,0:T(8,128)S(1)}, f32[8,128]{1,0:T(8,128)S(1)}, u32[]{:S(2)}, u32[]{:S(2)}) collective-permute-start(f32[8,128]{1,0:T(8,128)S(1)} %get-tuple-element.103), channel_id=1, source_target_pairs={{0,6},{2,4},{4,2},{6,0},{8,14},{10,12},{12,10},{14,8},{16,22},{18,... | collective-permute-start | bytes 12296 | tf_op jit(solution)/shard_map/ppermute | solution.py:549
  59.0 4.0 %collective-permute-start.13 = (f32[8,128]{1,0:T(8,128)S(1)}, f32[8,128]{1,0:T(8,128)S(1)}, u32[]{:S(2)}, u32[]{:S(2)}) collective-permute-start(f32[8,128]{1,0:T(8,128)S(1)} %get-tuple-element.103), channel_id=1, source_target_pairs={{0,4},{2,6},{4,0},{6,2},{8,12},{10,14},{12,8},{14,10},{16,20},{18,... | collective-permute-start | bytes 12296 | tf_op jit(solution)/shard_map/ppermute | solution.py:549
  60.0 3.0 %collective-permute-start.12 = (f32[8,128]{1,0:T(8,128)S(1)}, f32[8,128]{1,0:T(8,128)S(1)}, u32[]{:S(2)}, u32[]{:S(2)}) collective-permute-start(f32[8,128]{1,0:T(8,128)S(1)} %get-tuple-element.103), channel_id=1, source_target_pairs={{0,2},{2,0},{4,6},{6,4},{8,10},{10,8},{12,14},{14,12},{16,18},{18,... | collective-permute-start | bytes 12296 | tf_op jit(solution)/shard_map/ppermute | solution.py:549
  63.0 3.7 %collective-permute-start.17 = (f32[8,128]{1,0:T(8,128)S(1)}, f32[8,128]{1,0:T(8,128)S(1)}, u32[]{:S(2)}, u32[]{:S(2)}) collective-permute-start(f32[8,128]{1,0:T(8,128)S(1)} %add_add_fusion.t0), channel_id=1, source_target_pairs={{0,24},{2,26},{4,28},{6,30},{8,16},{10,18},{12,20},{14,22},{16,8},... | collective-permute-start | bytes 12296 | tf_op jit(solution)/shard_map/ppermute | solution.py:549
  64.4 4.0 %collective-permute-start.16 = (f32[8,128]{1,0:T(8,128)S(1)}, f32[8,128]{1,0:T(8,128)S(1)}, u32[]{:S(2)}, u32[]{:S(2)}) collective-permute-start(f32[8,128]{1,0:T(8,128)S(1)} %add_add_fusion.t0), channel_id=1, source_target_pairs={{0,16},{2,18},{4,20},{6,22},{8,24},{10,26},{12,28},{14,30},{16,0},... | collective-permute-start | bytes 12296 | tf_op jit(solution)/shard_map/ppermute | solution.py:549
  64.6 3.7 %collective-permute-start.15 = (f32[8,128]{1,0:T(8,128)S(1)}, f32[8,128]{1,0:T(8,128)S(1)}, u32[]{:S(2)}, u32[]{:S(2)}) collective-permute-start(f32[8,128]{1,0:T(8,128)S(1)} %add_add_fusion.t0), channel_id=1, source_target_pairs={{0,8},{2,10},{4,12},{6,14},{8,0},{10,2},{12,4},{14,6},{16,24},{18,... | collective-permute-start | bytes 12296 | tf_op jit(solution)/shard_map/ppermute | solution.py:549
  68.3 7.2 %copy-start = (f32[2,512,128]{2,1,0:T(8,128)S(1)}, f32[2,512,128]{2,1,0:T(8,128)}, u32[]{:S(2)}) copy-start(f32[2,512,128]{2,1,0:T(8,128)} %slow) | copy-start | bytes 1572868
  68.3 7.2 %copy-start.1 = (f32[3,2,128,128]{3,2,1,0:T(8,128)S(1)}, f32[3,2,128,128]{3,2,1,0:T(8,128)}, u32[]{:S(2)}) copy-start(f32[3,2,128,128]{3,2,1,0:T(8,128)} %dual) | copy-start | bytes 1179652
  69.6 7.5 %collective-permute-start.18 = (f32[4,2,128,128]{3,2,1,0:T(8,128)S(1)}, f32[4,2,128,128]{3,2,1,0:T(8,128)S(1)}, u32[]{:S(2)}, u32[]{:S(2)}) collective-permute-start(f32[4,2,128,128]{3,2,1,0:T(8,128)S(1)} %gradient.2), channel_id=1, source_target_pairs={{0,1},{1,0},{2,3},{3,2},{4,5},{5,4},{6,7},{7,6},{8,9},{9,8},{10,11... | collective-permute-start | bytes 1572872 | tf_op jit(solution)/shard_map/ppermute | solution.py:545
  78.4 6.8 %collective-permute-start.19 = (f32[2,136,128]{2,1,0:T(8,128)S(1)}, f32[2,136,128]{2,1,0:T(8,128)S(1)}, u32[]{:S(2)}, u32[]{:S(2)}) collective-permute-start(f32[2,136,128]{2,1,0:T(8,128)S(1)} %get-tuple-element.121), channel_id=1, source_target_pairs={{0,32},{32,0},{64,96},{96,64},{1,33},{33,1},{65,97},{97,65},{2,34}... | collective-permute-start | bytes 417800 | tf_op jit(solution)/shard_map/ppermute | solution.py:708
  79.7 8.9 %collective-permute-start.20 = (f32[2,136,128]{2,1,0:T(8,128)S(1)}, f32[2,136,128]{2,1,0:T(8,128)S(1)}, u32[]{:S(2)}, u32[]{:S(2)}) collective-permute-start(f32[2,136,128]{2,1,0:T(8,128)S(1)} %get-tuple-element.122), channel_id=1, source_target_pairs={{0,64},{32,96},{64,0},{96,32},{1,65},{33,97},{65,1},{97,33},{2,66}... | collective-permute-start | bytes 417800 | tf_op jit(solution)/shard_map/ppermute | solution.py:708
  82.2 8.9 %collective-permute-start.21 = (f32[2,136,128]{2,1,0:T(8,128)S(1)}, f32[2,136,128]{2,1,0:T(8,128)S(1)}, u32[]{:S(2)}, u32[]{:S(2)}) collective-permute-start(f32[2,136,128]{2,1,0:T(8,128)S(1)} %get-tuple-element.123), channel_id=1, source_target_pairs={{0,96},{32,64},{64,32},{96,0},{1,97},{33,65},{65,33},{97,1},{2,98}... | collective-permute-start | bytes 417800 | tf_op jit(solution)/shard_map/ppermute | solution.py:708
  82.4 2.8 %collective-permute-start.22 = (f32[1,128,128]{2,1,0:T(8,128)S(1)}, f32[1,128,128]{2,1,0:T(8,128)S(1)}, u32[]{:S(2)}, u32[]{:S(2)}) collective-permute-start(f32[1,128,128]{2,1,0:T(8,128)S(1)} %get-tuple-element.124), channel_id=1, source_target_pairs={{0,1},{1,2},{2,3},{3,4},{4,5},{5,6},{6,7},{7,8},{8,9},{9,10},{10,1... | collective-permute-start | bytes 196616 | tf_op jit(solution)/shard_map/ppermute | solution.py:541

commit v6 on v5

--- a/solution.py
+++ b/solution.py
@@ -280,7 +280,7 @@
             out.append(carry[c] + fold(x * q))
         return out
 
-    return [2.0 * m for m in walk(4, 8, body, nothing())]
+    return [2.0 * m for m in walk(4, 8, body, nothing(), True)]
 
 
 def message(moments):
@@ -646,7 +646,7 @@
         in_specs=[SMEM] + [VMEM] * 9,
         out_specs=(VMEM,) * 5,
         input_output_aliases={7: 0, 8: 1, 9: 2},
-        compiler_params=params(2),
+        compiler_params=params(4),
         cost_estimate=cost(20),
         name="forward",
     )(damping, touch_m, touch_t, beyond_m, beyond_t, b_near, held, inv, v0, v1)
@@ -668,7 +668,7 @@
         in_specs=[VMEM] * 12,
         out_specs=(VMEM,) * 5,
         input_output_aliases={5: 1, 6: 2, 7: 3},
-        compiler_params=params(2),
+        compiler_params=params(4),
         cost_estimate=cost(14),
         name="adjoint",
     )(*stage_terms(half_sum), inv, v0, v1, v2, ob_own, cn_own, ob_near, cn_near)

time: 107 us -> 107 us (level)
  no operation moved by 1% of the time
where the time goes in v6:
time: 107 us
  Pallas kernels  37.3 us (35%)
  starting transfers between devices  36 us (34%)
  waiting for transfers between devices  17.9 us (17%)
  blocking collectives  14.7 us (14%)
    all_to_all x1, blocking collectives, on_device(): power = lax.all_to_all(power, ('lap', 'pair', 'core'), 0, 0, tiled=True)  14.7 us
    ppermute x12, starting transfers between devices, others(): lax.ppermute(x, 'pair', [(i, i ^ d) for i in range(16)])  14.7 us
    pallas_call x6, Pallas kernels, scatter(): pl.pallas_call(kernel, out_shape=tuple((struct(*shape) for shape in shape...  14.6 us
    ppermute x4, starting transfers between devices, swapped(): return lax.ppermute(x, 'core', [(0, 1), (1, 0)])  8.07 us
    pallas_call x1, Pallas kernels, on_device(): pl.pallas_call(adjoint_kernel, out_shape=(struct(4, ROWS, 128), struct(13...  7.49 us
    pallas_call x1, Pallas kernels, on_device(): pl.pallas_call(forward_kernel, out_shape=(struct(PLANES, ROWS, 128), stru...  7.4 us
    ppermute x1, starting transfers between devices, on_device(): beyond_m = lax.ppermute(packed, space, outward)  6.29 us
    ppermute x3, waiting for transfers between devices, on_device(): lax.ppermute(bands[d], 'lap', [(i, i ^ d) for i in range(4)])  5.89 us
  transfers between devices with their start and end apart: 23, of which 12 were waited for; matrix products, arithmetic and copies ran while one was open for 0% of the time, Pallas kernels for 15%

profile of v6, /device:TPU:1, one launch (start us, length us, event | category | flops | bytes accessed | tf_op | source)
XLA Modules:
  0.0 106.8 jit_solution(4575106861976648825)
XLA Ops:
  0.6 1.4 %pack.1 = (f32[1112,128]{1,0:T(8,128)S(1)}, f32[88,128]{1,0:T(8,128)S(1)}) custom-call(f32[1024,128]{1,0:T(8,128)} %bitcast.7, s32[8,128]{1,0:T(8,128)} %bitcast.10, s32[8,128]{1,0:T(8,128)} %bitcast.11, f32[4,1024]{1,0:T(4,128)} %amp_in.1, f32[4,1024]{1,0:T(4,128)} %obs_in.1), custom_call_target="tpu_custom_call" | custom-call | tf_op jit(solution)/shard_map/pack/pallas_call | solution.py:580
  2.0 1.5 %collective-permute-start = (f32[1112,128]{1,0:T(8,128)S(1)}, f32[1112,128]{1,0:T(8,128)S(1)}, u32[]{:S(2)}, u32[]{:S(2)}) collective-permute-start(f32[1112,128]{1,0:T(8,128)S(1)} %get-tuple-element.68.mine.own_m), channel_id=1, source_target_pairs={{0,1},{1,0},{2,3},{3,2},{4,5},{5,4},{6,7},{7,6},{8,9},{9,8},{10,11... | collective-permute-start | bytes 1708040 | tf_op jit(solution)/shard_map/ppermute | solution.py:545
  3.5 6.3 %collective-permute-start.2 = (f32[1112,128]{1,0:T(8,128)S(1)}, f32[1112,128]{1,0:T(8,128)S(1)}, u32[]{:S(2)}, u32[]{:S(2)}) collective-permute-start(f32[1112,128]{1,0:T(8,128)S(1)} %get-tuple-element.68.mine.own_m), channel_id=1, source_target_pairs={{0,2},{1,31},{2,4},{3,1},{4,6},{5,3},{6,8},{7,5},{8,10},{9,7},{10,... | collective-permute-start | bytes 1708040 | tf_op jit(solution)/shard_map/ppermute | solution.py:605
  9.8 3.8 %scatter_other.1 = (f32[4,1024,128]{2,1,0:T(8,128)S(1)}, f32[4,1024,128]{2,1,0:T(8,128)S(1)}, f32[4,512,128]{2,1,0:T(8,128)S(1)}, f32[88,128]{1,0:T(8,128)S(1)}) custom-call(f32[1112,128]{1,0:T(8,128)S(1)} %get-tuple-element.68.mine.own_m, f32[1112,128]{1,0:T(8,128)S(1)} %collective-permute-done.other.own_t), custom_call_target="tpu_custom_call" | custom-call | flops 50000000 | bytes 10000 | tf_op jit(solution)/shard_map/scatter_other/pallas_call | solution.py:563
  13.6 1.5 %collective-permute-start.3 = (f32[88,128]{1,0:T(8,128)S(1)}, f32[88,128]{1,0:T(8,128)S(1)}, u32[]{:S(2)}, u32[]{:S(2)}) collective-permute-start(f32[88,128]{1,0:T(8,128)S(1)} %get-tuple-element.69.first_in), channel_id=1, source_target_pairs={{0,28},{2,30},{4,0},{6,2},{8,4},{10,6},{12,8},{14,10},{16,12},{18,... | collective-permute-start | bytes 135176 | tf_op jit(solution)/shard_map/ppermute | solution.py:541
  15.1 2.7 %scatter_own.1 = (f32[4,1024,128]{2,1,0:T(8,128)S(1)}, f32[4,1024,128]{2,1,0:T(8,128)S(1)}, f32[4,512,128]{2,1,0:T(8,128)S(1)}) custom-call(f32[88,128]{1,0:T(8,128)S(1)} %get-tuple-element.70.lists, f32[88,128]{1,0:T(8,128)S(1)} %get-tuple-element.69.first_in, ...), custom_call_target="tpu_custom_call", output_to_operand_aliasing={{0}: (2, {}), {1}: (3, {}), {2}: (4, {})} | custom-call | flops 50000000 | bytes 10000 | tf_op jit(solution)/shard_map/scatter_own/pallas_call | solution.py:563
  17.8 2.0 %forward_own.1 = (f32[13,1024,128]{2,1,0:T(8,128)S(1)}, f32[13,1024,128]{2,1,0:T(8,128)S(1)}, f32[11,1024,128]{2,1,0:T(8,128)S(1)}, f32[48,128]{1,0:T(8,128)S(1)}) custom-call(f32[4]{0:T(128)S(1)} %copy-done.2, f32[1112,128]{1,0:T(8,128)S(1)} %get-tuple-element.68.mine.own_m, f32[1112,128]{1,0:T(8,128)S(1)} %collective-permute-done.other.own_t, ...), custom_call_target="tpu_custom_call" | custom-call | flops 40000000 | bytes 10000 | tf_op jit(solution)/shard_map/forward_own/pallas_call | solution.py:617
  19.8 3.0 %collective-permute-done.2.beyond.beyond_m = f32[1112,128]{1,0:T(8,128)S(1)} collective-permute-done((f32[1112,128]{1,0:T(8,128)S(1)}, f32[1112,128]{1,0:T(8,128)S(1)}, u32[]{:S(2)}, u32[]{:S(2)}) %collective-permute-start.2) | collective-permute-done | bytes 569376 | tf_op jit(solution)/shard_map/ppermute | solution.py:605
  22.9 1.3 %collective-permute-done.1.touch.touch_m.mine = f32[1112,128]{1,0:T(8,128)S(1)} collective-permute-done((f32[1112,128]{1,0:T(8,128)S(1)}, f32[1112,128]{1,0:T(8,128)S(1)}, u32[]{:S(2)}, u32[]{:S(2)}) %collective-permute-start.1) | collective-permute-done | bytes 569376 | tf_op jit(solution)/shard_map/ppermute | solution.py:604
  24.2 0.6 collective-permute-start.4
  24.8 2.7 %scatter_mine.1.b_in = f32[9,1024,128]{2,1,0:T(8,128)S(1)} custom-call(f32[4]{0:T(128)S(1)} %copy-done.2, f32[1112,128]{1,0:T(8,128)S(1)} %collective-permute-done.1.touch.touch_m.mine, f32[1112,128]{1,0:T(8,128)S(1)} %collective-permute-done.2.beyond.beyond_m, f32[88,128]{1,0:T(8,128)S(1)} %collective-permute-done.3.far), custom_call_target="tpu_custom_call" | custom-call | flops 40000000 | bytes 10000 | tf_op jit(solution)/shard_map/scatter_mine/pallas_call | solution.py:563
  27.6 1.9 %scatter_theirs.1.b_near = f32[9,1024,128]{2,1,0:T(8,128)S(1)} custom-call(f32[1112,128]{1,0:T(8,128)S(1)} %collective-permute-done.4.touch.touch_t.theirs, f32[1112,128]{1,0:T(8,128)S(1)} %collective-permute-done.5.beyond.beyond_t, f32[9,1024,128]{2,1,0:T(8,128)S(1)} %scatter_mine.1.b_in), custom_call_target="tpu_custom_call", output_to_operand_aliasing={{}: (2, {})} | custom-call | flops 30000000 | bytes 10000 | tf_op jit(solution)/shard_map/scatter_theirs/pallas_call | solution.py:563
  29.4 7.4 %forward.1 = (f32[13,1024,128]{2,1,0:T(8,128)S(1)}, f32[13,1024,128]{2,1,0:T(8,128)S(1)}, f32[11,1024,128]{2,1,0:T(8,128)S(1)}, f32[9,1024,128]{2,1,0:T(8,128)S(1)}, f32[8,128]{1,0:T(8,128)S(1)}) custom-call(f32[4]{0:T(128)S(1)} %copy-done.2, ...), custom_call_target="tpu_custom_call", output_to_operand_aliasing={{0}: (7, {}), {1}: (8, {}), {2}: (9, {})} | custom-call | flops 200000000 | bytes 10000 | tf_op jit(solution)/shard_map/forward/pallas_call | solution.py:640
  36.8 1.5 %collective-permute-start.8 = (f32[8,128]{1,0:T(8,128)S(1)}, f32[8,128]{1,0:T(8,128)S(1)}, u32[]{:S(2)}, u32[]{:S(2)}) collective-permute-start(f32[8,128]{1,0:T(8,128)S(1)} %get-tuple-element.87), channel_id=1, source_target_pairs={{0,6},{2,4},{4,2},{6,0},{8,14},{10,12},{12,10},{14,8},{16,22},{18,... | collective-permute-start | bytes 12296 | tf_op jit(solution)/shard_map/ppermute | solution.py:549
  38.3 0.9 collective-permute-start.7
  39.2 1.0 collective-permute-start.6
  40.2 1.6 %scatter_later.1 = (f32[5,1024,128]{2,1,0:T(8,128)S(1)}, f32[5,512,128]{2,1,0:T(8,128)S(1)}) custom-call(f32[1112,128]{1,0:T(8,128)S(1)} %collective-permute-done.1.touch.touch_m.mine), custom_call_target="tpu_custom_call" | custom-call | flops 30000000 | bytes 10000 | tf_op jit(solution)/shard_map/scatter_later/pallas_call | solution.py:563
  41.8 0.5 collective-permute-done.7
  42.3 4.0 %collective-permute-start.11 = (f32[8,128]{1,0:T(8,128)S(1)}, f32[8,128]{1,0:T(8,128)S(1)}, u32[]{:S(2)}, u32[]{:S(2)}) collective-permute-start(f32[8,128]{1,0:T(8,128)S(1)} %add_add_fusion.1.t0), channel_id=1, source_target_pairs={{0,24},{2,26},{4,28},{6,30},{8,16},{10,18},{12,20},{14,22},{16,8},... | collective-permute-start | bytes 12296 | tf_op jit(solution)/shard_map/ppermute | solution.py:549
  46.3 0.7 collective-permute-start.9
  47.0 2.0 %scatter_late.1 = (f32[5,1024,128]{2,1,0:T(8,128)S(1)}, f32[5,512,128]{2,1,0:T(8,128)S(1)}) custom-call(f32[1112,128]{1,0:T(8,128)S(1)} %collective-permute-done.4.touch.touch_t.theirs, f32[1112,128]{1,0:T(8,128)S(1)} %collective-permute-done.2.beyond.beyond_m, ...), custom_call_target="tpu_custom_call", output_to_operand_aliasing={{0}: (3, {}), {1}: (4, {})} | custom-call | flops 40000000 | bytes 10000 | tf_op jit(solution)/shard_map/scatter_late/pallas_call | solution.py:563
  49.0 1.3 %collective-permute-done.10.t2 = f32[8,128]{1,0:T(8,128)S(1)} collective-permute-done((f32[8,128]{1,0:T(8,128)S(1)}, f32[8,128]{1,0:T(8,128)S(1)}, u32[]{:S(2)}, u32[]{:S(2)}) %collective-permute-start.10) | collective-permute-done | bytes 4128 | tf_op jit(solution)/shard_map/ppermute | solution.py:549
  50.2 7.5 %adjoint.1 = (f32[4,1024,128]{2,1,0:T(8,128)S(1)}, f32[13,1024,128]{2,1,0:T(8,128)S(1)}, f32[11,1024,128]{2,1,0:T(8,128)S(1)}, f32[9,1024,128]{2,1,0:T(8,128)S(1)}, f32[8,128]{1,0:T(8,128)S(1)}) custom-call(f32[8,128]{1,0:T(8,128)S(1)} %add_add_fusion.1.t0, ...), custom_call_target="tpu_custom_call", output_to_operand_aliasing={{1}: (5, {}), {2}: (6, {}), {3}: (7, {})} | custom-call | flops 140000000 | bytes 10000 | tf_op jit(solution)/shard_map/adjoint/pallas_call | solution.py:662
  57.7 1.4 %collective-permute-start.14 = (f32[8,128]{1,0:T(8,128)S(1)}, f32[8,128]{1,0:T(8,128)S(1)}, u32[]{:S(2)}, u32[]{:S(2)}) collective-permute-start(f32[8,128]{1,0:T(8,128)S(1)} %get-tuple-element.103), channel_id=1, source_target_pairs={{0,6},{2,4},{4,2},{6,0},{8,14},{10,12},{12,10},{14,8},{16,22},{18,... | collective-permute-start | bytes 12296 | tf_op jit(solution)/shard_map/ppermute | solution.py:549
  59.1 1.0 collective-permute-start.13
  60.1 1.0 collective-permute-start.12
  61.1 0.4 collective-permute-done.14
  61.5 1.6 %collective-permute-done.13 = f32[8,128]{1,0:T(8,128)S(1)} collective-permute-done((f32[8,128]{1,0:T(8,128)S(1)}, f32[8,128]{1,0:T(8,128)S(1)}, u32[]{:S(2)}, u32[]{:S(2)}) %collective-permute-start.13) | collective-permute-done | bytes 4128 | tf_op jit(solution)/shard_map/ppermute | solution.py:549
  63.1 1.4 %collective-permute-start.17 = (f32[8,128]{1,0:T(8,128)S(1)}, f32[8,128]{1,0:T(8,128)S(1)}, u32[]{:S(2)}, u32[]{:S(2)}) collective-permute-start(f32[8,128]{1,0:T(8,128)S(1)} %add_add_fusion.t0), channel_id=1, source_target_pairs={{0,24},{2,26},{4,28},{6,30},{8,16},{10,18},{12,20},{14,22},{16,8},... | collective-permute-start | bytes 12296 | tf_op jit(solution)/shard_map/ppermute | solution.py:549
  64.5 0.2 collective-permute-start.16
  64.7 1.7 %collective-permute-start.15 = (f32[8,128]{1,0:T(8,128)S(1)}, f32[8,128]{1,0:T(8,128)S(1)}, u32[]{:S(2)}, u32[]{:S(2)}) collective-permute-start(f32[8,128]{1,0:T(8,128)S(1)} %add_add_fusion.t0), channel_id=1, source_target_pairs={{0,8},{2,10},{4,12},{6,14},{8,0},{10,2},{12,4},{14,6},{16,24},{18,... | collective-permute-start | bytes 12296 | tf_op jit(solution)/shard_map/ppermute | solution.py:549
  66.4 0.4 collective-permute-done.17.t3
  66.8 1.6 %collective-permute-done.16.t2 = f32[8,128]{1,0:T(8,128)S(1)} collective-permute-done((f32[8,128]{1,0:T(8,128)S(1)}, f32[8,128]{1,0:T(8,128)S(1)}, u32[]{:S(2)}, u32[]{:S(2)}) %collective-permute-start.16) | collective-permute-done | bytes 4128 | tf_op jit(solution)/shard_map/ppermute | solution.py:549
  68.4 1.2 %gradient.2 = f32[4,2,128,128]{3,2,1,0:T(8,128)S(1)} custom-call(f32[4]{0:T(128)S(1)} %copy-done.2, f32[8,128]{1,0:T(8,128)S(1)} %add_add_fusion.t0, f32[8,128]{1,0:T(8,128)S(1)} %collective-permute-done.15.t1, f32[8,128]{1,0:T(8,128)S(1)} %collective-permute-done.16.t2, f32[8,128]{1,0:T(8,128)S(1)} %collective-permute-done.17.t3, ...), custom_call_target="tpu_custom_call" | custom-call | tf_op jit(solution)/shard_map/gradient/pallas_call | solution.py:680
  69.7 6.0 %collective-permute-start.18 = (f32[4,2,128,128]{3,2,1,0:T(8,128)S(1)}, f32[4,2,128,128]{3,2,1,0:T(8,128)S(1)}, u32[]{:S(2)}, u32[]{:S(2)}) collective-permute-start(f32[4,2,128,128]{3,2,1,0:T(8,128)S(1)} %gradient.2), channel_id=1, source_target_pairs={{0,1},{1,0},{2,3},{3,2},{4,5},{5,4},{6,7},{7,6},{8,9},{9,8},{10,11... | collective-permute-start | bytes 1572872 | tf_op jit(solution)/shard_map/ppermute | solution.py:545
  75.7 1.0 variation.1
  76.7 0.5 collective-permute-done.18.rest_0_
  77.2 1.3 %gradient.3 = (f32[2,136,128]{2,1,0:T(8,128)S(1)}, f32[2,136,128]{2,1,0:T(8,128)S(1)}, f32[2,136,128]{2,1,0:T(8,128)S(1)}, f32[2,136,128]{2,1,0:T(8,128)S(1)}) custom-call(f32[4]{0:T(128)S(1)} %copy-done.2, f32[8,128]{1,0:T(8,128)S(1)} %add_add_fusion.t0, f32[8,128]{1,0:T(8,128)S(1)} %collective-permute-done.15.t1, f32[8,128]{1,0:T(8,128)S(1)} %collective-permute-done.16.t2, ...), custom_call_target="tpu_custom_call" | custom-call | tf_op jit(solution)/shard_map/gradient/pallas_call | solution.py:680
  78.5 1.3 %collective-permute-start.19 = (f32[2,136,128]{2,1,0:T(8,128)S(1)}, f32[2,136,128]{2,1,0:T(8,128)S(1)}, u32[]{:S(2)}, u32[]{:S(2)}) collective-permute-start(f32[2,136,128]{2,1,0:T(8,128)S(1)} %get-tuple-element.121), channel_id=1, source_target_pairs={{0,32},{32,0},{64,96},{96,64},{1,33},{33,1},{65,97},{97,65},{2,34}... | collective-permute-start | bytes 417800 | tf_op jit(solution)/shard_map/ppermute | solution.py:708
  79.8 2.5 %collective-permute-start.20 = (f32[2,136,128]{2,1,0:T(8,128)S(1)}, f32[2,136,128]{2,1,0:T(8,128)S(1)}, u32[]{:S(2)}, u32[]{:S(2)}) collective-permute-start(f32[2,136,128]{2,1,0:T(8,128)S(1)} %get-tuple-element.122), channel_id=1, source_target_pairs={{0,64},{32,96},{64,0},{96,32},{1,65},{33,97},{65,1},{97,33},{2,66}... | collective-permute-start | bytes 417800 | tf_op jit(solution)/shard_map/ppermute | solution.py:708
  82.3 0.2 collective-permute-start.21
  82.5 1.5 %collective-permute-start.22 = (f32[1,128,128]{2,1,0:T(8,128)S(1)}, f32[1,128,128]{2,1,0:T(8,128)S(1)}, u32[]{:S(2)}, u32[]{:S(2)}) collective-permute-start(f32[1,128,128]{2,1,0:T(8,128)S(1)} %get-tuple-element.124), channel_id=1, source_target_pairs={{0,1},{1,2},{2,3},{3,4},{4,5},{5,6},{6,7},{7,8},{8,9},{9,10},{10,1... | collective-permute-start | bytes 196616 | tf_op jit(solution)/shard_map/ppermute | solution.py:541
  84.0 1.3 %collective-permute-done.22.prior_x = f32[1,128,128]{2,1,0:T(8,128)S(1)} collective-permute-done((f32[1,128,128]{2,1,0:T(8,128)S(1)}, f32[1,128,128]{2,1,0:T(8,128)S(1)}, u32[]{:S(2)}, u32[]{:S(2)}) %collective-permute-start.22) | collective-permute-done | bytes 65568 | tf_op jit(solution)/shard_map/ppermute | solution.py:541
  85.3 3.4 %collective-permute-done.20.g2 = f32[2,136,128]{2,1,0:T(8,128)S(1)} collective-permute-done((f32[2,136,128]{2,1,0:T(8,128)S(1)}, f32[2,136,128]{2,1,0:T(8,128)S(1)}, u32[]{:S(2)}, u32[]{:S(2)}) %collective-permute-start.20) | collective-permute-done | bytes 139296 | tf_op jit(solution)/shard_map/ppermute | solution.py:708
  88.7 2.5 %collective-permute-done.21.g3 = f32[2,136,128]{2,1,0:T(8,128)S(1)} collective-permute-done((f32[2,136,128]{2,1,0:T(8,128)S(1)}, f32[2,136,128]{2,1,0:T(8,128)S(1)}, u32[]{:S(2)}, u32[]{:S(2)}) %collective-permute-start.21) | collective-permute-done | bytes 139296 | tf_op jit(solution)/shard_map/ppermute | solution.py:708
  91.2 0.2 power.1
  91.4 14.7 %all_to_all.9 = f32[128,1,128]{2,1,0:T(1,128)S(1)} all-to-all(f32[128,1,128]{2,1,0:T(1,128)S(1)} %bitcast.9), channel_id=1, replica_groups=mesh['lap'=4,'pair'=16,'core'=2] {'lap','pair','core'}, dimensions={0} | all-to-all | bytes 131072 | tf_op jit(solution)/shard_map/all_to_all | solution.py:720
  106.1 0.7 model.1
  (22 shorter events, 0.1 us)
Async XLA Ops:
  0.6 17.2 %copy-start.2 = (f32[4]{0:T(128)S(1)}, f32[4]{0:T(128)}, u32[]{:S(2)}) copy-start(f32[4]{0:T(128)} %damp.9) | copy-start | bytes 52
  2.0 7.8 %collective-permute-start = (f32[1112,128]{1,0:T(8,128)S(1)}, f32[1112,128]{1,0:T(8,128)S(1)}, u32[]{:S(2)}, u32[]{:S(2)}) collective-permute-start(f32[1112,128]{1,0:T(8,128)S(1)} %get-tuple-element.68.mine.own_m), channel_id=1, source_target_pairs={{0,1},{1,0},{2,3},{3,2},{4,5},{5,4},{6,7},{7,6},{8,9},{9,8},{10,11... | collective-permute-start | bytes 1708040 | tf_op jit(solution)/shard_map/ppermute | solution.py:545
  3.5 19.3 %collective-permute-start.2 = (f32[1112,128]{1,0:T(8,128)S(1)}, f32[1112,128]{1,0:T(8,128)S(1)}, u32[]{:S(2)}, u32[]{:S(2)}) collective-permute-start(f32[1112,128]{1,0:T(8,128)S(1)} %get-tuple-element.68.mine.own_m), channel_id=1, source_target_pairs={{0,2},{1,31},{2,4},{3,1},{4,6},{5,3},{6,8},{7,5},{8,10},{9,7},{10,... | collective-permute-start | bytes 1708040 | tf_op jit(solution)/shard_map/ppermute | solution.py:605
  9.8 14.4 %collective-permute-start.1 = (f32[1112,128]{1,0:T(8,128)S(1)}, f32[1112,128]{1,0:T(8,128)S(1)}, u32[]{:S(2)}, u32[]{:S(2)}) collective-permute-start(f32[1112,128]{1,0:T(8,128)S(1)} %get-tuple-element.68.mine.own_m), channel_id=1, source_target_pairs={{0,30},{1,3},{2,0},{3,5},{4,2},{5,7},{6,4},{7,9},{8,6},{9,11},{10,... | collective-permute-start | bytes 1708040 | tf_op jit(solution)/shard_map/ppermute | solution.py:604
  13.6 10.6 %collective-permute-start.3 = (f32[88,128]{1,0:T(8,128)S(1)}, f32[88,128]{1,0:T(8,128)S(1)}, u32[]{:S(2)}, u32[]{:S(2)}) collective-permute-start(f32[88,128]{1,0:T(8,128)S(1)} %get-tuple-element.69.first_in), channel_id=1, source_target_pairs={{0,28},{2,30},{4,0},{6,2},{8,4},{10,6},{12,8},{14,10},{16,12},{18,... | collective-permute-start | bytes 135176 | tf_op jit(solution)/shard_map/ppermute | solution.py:541
  24.2 3.3 %collective-permute-start.4 = (f32[1112,128]{1,0:T(8,128)S(1)}, f32[1112,128]{1,0:T(8,128)S(1)}, u32[]{:S(2)}, u32[]{:S(2)}) collective-permute-start(f32[1112,128]{1,0:T(8,128)S(1)} %collective-permute-done.1.touch.touch_m.mine), channel_id=1, source_target_pairs={{0,1},{1,0},{2,3},{3,2},{4,5},{5,4},{6,7},{7,6},{8,9},{9,8},{10,11... | collective-permute-start | bytes 1708040 | tf_op jit(solution)/shard_map/ppermute | solution.py:545
  24.8 2.7 %collective-permute-start.5 = (f32[1112,128]{1,0:T(8,128)S(1)}, f32[1112,128]{1,0:T(8,128)S(1)}, u32[]{:S(2)}, u32[]{:S(2)}) collective-permute-start(f32[1112,128]{1,0:T(8,128)S(1)} %collective-permute-done.2.beyond.beyond_m), channel_id=1, source_target_pairs={{0,1},{1,0},{2,3},{3,2},{4,5},{5,4},{6,7},{7,6},{8,9},{9,8},{10,11... | collective-permute-start | bytes 1708040 | tf_op jit(solution)/shard_map/ppermute | solution.py:545
  36.8 4.9 %collective-permute-start.8 = (f32[8,128]{1,0:T(8,128)S(1)}, f32[8,128]{1,0:T(8,128)S(1)}, u32[]{:S(2)}, u32[]{:S(2)}) collective-permute-start(f32[8,128]{1,0:T(8,128)S(1)} %get-tuple-element.87), channel_id=1, source_target_pairs={{0,6},{2,4},{4,2},{6,0},{8,14},{10,12},{12,10},{14,8},{16,22},{18,... | collective-permute-start | bytes 12296 | tf_op jit(solution)/shard_map/ppermute | solution.py:549
  38.3 4.0 %collective-permute-start.7 = (f32[8,128]{1,0:T(8,128)S(1)}, f32[8,128]{1,0:T(8,128)S(1)}, u32[]{:S(2)}, u32[]{:S(2)}) collective-permute-start(f32[8,128]{1,0:T(8,128)S(1)} %get-tuple-element.87), channel_id=1, source_target_pairs={{0,4},{2,6},{4,0},{6,2},{8,12},{10,14},{12,8},{14,10},{16,20},{18,... | collective-permute-start | bytes 12296 | tf_op jit(solution)/shard_map/ppermute | solution.py:549
  39.2 3.1 %collective-permute-start.6 = (f32[8,128]{1,0:T(8,128)S(1)}, f32[8,128]{1,0:T(8,128)S(1)}, u32[]{:S(2)}, u32[]{:S(2)}) collective-permute-start(f32[8,128]{1,0:T(8,128)S(1)} %get-tuple-element.87), channel_id=1, source_target_pairs={{0,2},{2,0},{4,6},{6,4},{8,10},{10,8},{12,14},{14,12},{16,18},{18,... | collective-permute-start | bytes 12296 | tf_op jit(solution)/shard_map/ppermute | solution.py:549
  42.3 6.7 %collective-permute-start.11 = (f32[8,128]{1,0:T(8,128)S(1)}, f32[8,128]{1,0:T(8,128)S(1)}, u32[]{:S(2)}, u32[]{:S(2)}) collective-permute-start(f32[8,128]{1,0:T(8,128)S(1)} %add_add_fusion.1.t0), channel_id=1, source_target_pairs={{0,24},{2,26},{4,28},{6,30},{8,16},{10,18},{12,20},{14,22},{16,8},... | collective-permute-start | bytes 12296 | tf_op jit(solution)/shard_map/ppermute | solution.py:549
  46.3 4.0 %collective-permute-start.10 = (f32[8,128]{1,0:T(8,128)S(1)}, f32[8,128]{1,0:T(8,128)S(1)}, u32[]{:S(2)}, u32[]{:S(2)}) collective-permute-start(f32[8,128]{1,0:T(8,128)S(1)} %add_add_fusion.1.t0), channel_id=1, source_target_pairs={{0,16},{2,18},{4,20},{6,22},{8,24},{10,26},{12,28},{14,30},{16,0},... | collective-permute-start | bytes 12296 | tf_op jit(solution)/shard_map/ppermute | solution.py:549
  46.3 4.0 %collective-permute-start.9 = (f32[8,128]{1,0:T(8,128)S(1)}, f32[8,128]{1,0:T(8,128)S(1)}, u32[]{:S(2)}, u32[]{:S(2)}) collective-permute-start(f32[8,128]{1,0:T(8,128)S(1)} %add_add_fusion.1.t0), channel_id=1, source_target_pairs={{0,8},{2,10},{4,12},{6,14},{8,0},{10,2},{12,4},{14,6},{16,24},{18,... | collective-permute-start | bytes 12296 | tf_op jit(solution)/shard_map/ppermute | solution.py:549
  57.7 3.7 %collective-permute-start.14 = (f32[8,128]{1,0:T(8,128)S(1)}, f32[8,128]{1,0:T(8,128)S(1)}, u32[]{:S(2)}, u32[]{:S(2)}) collective-permute-start(f32[8,128]{1,0:T(8,128)S(1)} %get-tuple-element.103), channel_id=1, source_target_pairs={{0,6},{2,4},{4,2},{6,0},{8,14},{10,12},{12,10},{14,8},{16,22},{18,... | collective-permute-start | bytes 12296 | tf_op jit(solution)/shard_map/ppermute | solution.py:549
  59.1 4.0 %collective-permute-start.13 = (f32[8,128]{1,0:T(8,128)S(1)}, f32[8,128]{1,0:T(8,128)S(1)}, u32[]{:S(2)}, u32[]{:S(2)}) collective-permute-start(f32[8,128]{1,0:T(8,128)S(1)} %get-tuple-element.103), channel_id=1, source_target_pairs={{0,4},{2,6},{4,0},{6,2},{8,12},{10,14},{12,8},{14,10},{16,20},{18,... | collective-permute-start | bytes 12296 | tf_op jit(solution)/shard_map/ppermute | solution.py:549
  60.1 3.0 %collective-permute-start.12 = (f32[8,128]{1,0:T(8,128)S(1)}, f32[8,128]{1,0:T(8,128)S(1)}, u32[]{:S(2)}, u32[]{:S(2)}) collective-permute-start(f32[8,128]{1,0:T(8,128)S(1)} %get-tuple-element.103), channel_id=1, source_target_pairs={{0,2},{2,0},{4,6},{6,4},{8,10},{10,8},{12,14},{14,12},{16,18},{18,... | collective-permute-start | bytes 12296 | tf_op jit(solution)/shard_map/ppermute | solution.py:549
  63.1 3.7 %collective-permute-start.17 = (f32[8,128]{1,0:T(8,128)S(1)}, f32[8,128]{1,0:T(8,128)S(1)}, u32[]{:S(2)}, u32[]{:S(2)}) collective-permute-start(f32[8,128]{1,0:T(8,128)S(1)} %add_add_fusion.t0), channel_id=1, source_target_pairs={{0,24},{2,26},{4,28},{6,30},{8,16},{10,18},{12,20},{14,22},{16,8},... | collective-permute-start | bytes 12296 | tf_op jit(solution)/shard_map/ppermute | solution.py:549
  64.5 4.0 %collective-permute-start.16 = (f32[8,128]{1,0:T(8,128)S(1)}, f32[8,128]{1,0:T(8,128)S(1)}, u32[]{:S(2)}, u32[]{:S(2)}) collective-permute-start(f32[8,128]{1,0:T(8,128)S(1)} %add_add_fusion.t0), channel_id=1, source_target_pairs={{0,16},{2,18},{4,20},{6,22},{8,24},{10,26},{12,28},{14,30},{16,0},... | collective-permute-start | bytes 12296 | tf_op jit(solution)/shard_map/ppermute | solution.py:549
  64.7 3.7 %collective-permute-start.15 = (f32[8,128]{1,0:T(8,128)S(1)}, f32[8,128]{1,0:T(8,128)S(1)}, u32[]{:S(2)}, u32[]{:S(2)}) collective-permute-start(f32[8,128]{1,0:T(8,128)S(1)} %add_add_fusion.t0), channel_id=1, source_target_pairs={{0,8},{2,10},{4,12},{6,14},{8,0},{10,2},{12,4},{14,6},{16,24},{18,... | collective-permute-start | bytes 12296 | tf_op jit(solution)/shard_map/ppermute | solution.py:549
  68.4 7.2 %copy-start = (f32[2,512,128]{2,1,0:T(8,128)S(1)}, f32[2,512,128]{2,1,0:T(8,128)}, u32[]{:S(2)}) copy-start(f32[2,512,128]{2,1,0:T(8,128)} %slow) | copy-start | bytes 1572868
  68.4 7.2 %copy-start.1 = (f32[3,2,128,128]{3,2,1,0:T(8,128)S(1)}, f32[3,2,128,128]{3,2,1,0:T(8,128)}, u32[]{:S(2)}) copy-start(f32[3,2,128,128]{3,2,1,0:T(8,128)} %dual) | copy-start | bytes 1179652
  69.7 7.5 %collective-permute-start.18 = (f32[4,2,128,128]{3,2,1,0:T(8,128)S(1)}, f32[4,2,128,128]{3,2,1,0:T(8,128)S(1)}, u32[]{:S(2)}, u32[]{:S(2)}) collective-permute-start(f32[4,2,128,128]{3,2,1,0:T(8,128)S(1)} %gradient.2), channel_id=1, source_target_pairs={{0,1},{1,0},{2,3},{3,2},{4,5},{5,4},{6,7},{7,6},{8,9},{9,8},{10,11... | collective-permute-start | bytes 1572872 | tf_op jit(solution)/shard_map/ppermute | solution.py:545
  78.5 6.8 %collective-permute-start.19 = (f32[2,136,128]{2,1,0:T(8,128)S(1)}, f32[2,136,128]{2,1,0:T(8,128)S(1)}, u32[]{:S(2)}, u32[]{:S(2)}) collective-permute-start(f32[2,136,128]{2,1,0:T(8,128)S(1)} %get-tuple-element.121), channel_id=1, source_target_pairs={{0,32},{32,0},{64,96},{96,64},{1,33},{33,1},{65,97},{97,65},{2,34}... | collective-permute-start | bytes 417800 | tf_op jit(solution)/shard_map/ppermute | solution.py:708
  79.8 8.9 %collective-permute-start.20 = (f32[2,136,128]{2,1,0:T(8,128)S(1)}, f32[2,136,128]{2,1,0:T(8,128)S(1)}, u32[]{:S(2)}, u32[]{:S(2)}) collective-permute-start(f32[2,136,128]{2,1,0:T(8,128)S(1)} %get-tuple-element.122), channel_id=1, source_target_pairs={{0,64},{32,96},{64,0},{96,32},{1,65},{33,97},{65,1},{97,33},{2,66}... | collective-permute-start | bytes 417800 | tf_op jit(solution)/shard_map/ppermute | solution.py:708
  82.3 8.9 %collective-permute-start.21 = (f32[2,136,128]{2,1,0:T(8,128)S(1)}, f32[2,136,128]{2,1,0:T(8,128)S(1)}, u32[]{:S(2)}, u32[]{:S(2)}) collective-permute-start(f32[2,136,128]{2,1,0:T(8,128)S(1)} %get-tuple-element.123), channel_id=1, source_target_pairs={{0,96},{32,64},{64,32},{96,0},{1,97},{33,65},{65,33},{97,1},{2,98}... | collective-permute-start | bytes 417800 | tf_op jit(solution)/shard_map/ppermute | solution.py:708
  82.5 2.8 %collective-permute-start.22 = (f32[1,128,128]{2,1,0:T(8,128)S(1)}, f32[1,128,128]{2,1,0:T(8,128)S(1)}, u32[]{:S(2)}, u32[]{:S(2)}) collective-permute-start(f32[1,128,128]{2,1,0:T(8,128)S(1)} %get-tuple-element.124), channel_id=1, source_target_pairs={{0,1},{1,2},{2,3},{3,4},{4,5},{5,6},{6,7},{7,8},{8,9},{9,10},{10,1... | collective-permute-start | bytes 196616 | tf_op jit(solution)/shard_map/ppermute | solution.py:541
